TPU v7x, 128 devices: a whole 4x4x4 slice. The times are simulated.
128 devices in a mesh: les: 8 (over z_lo, y), ac: 16 (over x, z_hi, core).
Axes of the slice: x: 4, y: 4, z: 4 (z_hi: 2, z_lo: 2; z = z_hi * 2 + z_lo), core: 2. Of those that a mesh axis runs over, the one named last changes fastest.
Arguments:
- velocity: bfloat16 [3, 131072, 128], P(None, ('les', 'ac')), may hold values from -6 to 6
- vorticity: bfloat16 [3, 131072, 128], P(None, ('les', 'ac')), may hold values from -6 to 6
- cover: int32 [131072, 2], P(('les', 'ac')), may hold values from 0 to 127, all different within a row; in each aligned block of 1024 rows (0 to 1023, 1024 to 2047, ...) at most 32 rows name the same one
- target_line: int32 [131072, 2], P(('les', 'ac')), may hold values from 0 to 511
- phase: int32 [131072, 2], P(('les', 'ac')), may hold values from 0 to 3
- fringe_lines: int32 [128, 2], P(('les', 'ac')), may hold values from 0 to 511
- acoustic: float32 [4, 65536, 256], P(None, ('les', 'ac')), may hold values from -6 to 6
Outputs:
- acoustic_next: float32 [4, 65536, 256], P(None, ('les', 'ac'))
Inputs may be any that keep to these rules, and one draw needn't show every extreme that they name: `cover`: within the rows of one device, no acoustic block is named more than 32 times, and some block exactly 32 times; the 2 blocks of one slab differ.
All inputs are finite; a program needn't handle non-finite values.
Results may differ from a plain program's by a relative error of at most 0.003.
Values may be sent and summed in bfloat16 or wider, within the bound.
No kernel may reach another device: no remote copies, remote signals or barrier semaphores. Data moves between devices by JAX's collectives and lax.ppermute only.
A program may use at most 64 MiB of HBM per device.

v0:
```python
import jax
import jax.numpy as jnp
import numpy as np
from jax import lax
from jax.sharding import PartitionSpec as P

NOFF = 4


ADVECT = 0.5
STEP = 0.4


def from_behind(x, axis, by):
    peers = lax.axis_size(axis)
    pairs = [(i, i + by) for i in range(peers) if 0 <= i + by < peers]
    return lax.ppermute(x, axis, pairs)


def lagrange_table(coarse, fine, phases):
    fine_ids = jnp.arange(fine, dtype=jnp.int32)
    phase_ids = jnp.arange(phases, dtype=jnp.int32)
    numerator = phases * fine_ids[None, :] + phase_ids[:, None]
    first_tap = jnp.clip(numerator // (2 * phases) - 1, 0, coarse - 4)
    where_x = numerator.astype(jnp.float32) / (2.0 * phases)
    coarse_ids = jnp.arange(coarse, dtype=jnp.int32)
    lagrange = jnp.zeros((phases, coarse, fine), jnp.float32)
    for tap_index in range(4):
        weight = jnp.ones_like(where_x)
        for other_tap in range(4):
            if other_tap != tap_index:
                weight = (
                    weight
                    * (where_x - (first_tap + other_tap).astype(jnp.float32))
                    / float(tap_index - other_tap)
                )
        hit_mask = coarse_ids[None, :, None] == (first_tap + tap_index)[:, None, :]
        lagrange = lagrange + jnp.where(hit_mask, weight[:, None, :], jnp.float32(0.0))
    return lagrange


def derivative_matrix(cells):
    cell_ids = np.arange(cells)
    distance = cell_ids[:, None] - cell_ids[None, :]
    rhs_matrix = jnp.asarray(
        np.where(distance == -1, 0.75, np.where(distance == 1, -0.75, 0.0)), dtype=jnp.float32
    )
    main_band = jnp.ones((cells,), jnp.float32)
    lower_band = jnp.asarray(np.where(cell_ids == 0, 0.0, 0.25), dtype=jnp.float32)
    upper_band = jnp.asarray(np.where(cell_ids == cells - 1, 0.0, 0.25), dtype=jnp.float32)
    solved = lax.linalg.tridiagonal_solve(lower_band, main_band, upper_band, rhs_matrix)
    return solved.T


def ape_rates(dx_all, dy_pressure, dy_across, source):
    pressure = -ADVECT * dx_all[0] - dx_all[1] - dy_across
    along = -ADVECT * dx_all[1] - dx_all[0] - source[0]
    across = -ADVECT * dx_all[2] - dy_pressure - source[1]
    spanwise = -ADVECT * dx_all[3] - source[2]
    return jnp.stack([pressure, along, across, spanwise])


def deliver(payload, codes):
    return (
        lax.all_to_all(payload, ("les", "ac"), split_axis=1, concat_axis=1, tiled=True),
        lax.all_to_all(codes, ("les", "ac"), split_axis=1, concat_axis=1, tiled=True),
    )


def y_diff(field, low_row, high_row):
    extended = jnp.concatenate([low_row[None], field, high_row[None]], axis=0)
    return (extended[2:] - extended[:-2]) * 0.5


def local(velocity, vorticity, cover, target_line, phase, fringe_lines, acoustic):
    n_les = lax.axis_size("les")
    n_ac = lax.axis_size("ac")
    devices = n_les * n_ac
    slab_count = velocity.shape[1]
    coarse = velocity.shape[2]
    top_count = cover.shape[1]
    line_count = acoustic.shape[1]
    cells = acoustic.shape[2]
    capacity = 2 * slab_count * top_count // devices
    slot_total = devices * capacity
    pair_count = slab_count * top_count
    lamb = jnp.cross(vorticity.astype(jnp.float32), velocity.astype(jnp.float32), axis=0).astype(
        jnp.bfloat16
    )
    weights = lagrange_table(coarse, cells, NOFF).astype(jnp.bfloat16)
    destination = cover.reshape(-1)
    hit_table = (destination[:, None] == jnp.arange(devices, dtype=jnp.int32)[None, :]).astype(
        jnp.int32
    )
    earlier = jnp.cumsum(hit_table, axis=0) - hit_table
    slot_index = destination * capacity + jnp.sum(earlier * hit_table, axis=1)
    source_ids = jnp.arange(pair_count, dtype=jnp.int32) // top_count
    slot_source = jnp.full((slot_total,), slab_count, jnp.int32).at[slot_index].set(source_ids)
    padded_lamb = jnp.concatenate([lamb, jnp.zeros((3, 1, coarse), jnp.bfloat16)], axis=1)
    payload = jnp.take(padded_lamb, slot_source, axis=1)
    codes = (
        jnp.full((1, slot_total), -1, jnp.int32)
        .at[0, slot_index]
        .set(target_line.reshape(-1) * NOFF + phase.reshape(-1))
    )
    got_rows, got_codes = deliver(
        payload.reshape(3, devices, capacity, coarse), codes.reshape(1, devices, capacity)
    )
    got_rows = got_rows.reshape(3, slot_total, coarse)
    flat_codes = got_codes.reshape(-1)
    combo_table = (
        jnp.arange(line_count * NOFF, dtype=jnp.int32)[:, None] == flat_codes[None, :]
    ).astype(jnp.bfloat16)
    gathered = jnp.einsum(
        "rs,csk->crk", combo_table, got_rows, preferred_element_type=jnp.float32
    ).astype(jnp.bfloat16)
    gathered = gathered.reshape(3, line_count, NOFF, coarse)
    source = jnp.einsum("clok,okj->clj", gathered, weights, preferred_element_type=jnp.float32)
    dmat = derivative_matrix(cells)
    up_line = fringe_lines[0, 0]
    down_line = fringe_lines[0, 1]

    def tendency(state):
        dx_all = jnp.dot(state.reshape(-1, cells), dmat, precision=lax.Precision.HIGHEST).reshape(
            state.shape
        )
        pressure = state[0]
        across = state[2]
        up_face = jnp.stack(
            [
                lax.dynamic_index_in_dim(pressure, up_line, 0, keepdims=False),
                lax.dynamic_index_in_dim(across, up_line, 0, keepdims=False),
            ]
        )
        down_face = jnp.stack(
            [
                lax.dynamic_index_in_dim(pressure, down_line, 0, keepdims=False),
                lax.dynamic_index_in_dim(across, down_line, 0, keepdims=False),
            ]
        )
        low_ghost = from_behind(up_face, "ac", 1)
        high_ghost = from_behind(down_face, "ac", -1)
        dy_pressure = y_diff(pressure, low_ghost[0], high_ghost[0])
        dy_across = y_diff(across, low_ghost[1], high_ghost[1])
        return ape_rates(dx_all, dy_pressure, dy_across, source)

    first = tendency(acoustic)
    second = tendency(acoustic + 0.5 * STEP * first)
    third = tendency(acoustic + 0.5 * STEP * second)
    fourth = tendency(acoustic + STEP * third)
    return acoustic + STEP / 6.0 * (first + 2.0 * second + 2.0 * third + fourth)


def solution(mesh):
    return jax.shard_map(
        local,
        mesh=mesh,
        in_specs=(
            P(None, ("les", "ac"), None),
            P(None, ("les", "ac"), None),
            P(("les", "ac"), None),
            P(("les", "ac"), None),
            P(("les", "ac"), None),
            P(("les", "ac"), None),
            P(None, ("les", "ac"), None),
        ),
        out_specs=P(None, ("les", "ac"), None),
        check_vma=False,
    )
```

profile of v0, /device:TPU:6, one launch (start us, length us, event | category | flops | bytes accessed | tf_op | source)
XLA Modules:
  0.0 836.6 jit_solution(9133814853398877202)
XLA Ops:
  0.0 1.4 fusion.116
  4.1 1.9 copy.278
  6.0 1.3 slice_bitcast_fusion.10
  9.9 5.5 collective-permute-start
  16.2 1.9 collective-permute-start.1
  20.9 1.4 mul.1828
  23.7 8.1 scatter_custom_fusion.1
  32.5 10.9 %all-to-all-start.1 = ((s32[1,128,32]{2,0,1:T(1,128)}), s32[1,128,32]{2,0,1:T(1,128)}, u32[]{:S(2)}, u32[]{:S(2)}) async-start(s32[1,128,32]{2,0,1:T(1,128)} %bitcast.275), calls=%async_computation.1 | async-start | bytes 131072 | tf_op jit(solution)/shard_map/all_to_all | solution.py:66
  43.4 8.4 scatter_custom_fusion
  51.9 448.4 %while.34 = (s32[]{:T(128)}, f32[]{:T(128)}, f32[256]{0:T(256)S(1)}, f32[7,32]{1,0:T(8,128)S(1)}, f32[7,32,256]{2,1,0:T(8,128)S(1)}, /*index=5*/f32[7,32]{1,0:T(...) while((s32[]{:T(128)}, f32[]{:T(128)}, ...), condition=%wide.region_1.2_spmd.clone, body=%wide.region_0.1_spmd.clone.sunk | while | flops 24705 | bytes 268513 | solution.py:51
  92.7 1.3 constant_dynamic-slice_fusion.77
  95.1 20.0 %subtract_divide_fusion.125 = (f32[256]{0:T(256)S(1)}, f32[256]{0:T(256)S(1)}, f32[256]{0:T(256)S(1)}, f32[256]{0:T(256)S(1)}, f32[256]{0:T(256)S(1)}, /*index=5...) fusion(f32[256]{0:T(256)S(1)} %bitcast.1075, ...), kind=kLoop, calls=%fused_computation.103.clone.1 | loop fusion | flops 24576 | bytes 66816 | tf_op jit(solution)/shard_map/while/body/eval_jaxpr/div | solution.py:51
  159.0 20.0 %subtract_divide_fusion.125 = (f32[256]{0:T(256)S(1)}, f32[256]{0:T(256)S(1)}, f32[256]{0:T(256)S(1)}, f32[256]{0:T(256)S(1)}, f32[256]{0:T(256)S(1)}, /*index=5...) fusion(f32[256]{0:T(256)S(1)} %bitcast.1075, ...), kind=kLoop, calls=%fused_computation.103.clone.1 | loop fusion | flops 24576 | bytes 66816 | tf_op jit(solution)/shard_map/while/body/eval_jaxpr/div | solution.py:51
  223.0 20.0 %subtract_divide_fusion.125 = (f32[256]{0:T(256)S(1)}, f32[256]{0:T(256)S(1)}, f32[256]{0:T(256)S(1)}, f32[256]{0:T(256)S(1)}, f32[256]{0:T(256)S(1)}, /*index=5...) fusion(f32[256]{0:T(256)S(1)} %bitcast.1075, ...), kind=kLoop, calls=%fused_computation.103.clone.1 | loop fusion | flops 24576 | bytes 66816 | tf_op jit(solution)/shard_map/while/body/eval_jaxpr/div | solution.py:51
  284.8 1.3 constant_dynamic-slice_fusion.77
  287.1 20.0 %subtract_divide_fusion.125 = (f32[256]{0:T(256)S(1)}, f32[256]{0:T(256)S(1)}, f32[256]{0:T(256)S(1)}, f32[256]{0:T(256)S(1)}, f32[256]{0:T(256)S(1)}, /*index=5...) fusion(f32[256]{0:T(256)S(1)} %bitcast.1075, ...), kind=kLoop, calls=%fused_computation.103.clone.1 | loop fusion | flops 24576 | bytes 66816 | tf_op jit(solution)/shard_map/while/body/eval_jaxpr/div | solution.py:51
  351.1 20.0 %subtract_divide_fusion.125 = (f32[256]{0:T(256)S(1)}, f32[256]{0:T(256)S(1)}, f32[256]{0:T(256)S(1)}, f32[256]{0:T(256)S(1)}, f32[256]{0:T(256)S(1)}, /*index=5...) fusion(f32[256]{0:T(256)S(1)} %bitcast.1075, ...), kind=kLoop, calls=%fused_computation.103.clone.1 | loop fusion | flops 24576 | bytes 66816 | tf_op jit(solution)/shard_map/while/body/eval_jaxpr/div | solution.py:51
  412.8 1.3 constant_dynamic-slice_fusion.77
  415.2 20.0 %subtract_divide_fusion.125 = (f32[256]{0:T(256)S(1)}, f32[256]{0:T(256)S(1)}, f32[256]{0:T(256)S(1)}, f32[256]{0:T(256)S(1)}, f32[256]{0:T(256)S(1)}, /*index=5...) fusion(f32[256]{0:T(256)S(1)} %bitcast.1075, ...), kind=kLoop, calls=%fused_computation.103.clone.1 | loop fusion | flops 24576 | bytes 66816 | tf_op jit(solution)/shard_map/while/body/eval_jaxpr/div | solution.py:51
  477.0 1.3 constant_dynamic-slice_fusion.77
  479.4 20.0 %subtract_divide_fusion.125 = (f32[256]{0:T(256)S(1)}, f32[256]{0:T(256)S(1)}, f32[256]{0:T(256)S(1)}, f32[256]{0:T(256)S(1)}, f32[256]{0:T(256)S(1)}, /*index=5...) fusion(f32[256]{0:T(256)S(1)} %bitcast.1075, ...), kind=kLoop, calls=%fused_computation.103.clone.1 | loop fusion | flops 24576 | bytes 66816 | tf_op jit(solution)/shard_map/while/body/eval_jaxpr/div | solution.py:51
  501.7 1.3 convert_bitcast_fusion
  507.0 3.6 fusion.21
  510.6 28.6 %gather_fusion = bf16[4096,3,128]{2,1,0:T(4,128)(2,1)} fusion(bf16[3,1025,128]{2,0,1:T(4,128)(2,1)S(1)} %fusion.21, s32[4096]{0:T(1024)S(1)} %fusion.86), kind=kCustom, calls=%fused_computation | custom fusion | bytes 6307840 | tf_op jit(solution)/shard_map/jit(_take)/gather | solution.py:100
  539.5 4.1 copy_select_fusion
  544.5 10.9 %all-to-all-start = ((bf16[3,128,32,128]{3,2,0,1:T(8,128)(2,1)}), bf16[3,128,32,128]{3,2,0,1:T(8,128)(2,1)}, u32[]{:S(2)}, u32[]{:S(2)}) async-start(bf16[3,128,32,128]{3,2,0,1:T(8,128)(2,1)} %copy_select_fusion), calls=%async_computation | async-start | bytes 6291456 | tf_op jit(solution)/shard_map/all_to_all | solution.py:65
  555.5 153.2 %while.33 = (s32[]{:T(128)}, f32[256]{0:T(256)S(1)}, f32[7,32,256]{2,1,0:T(8,128)S(1)}, f32[7,32,256]{2,1,0:T(8,128)S(1)}, f32[7,32]{1,0:T(8,128)S(1)}, /*index=...) while((s32[]{:T(128)}, f32[256]{0:T(256)S(1)}, ...), condition=%wide.region_3.4_spmd, body=%wide.region_2.3_spmd.sunk | while | flops 16418 | bytes 266713 | solution.py:51
  557.1 20.1 %multiply_subtract_fusion.125 = (f32[256]{0:T(256)S(1)}, f32[256]{0:T(256)S(1)}, f32[256]{0:T(256)S(1)}, f32[256]{0:T(256)S(1)}, f32[256]{0:T(256)S(1)}, /*index...) fusion(f32[256]{0:T(256)S(1)} %bitcast.1124, ...), kind=kLoop, calls=%fused_computation.37.clone.1 | loop fusion | flops 16384 | bytes 66688 | tf_op jit(solution)/shard_map/while/body/eval_jaxpr/sub | solution.py:51
  579.0 20.1 %multiply_subtract_fusion.125 = (f32[256]{0:T(256)S(1)}, f32[256]{0:T(256)S(1)}, f32[256]{0:T(256)S(1)}, f32[256]{0:T(256)S(1)}, f32[256]{0:T(256)S(1)}, /*index...) fusion(f32[256]{0:T(256)S(1)} %bitcast.1124, ...), kind=kLoop, calls=%fused_computation.37.clone.1 | loop fusion | flops 16384 | bytes 66688 | tf_op jit(solution)/shard_map/while/body/eval_jaxpr/sub | solution.py:51
  600.9 20.1 %multiply_subtract_fusion.125 = (f32[256]{0:T(256)S(1)}, f32[256]{0:T(256)S(1)}, f32[256]{0:T(256)S(1)}, f32[256]{0:T(256)S(1)}, f32[256]{0:T(256)S(1)}, /*index...) fusion(f32[256]{0:T(256)S(1)} %bitcast.1124, ...), kind=kLoop, calls=%fused_computation.37.clone.1 | loop fusion | flops 16384 | bytes 66688 | tf_op jit(solution)/shard_map/while/body/eval_jaxpr/sub | solution.py:51
  622.8 20.1 %multiply_subtract_fusion.125 = (f32[256]{0:T(256)S(1)}, f32[256]{0:T(256)S(1)}, f32[256]{0:T(256)S(1)}, f32[256]{0:T(256)S(1)}, f32[256]{0:T(256)S(1)}, /*index...) fusion(f32[256]{0:T(256)S(1)} %bitcast.1124, ...), kind=kLoop, calls=%fused_computation.37.clone.1 | loop fusion | flops 16384 | bytes 66688 | tf_op jit(solution)/shard_map/while/body/eval_jaxpr/sub | solution.py:51
  644.7 20.1 %multiply_subtract_fusion.125 = (f32[256]{0:T(256)S(1)}, f32[256]{0:T(256)S(1)}, f32[256]{0:T(256)S(1)}, f32[256]{0:T(256)S(1)}, f32[256]{0:T(256)S(1)}, /*index...) fusion(f32[256]{0:T(256)S(1)} %bitcast.1124, ...), kind=kLoop, calls=%fused_computation.37.clone.1 | loop fusion | flops 16384 | bytes 66688 | tf_op jit(solution)/shard_map/while/body/eval_jaxpr/sub | solution.py:51
  666.6 20.1 %multiply_subtract_fusion.125 = (f32[256]{0:T(256)S(1)}, f32[256]{0:T(256)S(1)}, f32[256]{0:T(256)S(1)}, f32[256]{0:T(256)S(1)}, f32[256]{0:T(256)S(1)}, /*index...) fusion(f32[256]{0:T(256)S(1)} %bitcast.1124, ...), kind=kLoop, calls=%fused_computation.37.clone.1 | loop fusion | flops 16384 | bytes 66688 | tf_op jit(solution)/shard_map/while/body/eval_jaxpr/sub | solution.py:51
  688.4 20.1 %multiply_subtract_fusion.125 = (f32[256]{0:T(256)S(1)}, f32[256]{0:T(256)S(1)}, f32[256]{0:T(256)S(1)}, f32[256]{0:T(256)S(1)}, f32[256]{0:T(256)S(1)}, /*index...) fusion(f32[256]{0:T(256)S(1)} %bitcast.1124, ...), kind=kLoop, calls=%fused_computation.37.clone.1 | loop fusion | flops 16384 | bytes 66688 | tf_op jit(solution)/shard_map/while/body/eval_jaxpr/sub | solution.py:51
  710.1 19.4 %multiply_subtract_fusion.32 = (f32[256]{0:T(256)S(1)}, f32[256]{0:T(256)S(1)}, f32[256]{0:T(256)S(1)}, f32[256]{0:T(256)S(1)}, f32[256]{0:T(256)S(1)}, /*index=...) fusion(f32[256]{0:T(256)S(1)} %bitcast.1214, ...), kind=kLoop, calls=%fused_computation.337 | loop fusion | flops 15872 | bytes 64636 | tf_op jit(solution)/shard_map/eval_jaxpr/sub | solution.py:51
  729.7 4.8 convolution_bitcast_fusion
  736.3 1.6 reduce.39
  738.0 2.5 copy.245
  740.5 8.4 %fusion.7 = bf16[3,2048,128]{1,2,0:T(8,128)(2,1)} fusion(bf16[3,4096,128]{2,1,0:T(8,128)(2,1)S(1)} %bitcast.1002, s32[4096]{0:T(1024)S(1)} %eq.95), kind=kOutput, calls=%fused_computation.142 | convolution fusion | flops 6451625984 | bytes 4734976 | tf_op jit(solution)/shard_map/rs,csk->crk/dot_general | solution.py:114
  748.9 2.6 copy.249
  751.5 2.3 fusion.17
  756.1 1.3 copy-done.4
  757.5 1.3 slice_bitcast_fusion.8
  758.8 2.9 copy.255
  764.0 5.3 collective-permute-start.2
  770.1 2.1 collective-permute-start.3
  772.2 3.7 fusion.117
  776.2 2.8 collective-permute-done.3
  781.0 1.3 copy-done.5
  782.3 1.5 slice_bitcast_fusion.6
  783.8 2.9 copy.263
  790.0 4.1 collective-permute-start.4
  795.0 1.9 collective-permute-start.5
  796.9 3.7 fusion.118
  800.9 3.0 collective-permute-done.5
  805.9 1.3 copy-done.6
  807.2 1.4 slice_bitcast_fusion.4
  808.6 2.9 copy.271
  814.8 4.1 collective-permute-start.6
  819.7 2.1 collective-permute-start.7
  821.9 3.7 fusion.119
  825.8 2.8 collective-permute-done.7
  831.2 2.3 fusion.14
  833.5 2.9 copy.279
  (366 shorter events, 70.5 us)
Async XLA Ops:
  6.0 12.1 %copy-start.38 = (s32[1024,2]{0,1:T(2,128)S(1)}, s32[1024,2]{0,1:T(2,128)}, u32[]{:S(2)}) copy-start(s32[1024,2]{0,1:T(2,128)} %param.16) | copy-start | bytes 24580
  9.9 724.7 %collective-permute-start = (f32[2,256]{0,1:T(8,128)}, f32[2,256]{0,1:T(8,128)S(1)}, u32[]{:S(2)}, u32[]{:S(2)}) collective-permute-start(f32[2,256]{0,1:T(8,128)} %copy.234), channel_id=1, source_target_pairs={{1,0},{2,1},{3,2},{4,3},{5,4},{6,5},{7,6},{8,7},{9,8},{10,9},{11,1... | collective-permute-start | bytes 6152 | tf_op jit(solution)/shard_map/ppermute | solution.py:17
  16.2 718.5 %collective-permute-start.1 = (f32[2,256]{0,1:T(8,128)}, f32[2,256]{0,1:T(8,128)}, u32[]{:S(2)}, u32[]{:S(2)}) collective-permute-start(f32[2,256]{0,1:T(8,128)} %copy.235), channel_id=1, source_target_pairs={{0,1},{1,2},{2,3},{3,4},{4,5},{5,6},{6,7},{7,8},{8,9},{9,10},{10,1... | collective-permute-start | bytes 6152 | tf_op jit(solution)/shard_map/ppermute | solution.py:17
  19.5 3.5 copy-start.72
  19.5 3.5 copy-start.73
  19.5 3.6 copy-start.39
  19.5 3.6 copy-start.40
  19.9 32.0 %copy-start.37 = (f32[256]{0:T(256)S(1)}, f32[256]{0:T(256)}, u32[]{:S(2)}) copy-start(f32[256]{0:T(256)} %constant.237) | copy-start | bytes 3076
  32.5 512.1 %all-to-all-start.1 = ((s32[1,128,32]{2,0,1:T(1,128)}), s32[1,128,32]{2,0,1:T(1,128)}, u32[]{:S(2)}, u32[]{:S(2)}) async-start(s32[1,128,32]{2,0,1:T(1,128)} %bitcast.275), calls=%async_computation.1 | async-start | bytes 131072 | tf_op jit(solution)/shard_map/all_to_all | solution.py:66
  51.9 449.8 %copy-start.36 = (bf16[3,1024,128]{2,1,0:T(8,128)(2,1)S(1)}, bf16[3,1024,128]{2,1,0:T(8,128)(2,1)}, u32[]{:S(2)}) copy-start(bf16[3,1024,128]{2,1,0:T(8,128)(2,1)} %param.14) | copy-start | bytes 2359300
  539.1 4.4 copy-start.41
  539.1 4.4 copy-start.42
  539.2 4.4 copy-start.43
  539.2 4.4 copy-start.44
  539.2 4.4 copy-start.45
  539.2 4.4 copy-start.46
  539.2 4.4 copy-start.47
  539.2 4.4 copy-start.48
  539.2 4.4 copy-start.49
  539.2 4.4 copy-start.50
  539.2 4.4 copy-start.51
  539.2 4.4 copy-start.52
  539.3 4.4 copy-start.53
  539.3 4.4 copy-start.54
  539.3 4.4 copy-start.55
  539.3 4.4 copy-start.56
  539.3 4.4 copy-start.57
  539.3 4.4 copy-start.58
  539.3 4.4 copy-start.59
  539.4 4.4 copy-start.60
  539.4 4.4 copy-start.61
  539.4 4.4 copy-start.62
  539.4 4.4 copy-start.63
  539.4 4.4 copy-start.64
  539.4 4.4 copy-start.65
  539.4 4.4 copy-start.66
  539.4 4.4 copy-start.67
  539.5 4.4 copy-start.68
  539.5 4.4 copy-start.69
  539.5 4.4 copy-start.70
  539.5 4.4 copy-start.71
  544.5 193.5 %all-to-all-start = ((bf16[3,128,32,128]{3,2,0,1:T(8,128)(2,1)}), bf16[3,128,32,128]{3,2,0,1:T(8,128)(2,1)}, u32[]{:S(2)}, u32[]{:S(2)}) async-start(bf16[3,128,32,128]{3,2,0,1:T(8,128)(2,1)} %copy_select_fusion), calls=%async_computation | async-start | bytes 6291456 | tf_op jit(solution)/shard_map/all_to_all | solution.py:65
  751.5 2.3 copy-start.7
  751.5 2.4 copy-start.28
  751.5 2.4 copy-start.29
  764.0 12.1 %collective-permute-start.2 = (f32[2,256]{0,1:T(8,128)}, f32[2,256]{0,1:T(8,128)S(1)}, u32[]{:S(2)}, u32[]{:S(2)}) collective-permute-start(f32[2,256]{0,1:T(8,128)} %copy.258), channel_id=1, source_target_pairs={{1,0},{2,1},{3,2},{4,3},{5,4},{6,5},{7,6},{8,7},{9,8},{10,9},{11,1... | collective-permute-start | bytes 6152 | tf_op jit(solution)/shard_map/ppermute | solution.py:17
  770.1 8.9 %collective-permute-start.3 = (f32[2,256]{0,1:T(8,128)}, f32[2,256]{0,1:T(8,128)S(1)}, u32[]{:S(2)}, u32[]{:S(2)}) collective-permute-start(f32[2,256]{0,1:T(8,128)} %copy.259), channel_id=1, source_target_pairs={{0,1},{1,2},{2,3},{3,4},{4,5},{5,6},{6,7},{7,8},{8,9},{9,10},{10,1... | collective-permute-start | bytes 6152 | tf_op jit(solution)/shard_map/ppermute | solution.py:17
  772.2 3.7 copy-start.1
  776.0 3.1 copy-start.32
  776.0 3.1 copy-start.33
  790.0 10.7 %collective-permute-start.4 = (f32[2,256]{0,1:T(8,128)}, f32[2,256]{0,1:T(8,128)S(1)}, u32[]{:S(2)}, u32[]{:S(2)}) collective-permute-start(f32[2,256]{0,1:T(8,128)} %copy.266), channel_id=1, source_target_pairs={{1,0},{2,1},{3,2},{4,3},{5,4},{6,5},{7,6},{8,7},{9,8},{10,9},{11,1... | collective-permute-start | bytes 6152 | tf_op jit(solution)/shard_map/ppermute | solution.py:17
  795.0 8.9 %collective-permute-start.5 = (f32[2,256]{0,1:T(8,128)}, f32[2,256]{0,1:T(8,128)S(1)}, u32[]{:S(2)}, u32[]{:S(2)}) collective-permute-start(f32[2,256]{0,1:T(8,128)} %copy.267), channel_id=1, source_target_pairs={{0,1},{1,2},{2,3},{3,4},{4,5},{5,6},{6,7},{7,8},{8,9},{9,10},{10,1... | collective-permute-start | bytes 6152 | tf_op jit(solution)/shard_map/ppermute | solution.py:17
  796.9 3.7 copy-start.2
  800.6 3.3 copy-start.34
  800.6 3.3 copy-start.35
  800.7 3.9 copy-start.8
  814.8 10.9 %collective-permute-start.6 = (f32[2,256]{0,1:T(8,128)}, f32[2,256]{0,1:T(8,128)S(1)}, u32[]{:S(2)}, u32[]{:S(2)}) collective-permute-start(f32[2,256]{0,1:T(8,128)} %copy.274), channel_id=1, source_target_pairs={{1,0},{2,1},{3,2},{4,3},{5,4},{6,5},{7,6},{8,7},{9,8},{10,9},{11,1... | collective-permute-start | bytes 6152 | tf_op jit(solution)/shard_map/ppermute | solution.py:17
  819.7 8.9 %collective-permute-start.7 = (f32[2,256]{0,1:T(8,128)}, f32[2,256]{0,1:T(8,128)S(1)}, u32[]{:S(2)}, u32[]{:S(2)}) collective-permute-start(f32[2,256]{0,1:T(8,128)} %copy.275), channel_id=1, source_target_pairs={{0,1},{1,2},{2,3},{3,4},{4,5},{5,6},{6,7},{7,8},{8,9},{9,10},{10,1... | collective-permute-start | bytes 6152 | tf_op jit(solution)/shard_map/ppermute | solution.py:17
  821.8 3.7 copy-start.3
  825.6 3.1 copy-start.30
  825.6 3.1 copy-start.31
  828.8 2.1 copy-start.23
  828.8 2.2 copy-start.25
  828.8 2.4 copy-start.27
  (20 other events, 24.6 us)
where the time goes:
time: 852 us; the launch traced here: 837 us
  other arithmetic  319 us (37%)
  loops' own time  281 us (33%)
  local copies, waits for them, and re-layouts  145 us (17%)
  starting transfers between devices  48.8 us (6%)
  matrix products  26.7 us (3%)
  waiting for transfers between devices  8.61 us (1%)
    another operation x2, loops' own time, derivative_matrix(): lax.linalg.tridiagonal_solve(lower_band, main_band, upper_band, rhs_matrix)  281 us
    sub x8, other arithmetic, derivative_matrix(): lax.linalg.tridiagonal_solve(lower_band, main_band, upper_band, rhs_matrix)  160 us
    div x8, other arithmetic, derivative_matrix(): lax.linalg.tridiagonal_solve(lower_band, main_band, upper_band, rhs_matrix)  140 us
    slice x62, local copies, waits for them, and re-layouts, derivative_matrix(): lax.linalg.tridiagonal_solve(lower_band, main_band, upper_band, rhs_matrix)  39 us
    gather x1, local copies, waits for them, and re-layouts, local(): payload = jnp.take(padded_lamb, slot_source, axis=1)  28.6 us
    ppermute x8, starting transfers between devices, from_behind(): return lax.ppermute(x, axis, pairs)  27 us
    unnamed x151, local copies, waits for them, and re-layouts  18.4 us
  transfers between devices with their start and end apart: 10, of which 3 were waited for; matrix products, arithmetic and copies ran while one was open for 51% of the time, Pallas kernels for 0%

commit v1 on v0

v1 whole, which is shorter than its diff:
```python
import functools

import jax
import jax.numpy as jnp
import numpy as np
from jax import lax
from jax.experimental import pallas as pl
from jax.experimental.pallas import tpu as pltpu
from jax.sharding import PartitionSpec as P

PHASES = 4
ADVECT = 0.5
STEP = 0.4
AXES = ("les", "ac")
CODE_ROWS = 8
GROUP = 16
MIB = 1 << 20


def lagrange_weights(coarse, fine):
    table = np.zeros((PHASES, coarse, fine), np.float32)
    for phase in range(PHASES):
        numerator = PHASES * np.arange(fine) + phase
        first_tap = np.clip(numerator // (2 * PHASES) - 1, 0, coarse - 4)
        where_x = numerator.astype(np.float32) / np.float32(2 * PHASES)
        for tap in range(4):
            weight = np.ones((fine,), np.float32)
            for other in range(4):
                if other != tap:
                    gap = where_x - (first_tap + other).astype(np.float32)
                    weight = weight * gap / np.float32(tap - other)
            table[phase, first_tap + tap, np.arange(fine)] += weight
    return table.reshape(PHASES * coarse, fine)


def derivative_matrix(cells):
    off = np.eye(cells, k=1)
    a = np.eye(cells) + 0.25 * (off + off.T)
    b = 0.75 * (off - off.T)
    return np.linalg.solve(a, b).T


def whole(count):
    return [pl.BlockSpec(memory_space=pltpu.VMEM)] * count


def scalars():
    return pl.BlockSpec(memory_space=pltpu.SMEM)


def f32(x):
    return x.astype(jnp.float32)


def pack_kernel(place, velocity, vorticity, cover, line, phase, payload, table, ranks):
    devices = payload.shape[0]
    slabs = velocity.shape[1]
    coarse = velocity.shape[2]
    capacity = (payload.shape[1] - CODE_ROWS) // 3
    for c in range(3):
        a, b = (c + 1) % 3, (c + 2) % 3
        lamb = f32(vorticity[a]) * f32(velocity[b]) - f32(vorticity[b]) * f32(velocity[a])
        table[:, c * coarse:(c + 1) * coarse] = lamb.astype(jnp.bfloat16)
    cov = cover[...]
    code = line[...] * PHASES + phase[...]
    high = f32((code // 8) * 8)
    low = f32(code % 8)
    row8 = lax.broadcasted_iota(jnp.int32, (128, slabs), 0)
    facts = jnp.where(row8 == 0, high[0:1], 0.0)
    facts = jnp.where(row8 == 1, low[0:1], facts)
    facts = jnp.where(row8 == 2, high[1:2], facts)
    facts = jnp.where(row8 == 3, low[1:2], facts)
    facts = jnp.where(row8 == 4, f32(cov[0:1]), facts)
    table[:, 3 * coarse:] = facts.T.astype(jnp.bfloat16)

    ids = lax.broadcasted_iota(jnp.int32, (devices, slabs), 0)
    hit = (cov[0:1] == ids) | (cov[1:2] == ids)
    hit_f = jnp.where(hit, 1.0, 0.0)
    width = 256
    earlier = (
        lax.broadcasted_iota(jnp.int32, (width, width), 0)
        < lax.broadcasted_iota(jnp.int32, (width, width), 1)
    )
    earlier = jnp.where(earlier, 1.0, 0.0).astype(jnp.bfloat16)
    before = jnp.zeros((devices, 1), jnp.float32)
    for k in range(slabs // width):
        part = hit_f[:, k * width:(k + 1) * width]
        rank = jnp.dot(part.astype(jnp.bfloat16), earlier, preferred_element_type=jnp.float32)
        ranks[:, k * width:(k + 1) * width] = jnp.where(part > 0.0, rank + before, -1.0)
        before = before + jnp.sum(part, axis=1, keepdims=True)

    slot = f32(lax.broadcasted_iota(jnp.int32, (GROUP, capacity, slabs), 1))
    span = GROUP * capacity
    lane_owner = lax.broadcasted_iota(jnp.int32, (1, span), 1) // capacity
    own_lanes = (
        lax.broadcasted_iota(jnp.int32, (GROUP, span), 1) // capacity
        == lax.broadcasted_iota(jnp.int32, (GROUP, span), 0)
    )
    my_part = lax.broadcasted_iota(jnp.int32, (GROUP, 128), 1) // capacity == place[0]
    which_row = lax.broadcasted_iota(jnp.int32, (GROUP, CODE_ROWS, 128), 1)

    def spread(values):
        rows = jnp.where(own_lanes, jnp.broadcast_to(values, (GROUP, span)), 0.0)
        total = rows[:, :128]
        for k in range(1, span // 128):
            total = total + rows[:, k * 128:(k + 1) * 128]
        shift = 64
        while shift >= capacity:
            total = total + pltpu.roll(total, shift, 1)
            shift //= 2
        return jnp.where(my_part, total, 0.0)[:, None, :]

    def group(g, carry):
        first = pl.multiple_of(g * GROUP, GROUP)
        mine = ranks[pl.ds(first, GROUP), :]
        choose = jnp.where(mine[:, None, :] == slot, 1.0, 0.0)
        choose = choose.reshape(span, slabs).astype(jnp.bfloat16)
        picked = jnp.dot(choose, table[...], preferred_element_type=jnp.float32)
        for c in range(3):
            rows = picked[:, c * coarse:(c + 1) * coarse].reshape(GROUP, capacity, coarse)
            payload[pl.ds(first, GROUP), c * capacity:(c + 1) * capacity, :] = rows.astype(
                jnp.bfloat16
            )
        codes = picked[:, 3 * coarse:].T
        is_first = codes[4:5] == f32(lane_owner + first)
        upper = spread(jnp.where(is_first, codes[0:1], codes[2:3]))
        lower = spread(jnp.where(is_first, codes[1:2], codes[3:4]))
        tile = jnp.where(which_row == 0, upper, jnp.where(which_row == 1, lower, 0.0))
        payload[pl.ds(first, GROUP), 3 * capacity:, :] = tile.astype(jnp.bfloat16)
        return carry

    lax.fori_loop(0, devices // GROUP, group, 0)


def pack(place, velocity, vorticity, cover, line, phase, devices, capacity):
    _, slabs, coarse = velocity.shape
    return pl.pallas_call(
        pack_kernel,
        out_shape=jax.ShapeDtypeStruct((devices, 3 * capacity + CODE_ROWS, coarse), jnp.bfloat16),
        in_specs=[scalars()] + whole(5),
        out_specs=whole(1)[0],
        scratch_shapes=[
            pltpu.VMEM((slabs, 3 * coarse + 128), jnp.bfloat16),
            pltpu.VMEM((devices, slabs), jnp.float32),
        ],
        compiler_params=pltpu.CompilerParams(vmem_limit_bytes=32 * MIB),
        name="pack",
    )(place, velocity, vorticity, cover, line, phase)


def split(x):
    high = x.astype(jnp.bfloat16)
    return high, (x - f32(high)).astype(jnp.bfloat16)


def dx(field, dmat):
    high, low = split(field)
    cells = field.shape[-1]
    both = jnp.dot(high, dmat[...], preferred_element_type=jnp.float32)
    return (
        both[:, :cells]
        + both[:, cells:]
        + jnp.dot(low, dmat[:, :cells], preferred_element_type=jnp.float32)
    )


def dy(field, low_row, high_row):
    lines = field.shape[0]
    at = lax.broadcasted_iota(jnp.int32, field.shape, 0)
    above = jnp.where(at == lines - 1, high_row, pltpu.roll(field, lines - 1, 0))
    below = jnp.where(at == 0, low_row, pltpu.roll(field, 1, 0))
    return (above - below) * 0.5


def homogeneous(state, low_ghost, high_ghost, dmat):
    dx_p, dx_u = dx(state[0], dmat), dx(state[1], dmat)
    yield 0, -ADVECT * dx_p - dx_u - dy(state[2], low_ghost[1:2], high_ghost[1:2])
    yield 1, -ADVECT * dx_u - dx_p
    yield 2, -ADVECT * dx(state[2], dmat) - dy(state[0], low_ghost[0:1], high_ghost[0:1])
    yield 3, -ADVECT * dx(state[3], dmat)


def faces_of(fringe, fields, up, down):
    for n, c in enumerate((0, 2)):
        up[n:n + 1, :] = fields[c, pl.ds(fringe[0, 0], 1), :]
        down[n:n + 1, :] = fields[c, pl.ds(fringe[0, 1], 1), :]


def start_kernel(state, low_ghost, high_ghost, dmat, out):
    for c, value in homogeneous(state, low_ghost, high_ghost, dmat):
        out[c] = value


def stage_kernel(scale, fringe, rate, state, low_ghost, high_ghost, dmat, out, up, down):
    for c, value in homogeneous(state, low_ghost, high_ghost, dmat):
        out[c] = rate[c] + scale * value
    faces_of(fringe, out, up, down)


def last_kernel(scale, rate, state, low_ghost, high_ghost, dmat, acoustic, out):
    for c, value in homogeneous(state, low_ghost, high_ghost, dmat):
        out[c] = acoustic[c] + STEP * (rate[c] + scale * value)


def unpack_kernel(fringe, payload, weights, rate, out, up, down, rows, codes, source):
    devices, height, coarse = payload.shape
    capacity = (height - CODE_ROWS) // 3
    slots = devices * capacity
    lines = rate.shape[1]
    for c in range(3):
        rows[:, c * coarse:(c + 1) * coarse] = payload[
            :, c * capacity:(c + 1) * capacity, :
        ].reshape(slots, coarse)
    per = 128 // capacity
    tiles = f32(payload[:, 3 * capacity:, :])
    tiles = tiles.reshape(devices // per, per, CODE_ROWS, 128).sum(axis=1)
    for k in range(devices // per):
        codes[:, k * 128:(k + 1) * 128] = jnp.sum(tiles[k], axis=0, keepdims=True).astype(jnp.int32)
    source[...] = jnp.zeros_like(source)

    def one_phase(o, carry):
        combo = lax.broadcasted_iota(jnp.int32, (lines, slots), 0) * PHASES + o
        lands = jnp.where(codes[...] == combo, 1.0, 0.0).astype(jnp.bfloat16)
        gathered = jnp.dot(lands, rows[...], preferred_element_type=jnp.float32)
        gathered = gathered.astype(jnp.bfloat16)
        here = weights[pl.ds(pl.multiple_of(o * coarse, coarse), coarse), :]
        for c in range(3):
            source[c] += jnp.dot(
                gathered[:, c * coarse:(c + 1) * coarse], here, preferred_element_type=jnp.float32
            )
        return carry

    lax.fori_loop(0, PHASES, one_phase, 0)
    out[0] = rate[0]
    for c in range(3):
        out[c + 1] = rate[c + 1] - source[c]
    faces_of(fringe, out, up, down)


def call(kernel, name, inputs, outputs, smem=0, scratch=(), limit=24):
    return pl.pallas_call(
        kernel,
        out_shape=outputs,
        in_specs=[scalars()] * smem + whole(len(inputs) - smem),
        out_specs=jax.tree.map(lambda _: whole(1)[0], outputs),
        scratch_shapes=list(scratch),
        compiler_params=pltpu.CompilerParams(vmem_limit_bytes=limit * MIB),
        name=name,
    )(*inputs)


def exchange(up, down):
    peers = lax.axis_size("ac")
    low = lax.ppermute(up, "ac", [(i, i + 1) for i in range(peers - 1)])
    high = lax.ppermute(down, "ac", [(i + 1, i) for i in range(peers - 1)])
    return low, high


def local(velocity, vorticity, cover, target_line, phase, fringe, acoustic):
    devices = lax.axis_size("les") * lax.axis_size("ac")
    slabs, coarse = velocity.shape[1:]
    lines, cells = acoustic.shape[1:]
    capacity = 2 * slabs * cover.shape[1] // devices
    me = lax.axis_index("les") * lax.axis_size("ac") + lax.axis_index("ac")
    place = (me % (128 // capacity)).reshape(1)

    exact = derivative_matrix(cells)
    high = exact.astype(np.float32).astype(jnp.bfloat16)
    rest = (exact - high.astype(np.float64)).astype(np.float32).astype(jnp.bfloat16)
    dmat = jnp.asarray(np.concatenate([high, rest], axis=1))
    weights = jnp.asarray(lagrange_weights(coarse, cells).astype(jnp.bfloat16))

    state_type = jax.ShapeDtypeStruct(acoustic.shape, jnp.float32)
    face_type = jax.ShapeDtypeStruct((2, cells), jnp.float32)
    staged = (state_type, face_type, face_type)

    def donor(column):
        rows = lax.dynamic_slice_in_dim(acoustic, fringe[0, column], 1, 1)[:, 0]
        return jnp.stack([rows[0], rows[2]])

    ghosts = exchange(donor(0), donor(1))
    payload = pack(
        place, velocity, vorticity, cover.T, target_line.T, phase.T, devices, capacity
    )
    payload = lax.all_to_all(payload, AXES, split_axis=0, concat_axis=0, tiled=True)
    rate = call(start_kernel, "start", (acoustic, *ghosts, dmat), state_type)
    rate, up, down = call(
        unpack_kernel, "unpack", (fringe, payload, weights, rate), staged, smem=1, limit=48,
        scratch=(
            pltpu.VMEM((devices * capacity, 3 * coarse), jnp.bfloat16),
            pltpu.VMEM((1, devices * capacity), jnp.int32),
            pltpu.VMEM((3, lines, cells), jnp.float32),
        ),
    )
    state = rate
    for order in (4, 3):
        low, high = exchange(up, down)
        state, up, down = call(
            functools.partial(stage_kernel, STEP / order), "stage",
            (fringe, rate, state, low, high, dmat), staged, smem=1,
        )
    low, high = exchange(up, down)
    return call(
        functools.partial(last_kernel, STEP / 2), "last",
        (rate, state, low, high, dmat, acoustic), state_type,
    )


def solution(mesh):
    split_rows = P(None, AXES, None)
    pairs = P(AXES, None)
    return jax.shard_map(
        local,
        mesh=mesh,
        in_specs=(split_rows, split_rows, pairs, pairs, pairs, pairs, split_rows),
        out_specs=split_rows,
        check_vma=False,
    )
```

time: 852 us -> 121 us (0.14)
  the two profiles are of different devices: /device:TPU:6 before, /device:TPU:1 now
where the time goes in v1:
time: 121 us
  waiting for transfers between devices  44.5 us (37%)
  starting transfers between devices  34 us (28%)
  Pallas kernels  30.5 us (25%)
  local copies, waits for them, and re-layouts  7.88 us (7%)
  between operations  3.97 us (3%)
    all_to_all x1, waiting for transfers between devices, local(): lax.all_to_all(payload, AXES, split_axis=0, concat_axis=0, tiled=True)  23.3 us
    ppermute x4, waiting for transfers between devices, exchange(): high = lax.ppermute(down, 'ac', [(i + 1, i) for i in range(peers - 1)])  21.2 us
    pallas_call x5, Pallas kernels, call(): pl.pallas_call(kernel, out_shape=outputs, in_specs=[scalars()] * smem + w...  20.4 us
    ppermute x4, starting transfers between devices, exchange(): low = lax.ppermute(up, 'ac', [(i, i + 1) for i in range(peers - 1)])  13.5 us
    all_to_all x1, starting transfers between devices, local(): lax.all_to_all(payload, AXES, split_axis=0, concat_axis=0, tiled=True)  11.9 us
    pallas_call x1, Pallas kernels, pack(): pl.pallas_call(pack_kernel, out_shape=jax.ShapeDtypeStruct((devices, 3 *...  10 us
    ppermute x4, starting transfers between devices, exchange(): high = lax.ppermute(down, 'ac', [(i + 1, i) for i in range(peers - 1)])  8.56 us
    unnamed x22, local copies, waits for them, and re-layouts  7.28 us
  transfers between devices with their start and end apart: 9, of which 5 were waited for; matrix products, arithmetic and copies ran while one was open for 1% of the time, Pallas kernels for 1%

profile of v1, /device:TPU:1, one launch (start us, length us, event | category | flops | bytes accessed | tf_op | source)
XLA Modules:
  0.0 120.8 jit_solution(1333749944483845837)
XLA Ops:
  0.0 0.0 copy-start.4
  0.0 1.1 copy-done.4
  1.1 0.0 copy-start.5
  1.1 1.1 copy-done.5
  2.3 0.0 copy-start.8
  2.3 0.7 copy-done.8
  3.0 0.0 copy-start.9
  3.0 0.7 copy-done.9
  3.7 0.0 copy-start.10
  3.7 0.7 copy-done.10
  4.4 10.0 %pack.1 = bf16[128,104,128]{2,1,0:T(8,128)(2,1)} custom-call(s32[1]{0:T(128)} %bitcast.place, bf16[3,1024,128]{2,1,0:T(8,128)(2,1)S(1)} %copy-done.4, bf16[3,1024,128]{2,1,0:T(8,128)(2,1)S(1)} %copy-done.5, s32[2,1024]{1,0:T(2,128)S(1)} %bitcast.14, s32[2,1024]{1,0:T(2,128)S(1)} %bitcast.15, s32[2,1024]{1,0:T(2,128)S(1)} %bitcast.16), custom_call_target="tpu_custom_call" | custom-call | tf_op jit(solution)/shard_map/pack/pallas_call | solution.py:137
  14.4 0.0 copy-start.7
  14.4 0.0 copy-start
  14.4 0.0 copy-start.3
  14.4 11.9 %all-to-all-start = ((bf16[128,104,128]{2,1,0:T(8,128)(2,1)}), bf16[128,104,128]{2,1,0:T(8,128)(2,1)}, u32[]{:S(2)}, u32[]{:S(2)}) async-start(bf16[128,104,128]{2,1,0:T(8,128)(2,1)} %pack.1), calls=%async_computation | async-start | bytes 6815744 | tf_op jit(solution)/shard_map/all_to_all | solution.py:285
  26.3 0.0 copy-done.7
  26.3 0.6 fusion
  30.7 0.0 copy-done
  30.7 5.4 %collective-permute-start = (f32[2,256]{1,0:T(2,128)S(1)}, f32[2,256]{1,0:T(2,128)S(1)}, u32[]{:S(2)}, u32[]{:S(2)}) collective-permute-start(f32[2,256]{1,0:T(2,128)S(1)} %pad_maximum_fusion), channel_id=1, source_target_pairs={{0,1},{1,2},{2,3},{3,4},{4,5},{5,6},{6,7},{7,8},{8,9},{9,10},{10,1... | collective-permute-start | bytes 6152 | tf_op jit(solution)/shard_map/ppermute | solution.py:254
  36.2 0.0 copy-start.6
  36.2 2.1 %collective-permute-start.1 = (f32[2,256]{1,0:T(2,128)S(1)}, f32[2,256]{1,0:T(2,128)S(1)}, u32[]{:S(2)}, u32[]{:S(2)}) collective-permute-start(f32[2,256]{1,0:T(2,128)S(1)} %pad_maximum_fusion.1), channel_id=1, source_target_pairs={{1,0},{2,1},{3,2},{4,3},{5,4},{6,5},{7,6},{8,7},{9,8},{10,9},{11,1... | collective-permute-start | bytes 6152 | tf_op jit(solution)/shard_map/ppermute | solution.py:255
  38.2 0.0 collective-permute-done.low_ghost
  38.3 6.1 %collective-permute-done.1.high_ghost = f32[2,256]{1,0:T(2,128)S(1)} collective-permute-done((f32[2,256]{1,0:T(2,128)S(1)}, f32[2,256]{1,0:T(2,128)S(1)}, u32[]{:S(2)}, u32[]{:S(2)}) %collective-permute-start.1) | collective-permute-done | bytes 2080 | tf_op jit(solution)/shard_map/ppermute | solution.py:255
  44.4 0.0 copy-done.3
  44.4 1.0 start.1.rate
  45.4 0.0 copy-start.1
  45.4 1.3 %copy-done.1 = f32[4,512,256]{2,1,0:T(8,128)} copy-done((f32[4,512,256]{2,1,0:T(8,128)}, f32[4,512,256]{2,1,0:T(8,128)S(1)}, u32[]{:S(2)}) %copy-start.1) | copy-done | bytes 2097176
  46.7 23.3 %all-to-all-done.payload = bf16[128,104,128]{2,1,0:T(8,128)(2,1)} async-done(((bf16[128,104,128]{2,1,0:T(8,128)(2,1)}), bf16[128,104,128]{2,1,0:T(8,128)(2,1)}, u32[]{:S(2)}, u32[]{:S(2)}) %all-to-all-start) | async-done | bytes 3407904 | tf_op jit(solution)/shard_map/all_to_all | solution.py:285
  70.0 0.0 copy-done.6
  70.0 0.0 copy-start.2
  70.0 1.6 %copy-done.2 = f32[4,512,256]{2,1,0:T(8,128)S(1)} copy-done((f32[4,512,256]{2,1,0:T(8,128)S(1)}, f32[4,512,256]{2,1,0:T(8,128)}, u32[]{:S(2)}) %copy-start.2) | copy-done | bytes 2097176
  71.6 13.0 %unpack.1 = (f32[4,512,256]{2,1,0:T(8,128)S(1)}, f32[2,256]{1,0:T(2,128)S(1)}, f32[2,256]{1,0:T(2,128)S(1)}) custom-call(s32[1,2]{1,0:T(1,128)S(1)} %copy-done.7, bf16[128,104,128]{2,1,0:T(8,128)(2,1)} %all-to-all-done.payload, bf16[512,256]{1,0:T(8,128)(2,1)S(1)} %copy-done.6, f32[4,512,256]{2,1,0:T(8,128)S(1)} %copy-done.2), custom_call_target="tpu_custom_call" | custom-call | tf_op jit(solution)/shard_map/unpack/pallas_call | solution.py:241
  84.6 4.0 %collective-permute-start.2 = (f32[2,256]{1,0:T(2,128)S(1)}, f32[2,256]{1,0:T(2,128)S(1)}, u32[]{:S(2)}, u32[]{:S(2)}) collective-permute-start(f32[2,256]{1,0:T(2,128)S(1)} %get-tuple-element.15), channel_id=1, source_target_pairs={{0,1},{1,2},{2,3},{3,4},{4,5},{5,6},{6,7},{7,8},{8,9},{9,10},{10,1... | collective-permute-start | bytes 6152 | tf_op jit(solution)/shard_map/ppermute | solution.py:254
  88.6 1.9 %collective-permute-start.3 = (f32[2,256]{1,0:T(2,128)S(1)}, f32[2,256]{1,0:T(2,128)S(1)}, u32[]{:S(2)}, u32[]{:S(2)}) collective-permute-start(f32[2,256]{1,0:T(2,128)S(1)} %get-tuple-element.16), channel_id=1, source_target_pairs={{1,0},{2,1},{3,2},{4,3},{5,4},{6,5},{7,6},{8,7},{9,8},{10,9},{11,1... | collective-permute-start | bytes 6152 | tf_op jit(solution)/shard_map/ppermute | solution.py:255
  90.6 0.0 collective-permute-done.2.low_ghost
  90.6 4.5 %collective-permute-done.3.high_ghost = f32[2,256]{1,0:T(2,128)S(1)} collective-permute-done((f32[2,256]{1,0:T(2,128)S(1)}, f32[2,256]{1,0:T(2,128)S(1)}, u32[]{:S(2)}, u32[]{:S(2)}) %collective-permute-start.3) | collective-permute-done | bytes 2080 | tf_op jit(solution)/shard_map/ppermute | solution.py:255
  95.1 1.8 %stage.2 = (f32[4,512,256]{2,1,0:T(8,128)S(1)}, f32[2,256]{1,0:T(2,128)S(1)}, f32[2,256]{1,0:T(2,128)S(1)}) custom-call(s32[1,2]{1,0:T(1,128)S(1)} %copy-done.7, f32[4,512,256]{2,1,0:T(8,128)S(1)} %get-tuple-element.14.rate.state, f32[4,512,256]{2,1,0:T(8,128)S(1)} %get-tuple-element.14.rate.state, f32[2,256]{1,0:T(2,128)S(1)} %collective-permute-done.2.low_ghost, ...), custom_call_target="tpu_custom_call" | custom-call | tf_op jit(solution)/shard_map/stage/pallas_call | solution.py:241
  96.9 2.1 %collective-permute-start.4 = (f32[2,256]{1,0:T(2,128)S(1)}, f32[2,256]{1,0:T(2,128)S(1)}, u32[]{:S(2)}, u32[]{:S(2)}) collective-permute-start(f32[2,256]{1,0:T(2,128)S(1)} %get-tuple-element.18), channel_id=1, source_target_pairs={{0,1},{1,2},{2,3},{3,4},{4,5},{5,6},{6,7},{7,8},{8,9},{9,10},{10,1... | collective-permute-start | bytes 6152 | tf_op jit(solution)/shard_map/ppermute | solution.py:254
  99.0 2.2 %collective-permute-start.5 = (f32[2,256]{1,0:T(2,128)S(1)}, f32[2,256]{1,0:T(2,128)S(1)}, u32[]{:S(2)}, u32[]{:S(2)}) collective-permute-start(f32[2,256]{1,0:T(2,128)S(1)} %get-tuple-element.19), channel_id=1, source_target_pairs={{1,0},{2,1},{3,2},{4,3},{5,4},{6,5},{7,6},{8,7},{9,8},{10,9},{11,1... | collective-permute-start | bytes 6152 | tf_op jit(solution)/shard_map/ppermute | solution.py:255
  101.2 0.0 collective-permute-done.4.low_ghost
  101.2 5.7 %collective-permute-done.5.high_ghost = f32[2,256]{1,0:T(2,128)S(1)} collective-permute-done((f32[2,256]{1,0:T(2,128)S(1)}, f32[2,256]{1,0:T(2,128)S(1)}, u32[]{:S(2)}, u32[]{:S(2)}) %collective-permute-start.5) | collective-permute-done | bytes 2080 | tf_op jit(solution)/shard_map/ppermute | solution.py:255
  106.9 1.8 %stage.3 = (f32[4,512,256]{2,1,0:T(8,128)S(1)}, f32[2,256]{1,0:T(2,128)S(1)}, f32[2,256]{1,0:T(2,128)S(1)}) custom-call(s32[1,2]{1,0:T(1,128)S(1)} %copy-done.7, f32[4,512,256]{2,1,0:T(8,128)S(1)} %get-tuple-element.14.rate.state, f32[4,512,256]{2,1,0:T(8,128)S(1)} %get-tuple-element.17.state, f32[2,256]{1,0:T(2,128)S(1)} %collective-permute-done.4.low_ghost, ...), custom_call_target="tpu_custom_call" | custom-call | tf_op jit(solution)/shard_map/stage/pallas_call | solution.py:241
  108.7 2.0 %collective-permute-start.6 = (f32[2,256]{1,0:T(2,128)S(1)}, f32[2,256]{1,0:T(2,128)S(1)}, u32[]{:S(2)}, u32[]{:S(2)}) collective-permute-start(f32[2,256]{1,0:T(2,128)S(1)} %get-tuple-element.21), channel_id=1, source_target_pairs={{0,1},{1,2},{2,3},{3,4},{4,5},{5,6},{6,7},{7,8},{8,9},{9,10},{10,1... | collective-permute-start | bytes 6152 | tf_op jit(solution)/shard_map/ppermute | solution.py:254
  110.7 2.4 %collective-permute-start.7 = (f32[2,256]{1,0:T(2,128)S(1)}, f32[2,256]{1,0:T(2,128)S(1)}, u32[]{:S(2)}, u32[]{:S(2)}) collective-permute-start(f32[2,256]{1,0:T(2,128)S(1)} %get-tuple-element.22), channel_id=1, source_target_pairs={{1,0},{2,1},{3,2},{4,3},{5,4},{6,5},{7,6},{8,7},{9,8},{10,9},{11,1... | collective-permute-start | bytes 6152 | tf_op jit(solution)/shard_map/ppermute | solution.py:255
  113.1 0.0 collective-permute-done.6.low_ghost
  113.1 4.9 %collective-permute-done.7.high_ghost = f32[2,256]{1,0:T(2,128)S(1)} collective-permute-done((f32[2,256]{1,0:T(2,128)S(1)}, f32[2,256]{1,0:T(2,128)S(1)}, u32[]{:S(2)}, u32[]{:S(2)}) %collective-permute-start.7) | collective-permute-done | bytes 2080 | tf_op jit(solution)/shard_map/ppermute | solution.py:255
  118.0 2.8 %last.1 = f32[4,512,256]{2,1,0:T(8,128)} custom-call(f32[4,512,256]{2,1,0:T(8,128)S(1)} %get-tuple-element.14.rate.state, f32[4,512,256]{2,1,0:T(8,128)S(1)} %get-tuple-element.20.state, f32[2,256]{1,0:T(2,128)S(1)} %collective-permute-done.6.low_ghost, f32[2,256]{1,0:T(2,128)S(1)} %collective-permute-done.7.high_ghost, bf16[256,512]{1,0:T(8,128)(2,1)S(1)} %copy-done.3, ...), custom_call_target="tpu_custom_call" | custom-call | tf_op jit(solution)/shard_map/last/pallas_call | solution.py:241
  (3 shorter events, 0.0 us)
Async XLA Ops:
  0.0 1.1 copy-start.4
  1.1 1.1 copy-start.5
  2.3 0.7 copy-start.8
  3.0 0.7 copy-start.9
  3.7 0.7 copy-start.10
  14.4 11.9 %copy-start.7 = (s32[1,2]{1,0:T(1,128)S(1)}, s32[1,2]{1,0:T(1,128)}, u32[]{:S(2)}) copy-start(s32[1,2]{1,0:T(1,128)} %fringe.5) | copy-start | bytes 28
  14.4 16.3 %copy-start = (f32[4,512,256]{2,1,0:T(8,128)S(1)}, f32[4,512,256]{2,1,0:T(8,128)}, u32[]{:S(2)}) copy-start(f32[4,512,256]{2,1,0:T(8,128)} %acoustic.1) | copy-start | bytes 6291460
  14.4 30.0 %copy-start.3 = (bf16[256,512]{1,0:T(8,128)(2,1)S(1)}, bf16[256,512]{1,0:T(8,128)(2,1)}, u32[]{:S(2)}) copy-start(bf16[256,512]{1,0:T(8,128)(2,1)} %constant.31.clone.dmat) | copy-start | bytes 786436
  14.4 55.6 %all-to-all-start = ((bf16[128,104,128]{2,1,0:T(8,128)(2,1)}), bf16[128,104,128]{2,1,0:T(8,128)(2,1)}, u32[]{:S(2)}, u32[]{:S(2)}) async-start(bf16[128,104,128]{2,1,0:T(8,128)(2,1)} %pack.1), calls=%async_computation | async-start | bytes 6815744 | tf_op jit(solution)/shard_map/all_to_all | solution.py:285
  30.7 7.5 %collective-permute-start = (f32[2,256]{1,0:T(2,128)S(1)}, f32[2,256]{1,0:T(2,128)S(1)}, u32[]{:S(2)}, u32[]{:S(2)}) collective-permute-start(f32[2,256]{1,0:T(2,128)S(1)} %pad_maximum_fusion), channel_id=1, source_target_pairs={{0,1},{1,2},{2,3},{3,4},{4,5},{5,6},{6,7},{7,8},{8,9},{9,10},{10,1... | collective-permute-start | bytes 6152 | tf_op jit(solution)/shard_map/ppermute | solution.py:254
  36.2 33.8 %copy-start.6 = (bf16[512,256]{1,0:T(8,128)(2,1)S(1)}, bf16[512,256]{1,0:T(8,128)(2,1)}, u32[]{:S(2)}) copy-start(bf16[512,256]{1,0:T(8,128)(2,1)} %constant.32.clone.weights) | copy-start | bytes 786436
  36.2 8.2 %collective-permute-start.1 = (f32[2,256]{1,0:T(2,128)S(1)}, f32[2,256]{1,0:T(2,128)S(1)}, u32[]{:S(2)}, u32[]{:S(2)}) collective-permute-start(f32[2,256]{1,0:T(2,128)S(1)} %pad_maximum_fusion.1), channel_id=1, source_target_pairs={{1,0},{2,1},{3,2},{4,3},{5,4},{6,5},{7,6},{8,7},{9,8},{10,9},{11,1... | collective-permute-start | bytes 6152 | tf_op jit(solution)/shard_map/ppermute | solution.py:255
  45.4 1.3 %copy-start.1 = (f32[4,512,256]{2,1,0:T(8,128)}, f32[4,512,256]{2,1,0:T(8,128)S(1)}, u32[]{:S(2)}) copy-start(f32[4,512,256]{2,1,0:T(8,128)S(1)} %start.1.rate) | copy-start | bytes 6291460
  70.0 1.6 %copy-start.2 = (f32[4,512,256]{2,1,0:T(8,128)S(1)}, f32[4,512,256]{2,1,0:T(8,128)}, u32[]{:S(2)}) copy-start(f32[4,512,256]{2,1,0:T(8,128)} %copy-done.1) | copy-start | bytes 6291460
  84.6 6.0 %collective-permute-start.2 = (f32[2,256]{1,0:T(2,128)S(1)}, f32[2,256]{1,0:T(2,128)S(1)}, u32[]{:S(2)}, u32[]{:S(2)}) collective-permute-start(f32[2,256]{1,0:T(2,128)S(1)} %get-tuple-element.15), channel_id=1, source_target_pairs={{0,1},{1,2},{2,3},{3,4},{4,5},{5,6},{6,7},{7,8},{8,9},{9,10},{10,1... | collective-permute-start | bytes 6152 | tf_op jit(solution)/shard_map/ppermute | solution.py:254
  88.6 6.4 %collective-permute-start.3 = (f32[2,256]{1,0:T(2,128)S(1)}, f32[2,256]{1,0:T(2,128)S(1)}, u32[]{:S(2)}, u32[]{:S(2)}) collective-permute-start(f32[2,256]{1,0:T(2,128)S(1)} %get-tuple-element.16), channel_id=1, source_target_pairs={{1,0},{2,1},{3,2},{4,3},{5,4},{6,5},{7,6},{8,7},{9,8},{10,9},{11,1... | collective-permute-start | bytes 6152 | tf_op jit(solution)/shard_map/ppermute | solution.py:255
  96.9 4.3 %collective-permute-start.4 = (f32[2,256]{1,0:T(2,128)S(1)}, f32[2,256]{1,0:T(2,128)S(1)}, u32[]{:S(2)}, u32[]{:S(2)}) collective-permute-start(f32[2,256]{1,0:T(2,128)S(1)} %get-tuple-element.18), channel_id=1, source_target_pairs={{0,1},{1,2},{2,3},{3,4},{4,5},{5,6},{6,7},{7,8},{8,9},{9,10},{10,1... | collective-permute-start | bytes 6152 | tf_op jit(solution)/shard_map/ppermute | solution.py:254
  99.0 7.9 %collective-permute-start.5 = (f32[2,256]{1,0:T(2,128)S(1)}, f32[2,256]{1,0:T(2,128)S(1)}, u32[]{:S(2)}, u32[]{:S(2)}) collective-permute-start(f32[2,256]{1,0:T(2,128)S(1)} %get-tuple-element.19), channel_id=1, source_target_pairs={{1,0},{2,1},{3,2},{4,3},{5,4},{6,5},{7,6},{8,7},{9,8},{10,9},{11,1... | collective-permute-start | bytes 6152 | tf_op jit(solution)/shard_map/ppermute | solution.py:255
  108.7 4.3 %collective-permute-start.6 = (f32[2,256]{1,0:T(2,128)S(1)}, f32[2,256]{1,0:T(2,128)S(1)}, u32[]{:S(2)}, u32[]{:S(2)}) collective-permute-start(f32[2,256]{1,0:T(2,128)S(1)} %get-tuple-element.21), channel_id=1, source_target_pairs={{0,1},{1,2},{2,3},{3,4},{4,5},{5,6},{6,7},{7,8},{8,9},{9,10},{10,1... | collective-permute-start | bytes 6152 | tf_op jit(solution)/shard_map/ppermute | solution.py:254
  110.7 7.3 %collective-permute-start.7 = (f32[2,256]{1,0:T(2,128)S(1)}, f32[2,256]{1,0:T(2,128)S(1)}, u32[]{:S(2)}, u32[]{:S(2)}) collective-permute-start(f32[2,256]{1,0:T(2,128)S(1)} %get-tuple-element.22), channel_id=1, source_target_pairs={{1,0},{2,1},{3,2},{4,3},{5,4},{6,5},{7,6},{8,7},{9,8},{10,9},{11,1... | collective-permute-start | bytes 6152 | tf_op jit(solution)/shard_map/ppermute | solution.py:255

commit v2 on v1

v2 whole, which is shorter than its diff:
```python
import functools

import jax
import jax.numpy as jnp
import numpy as np
from jax import lax
from jax.experimental import pallas as pl
from jax.experimental.pallas import tpu as pltpu
from jax.sharding import PartitionSpec as P

PHASES = 4
ADVECT = 0.5
STEP = 0.4
AXES = ("les", "ac")
CODE_ROWS = 8
GROUP = 16
PARTS = 4
MIB = 1 << 20
VMEM_LIMIT = 60 * MIB
PAD = 8


def lagrange_weights(coarse, fine):
    table = np.zeros((PHASES, coarse, fine), np.float32)
    for phase in range(PHASES):
        numerator = PHASES * np.arange(fine) + phase
        first_tap = np.clip(numerator // (2 * PHASES) - 1, 0, coarse - 4)
        where_x = numerator.astype(np.float32) / np.float32(2 * PHASES)
        for tap in range(4):
            weight = np.ones((fine,), np.float32)
            for other in range(4):
                if other != tap:
                    gap = where_x - (first_tap + other).astype(np.float32)
                    weight = weight * gap / np.float32(tap - other)
            table[phase, first_tap + tap, np.arange(fine)] += weight
    return table.reshape(PHASES * coarse, fine)


def derivative_matrix(cells):
    off = np.eye(cells, k=1)
    a = np.eye(cells) + 0.25 * (off + off.T)
    b = 0.75 * (off - off.T)
    return np.linalg.solve(a, b).T


def whole(count):
    return [pl.BlockSpec(memory_space=pltpu.VMEM)] * count


def far(count):
    return [pl.BlockSpec(memory_space=pltpu.HBM)] * count


def scalars():
    return pl.BlockSpec(memory_space=pltpu.SMEM)


def f32(x):
    return x.astype(jnp.float32)


def pack_kernel(
    place, velocity, vorticity, cover, line, phase, payload_out,
    payload, table, ranks, vel, vor, cov, lin, pha, arrived, left,
):
    devices = payload.shape[0]
    slabs = vel.shape[1]
    coarse = vel.shape[2]
    capacity = (payload.shape[1] - CODE_ROWS) // 3
    copies = [
        pltpu.make_async_copy(src, dst, arrived.at[n])
        for n, (src, dst) in enumerate(
            ((cover, cov), (line, lin), (phase, pha), (velocity, vel), (vorticity, vor))
        )
    ]
    for copy in copies:
        copy.start()

    copies[0].wait()
    first_block, second_block = cov[0:1, :], cov[1:2, :]
    ids = lax.broadcasted_iota(jnp.int32, (devices, slabs), 0)
    hit = (first_block == ids) | (second_block == ids)
    hit_f = jnp.where(hit, 1.0, 0.0)
    width = 256
    earlier = (
        lax.broadcasted_iota(jnp.int32, (width, width), 0)
        < lax.broadcasted_iota(jnp.int32, (width, width), 1)
    )
    earlier = jnp.where(earlier, 1.0, 0.0).astype(jnp.bfloat16)
    before = jnp.zeros((devices, 1), jnp.float32)
    for k in range(slabs // width):
        part = hit_f[:, k * width:(k + 1) * width]
        rank = jnp.dot(part.astype(jnp.bfloat16), earlier, preferred_element_type=jnp.float32)
        ranks[:, k * width:(k + 1) * width] = jnp.where(part > 0.0, rank + before, -1.0)
        before = before + jnp.sum(part, axis=1, keepdims=True)

    copies[1].wait()
    copies[2].wait()
    code = lin[...] * PHASES + pha[...]
    high = f32((code // 8) * 8)
    low = f32(code % 8)
    row8 = lax.broadcasted_iota(jnp.int32, (128, slabs), 0)
    facts = jnp.where(row8 == 0, high[0:1], 0.0)
    facts = jnp.where(row8 == 1, low[0:1], facts)
    facts = jnp.where(row8 == 2, high[1:2], facts)
    facts = jnp.where(row8 == 3, low[1:2], facts)
    facts = jnp.where(row8 == 4, f32(first_block), facts)
    table[:, 3 * coarse:] = facts.T.astype(jnp.bfloat16)

    copies[3].wait()
    copies[4].wait()
    for c in range(3):
        a, b = (c + 1) % 3, (c + 2) % 3
        lamb = f32(vor[a]) * f32(vel[b]) - f32(vor[b]) * f32(vel[a])
        table[:, c * coarse:(c + 1) * coarse] = lamb.astype(jnp.bfloat16)

    rows16 = lax.broadcasted_iota(jnp.int32, (16, slabs), 0)
    slots = [f32(rows16 + start).astype(jnp.bfloat16) for start in range(0, capacity, 16)]
    one, zero = jnp.bfloat16(1), jnp.bfloat16(0)
    span = GROUP * capacity
    lane_owner = lax.broadcasted_iota(jnp.int32, (1, span), 1) // capacity
    own_lanes = (
        lax.broadcasted_iota(jnp.int32, (GROUP, span), 1) // capacity
        == lax.broadcasted_iota(jnp.int32, (GROUP, span), 0)
    )
    my_part = lax.broadcasted_iota(jnp.int32, (GROUP, 128), 1) // capacity == place[0]
    which_row = lax.broadcasted_iota(jnp.int32, (GROUP, CODE_ROWS, 128), 1)

    def spread(values):
        rows = jnp.where(own_lanes, jnp.broadcast_to(values, (GROUP, span)), 0.0)
        total = rows[:, :128]
        for k in range(1, span // 128):
            total = total + rows[:, k * 128:(k + 1) * 128]
        shift = 64
        while shift >= capacity:
            total = total + pltpu.roll(total, shift, 1)
            shift //= 2
        return jnp.where(my_part, total, 0.0)[:, None, :]

    def group(g, carry):
        first = pl.multiple_of(g * GROUP, GROUP)
        mine = ranks[pl.ds(first, GROUP), :]
        pieces = []
        for n in range(GROUP):
            row = jnp.broadcast_to(mine[n:n + 1, :], (16, slabs)).astype(jnp.bfloat16)
            pieces += [jnp.where(row == slot, one, zero) for slot in slots]
        choose = jnp.concatenate(pieces, axis=0)
        picked = jnp.dot(choose, table[...], preferred_element_type=jnp.float32)
        for c in range(3):
            rows = picked[:, c * coarse:(c + 1) * coarse].reshape(GROUP, capacity, coarse)
            payload[pl.ds(first, GROUP), c * capacity:(c + 1) * capacity, :] = rows.astype(
                jnp.bfloat16
            )
        codes = picked[:, 3 * coarse:].T
        is_first = codes[4:5] == f32(lane_owner + first)
        upper = spread(jnp.where(is_first, codes[0:1], codes[2:3]))
        lower = spread(jnp.where(is_first, codes[1:2], codes[3:4]))
        tile = jnp.where(which_row == 0, upper, jnp.where(which_row == 1, lower, 0.0))
        payload[pl.ds(first, GROUP), 3 * capacity:, :] = tile.astype(jnp.bfloat16)
        leave(g).start()
        return carry

    def leave(g):
        mine = pl.ds(pl.multiple_of(g * GROUP, GROUP), GROUP)
        return pltpu.make_async_copy(payload.at[mine], payload_out.at[mine], left.at[g])

    def gone(g, carry):
        leave(g).wait()
        return carry

    lax.fori_loop(0, devices // GROUP, group, 0)
    lax.fori_loop(0, devices // GROUP, gone, 0)


def pack(place, velocity, vorticity, cover, line, phase, devices, capacity):
    _, slabs, coarse = velocity.shape
    return pl.pallas_call(
        pack_kernel,
        out_shape=jax.ShapeDtypeStruct((devices, 3 * capacity + CODE_ROWS, coarse), jnp.bfloat16),
        in_specs=[scalars()] + far(5),
        out_specs=far(1)[0],
        scratch_shapes=[
            pltpu.VMEM((devices, 3 * capacity + CODE_ROWS, coarse), jnp.bfloat16),
            pltpu.VMEM((slabs, 3 * coarse + 128), jnp.bfloat16),
            pltpu.VMEM((devices, slabs), jnp.float32),
            pltpu.VMEM(velocity.shape, velocity.dtype),
            pltpu.VMEM(vorticity.shape, vorticity.dtype),
            pltpu.VMEM(cover.shape, cover.dtype),
            pltpu.VMEM(line.shape, line.dtype),
            pltpu.VMEM(phase.shape, phase.dtype),
            pltpu.SemaphoreType.DMA((5,)),
            pltpu.SemaphoreType.DMA((devices // GROUP,)),
        ],
        compiler_params=pltpu.CompilerParams(vmem_limit_bytes=VMEM_LIMIT),
        name="pack",
    )(place, velocity, vorticity, cover, line, phase)


def split(x):
    high = x.astype(jnp.bfloat16)
    return high, (x - f32(high)).astype(jnp.bfloat16)


def dx(field, dmat):
    high, low = split(field)
    cells = field.shape[-1]
    both = jnp.dot(high, dmat[...], preferred_element_type=jnp.float32)
    return (
        both[:, :cells]
        + both[:, cells:]
        + jnp.dot(low, dmat[:, :cells], preferred_element_type=jnp.float32)
    )


def dy_inside(field):
    lines = field.shape[0]
    at = lax.broadcasted_iota(jnp.int32, field.shape, 0)
    above = jnp.where(at == lines - 1, 0.0, pltpu.roll(field, lines - 1, 0))
    below = jnp.where(at == 0, 0.0, pltpu.roll(field, 1, 0))
    return (above - below) * 0.5


def homogeneous(state, dmat):
    field = [state[c][...] for c in range(4)]
    dx_p, dx_u = dx(field[0], dmat), dx(field[1], dmat)
    yield 0, -ADVECT * dx_p - dx_u - dy_inside(field[2])
    yield 1, -ADVECT * dx_u - dx_p
    yield 2, -ADVECT * dx(field[2], dmat) - dy_inside(field[0])
    yield 3, -ADVECT * dx(field[3], dmat)


def start_kernel(state, low_ghost, high_ghost, dmat, out):
    lines = state.shape[1]
    for c, value in homogeneous(state, dmat):
        out[c] = value
    for c, n in ((0, 1), (2, 0)):
        out[c, 0:1, :] += 0.5 * low_ghost[n:n + 1]
        out[c, lines - 1:lines, :] -= 0.5 * high_ghost[n:n + 1]


def inside_kernel(rate, dmat, acoustic, out, one, two):
    for c, value in homogeneous(rate, dmat):
        one[c] = rate[c] + FIRST * value
    for c, value in homogeneous(one, dmat):
        two[c] = rate[c] + SECOND * value
    for c, value in homogeneous(two, dmat):
        out[c] = acoustic[c] + STEP * (rate[c] + THIRD * value)


FIRST, SECOND, THIRD = STEP / 4, STEP / 3, STEP / 2


def edge_kernel(lines, peers, here_at, got, dmat, inside, out, fix):
    me = here_at[0]

    def bundle(by):
        exists = (me + by >= 0) & (me + by < peers)
        return jnp.where(exists, got[jnp.clip(me + by, 0, peers - 1)], 0.0)

    def pair(sent, level, column):
        first = 4 * level + 2 * column
        return sent[first:first + 1, :], sent[first + 1:first + 2, :]

    def at(sent, column, line):
        return sent[12 + column:13 + column, :] == float(line + 1)

    def first_change(sign, ghost):
        p, v = ghost
        return 0.5 * sign * FIRST * v, 0.5 * sign * FIRST * p

    def second_level(sent, column, low, high):
        p, v = pair(sent, 1, column)
        for sign, line, ghost in ((1, 0, low), (-1, lines - 1, high)):
            dp, dv = first_change(sign, ghost)
            here = at(sent, column, line)
            p, v = p + jnp.where(here, dp, 0.0), v + jnp.where(here, dv, 0.0)
        return p, v

    @pl.when(pl.program_id(0) == 0)
    def _():
        mine, back1, back2, back3 = (bundle(-n) for n in range(4))
        next1, next2, next3 = (bundle(n) for n in range(1, 4))
        up0, up1, up2 = pair(mine, 0, 0), pair(back1, 0, 0), pair(back2, 0, 0)
        down0, down1, down2 = pair(mine, 0, 1), pair(next1, 0, 1), pair(next2, 0, 1)
        up3, down3 = pair(back3, 0, 0), pair(next3, 0, 1)
        second_up = [
            second_level(mine, 0, up1, down1),
            second_level(back1, 0, up2, down0),
            second_level(back2, 0, up3, pair(back1, 0, 1)),
        ]
        second_down = [
            second_level(mine, 1, up1, down1),
            second_level(next1, 1, up0, down2),
            second_level(next2, 1, pair(next1, 0, 0), down3),
        ]
        ends = [
            (1, up1, second_up[1]), (-1, down1, second_down[1]),
            (1, up2, second_up[2]), (-1, down0, second_down[0]),
            (1, up0, second_up[0]), (-1, down2, second_down[2]),
        ]
        changes = [first_change(sign, ghost) for sign, ghost, _ in ends]
        slopes = dx(jnp.concatenate([x for pv in changes for x in pv] + [jnp.zeros_like(up0[0])] * 4), dmat)
        seconds = []
        for n, (sign, _, ghost) in enumerate(ends):
            dp, dv = changes[n]
            sp, sv = slopes[2 * n:2 * n + 1], slopes[2 * n + 1:2 * n + 2]
            edge = (
                SECOND * (-ADVECT * sp + 0.5 * sign * ghost[1]),
                SECOND * -sp,
                SECOND * (-ADVECT * sv + 0.5 * sign * ghost[0]),
            )
            seconds.append((edge, (0.5 * SECOND * sign * dv, 0.5 * SECOND * sign * dp)))

        def third_level(sent, column, low, high):
            p, v = pair(sent, 2, column)
            for line, step, (edge, inner) in ((0, 1, low), (lines - 1, -1, high)):
                for where, dp, dv in ((line, edge[0], edge[2]), (line + step, *inner)):
                    here = at(sent, column, where)
                    p, v = p + jnp.where(here, dp, 0.0), v + jnp.where(here, dv, 0.0)
            return p, v

        ghosts = (
            third_level(back1, 0, seconds[2], seconds[3]),
            third_level(next1, 1, seconds[4], seconds[5]),
        )
        rows = [x for edge, inner in seconds[:2] for x in (*edge, *inner)]
        slopes = dx(jnp.concatenate(rows + [jnp.zeros_like(rows[0])] * 6), dmat)
        for n, sign in enumerate((1, -1)):
            (p0, u0, v0), (p1, v1) = seconds[n]
            sp0, su0, sv0, sp1, sv1 = (slopes[5 * n + k:5 * n + k + 1] for k in range(5))
            half = 0.5 * sign
            ghost_p, ghost_v = ghosts[n]
            change = (
                (-ADVECT * sp0 - su0 - half * v1 + half * ghost_v, -ADVECT * sp1 + half * v0, half * v1),
                (-ADVECT * su0 - sp0, -sp1, jnp.zeros_like(p0)),
                (-ADVECT * sv0 - half * p1 + half * ghost_p, -ADVECT * sv1 + half * p0, half * p1),
            )
            fix[n] = jnp.zeros(fix.shape[1:], fix.dtype)
            for c in range(3):
                for k in range(3):
                    row = k if n == 0 else 7 - k
                    fix[n, c, row:row + 1, :] = STEP * THIRD * change[c][k]

    out[...] = inside[...] + fix[pl.program_id(0)]


def add_edges(inside, dmat, got, here_at):
    fields, lines, cells = inside.shape
    block = pl.BlockSpec((fields, 8, cells), lambda i: (0, i * (lines // 8 - 1), 0))
    return pl.pallas_call(
        functools.partial(edge_kernel, lines, got.shape[0]),
        out_shape=jax.ShapeDtypeStruct(inside.shape, inside.dtype),
        grid=(2,),
        in_specs=[scalars()] + whole(2) + [block],
        out_specs=block,
        scratch_shapes=[pltpu.VMEM((2, fields, 8, cells), jnp.float32)],
        input_output_aliases={3: 0},
        compiler_params=pltpu.CompilerParams(vmem_limit_bytes=VMEM_LIMIT),
        name="edges",
    )(here_at, got, dmat, inside)


def receive_kernel(
    fringe, payload, weights_in, rate_in, dmat_in, out, sent,
    held, lands, rows, total, weights, rate, dmat, state, bundle, arrived, left,
):
    devices, height, coarse = payload.shape
    capacity = (height - CODE_ROWS) // 3
    lines = rate.shape[1]
    cells = rate.shape[2]
    part = devices // PARTS
    copies = [
        pltpu.make_async_copy(
            payload.at[k * part:(k + 1) * part], held.at[k * part:(k + 1) * part], arrived.at[k]
        )
        for k in range(PARTS)
    ]
    others = [
        pltpu.make_async_copy(src, dst, arrived.at[PARTS + k])
        for k, (src, dst) in enumerate(((weights_in, weights), (rate_in, rate), (dmat_in, dmat)))
    ]
    for copy in copies + others:
        copy.start()
    per = 128 // capacity
    tiles = part // per
    slots = part * capacity
    one, zero = jnp.bfloat16(1), jnp.bfloat16(0)
    row16 = lax.broadcasted_iota(jnp.int32, (16, slots), 0)
    for k, copy in enumerate(copies):
        copy.wait()
        mine = held.at[k * part:(k + 1) * part]
        codes = f32(mine[:, 3 * capacity:, :])
        codes = codes.reshape(tiles, per, CODE_ROWS, 128).sum(axis=1)
        codes = codes.sum(axis=1).astype(jnp.int32)
        phases = f32(codes % PHASES)
        phases = jnp.concatenate([phases, jnp.zeros((128 - tiles, 128), jnp.float32)], axis=0).T
        target = f32(codes // PHASES - lines // 2)
        target = jnp.concatenate([target[n:n + 1, :] for n in range(tiles)], axis=1)
        target = jnp.broadcast_to(target, (16, slots)).astype(jnp.bfloat16)
        for n in range(lines // 16):
            line = f32(row16 + (16 * n - lines // 2)).astype(jnp.bfloat16)
            lands[16 * n:16 * (n + 1), :] = jnp.where(target == line, one, zero)
        for n in range(tiles):
            phase = jnp.broadcast_to(phases[:, n:n + 1], (128, coarse)).astype(jnp.bfloat16)
            for c in range(3):
                values = mine[n * per:(n + 1) * per, c * capacity:(c + 1) * capacity, :]
                values = values.reshape(128, coarse)
                for o in range(PHASES):
                    at = (c * PHASES + o) * coarse
                    rows[128 * n:128 * (n + 1), at:at + coarse] = jnp.where(
                        phase == jnp.bfloat16(o), values, zero
                    )
        landed = jnp.dot(lands[...], rows[...], preferred_element_type=jnp.float32)
        total[...] = landed if k == 0 else total[...] + landed
    for copy in others:
        copy.wait()
    inner = slice(PAD, PAD + lines)
    state[:, :PAD, :] = jnp.zeros((4, PAD, cells), jnp.float32)
    state[:, PAD + lines:, :] = jnp.zeros((4, PAD, cells), jnp.float32)
    state[0, inner, :] = rate[0]
    deep = PHASES * coarse
    for c in range(3):
        gathered = total[:, c * deep:(c + 1) * deep].astype(jnp.bfloat16)
        source = jnp.dot(gathered, weights[...], preferred_element_type=jnp.float32)
        state[c + 1, inner, :] = rate[c + 1] - source
    leave = pltpu.make_async_copy(state.at[:, inner, :], out, left.at[0])
    leave.start()

    blank = jnp.zeros((1, cells), jnp.float32)
    near = [
        [[state[c, pl.ds(PAD + fringe[0, n] + k, 1), :] for k in range(-2, 3)] for c in range(3)]
        for n in range(2)
    ]
    slopes = [near[n][c][k] for n in range(2) for c in range(3) for k in (1, 2, 3)]
    slopes = dx(jnp.concatenate(slopes + [blank] * 6, axis=0), dmat)
    stage = []
    for n in range(2):
        p, u, v = near[n]
        dp, du, dv = (
            [slopes[9 * n + 3 * c + k:9 * n + 3 * c + k + 1] for k in range(3)] for c in range(3)
        )
        stage.append([[], [], []])
        for k in range(3):
            line = fringe[0, n] + k - 1
            real = (line >= 0) & (line < lines)
            change = (
                -ADVECT * dp[k] - du[k] - 0.5 * (v[k + 2] - v[k]),
                -ADVECT * du[k] - dp[k],
                -ADVECT * dv[k] - 0.5 * (p[k + 2] - p[k]),
            )
            for c in range(3):
                value = near[n][c][k + 1] + FIRST * change[c]
                stage[n][c].append(jnp.where(real, value, 0.0))
    slopes = [stage[n][c][1] for n in range(2) for c in range(3)]
    slopes = dx(jnp.concatenate(slopes + [blank] * 2, axis=0), dmat)
    for n in range(2):
        p, _, v = stage[n]
        dp, du, dv = (slopes[3 * n + c:3 * n + c + 1] for c in range(3))
        last_p = near[n][0][2] + SECOND * (-ADVECT * dp - du - 0.5 * (v[2] - v[0]))
        last_v = near[n][2][2] + SECOND * (-ADVECT * dv - 0.5 * (p[2] - p[0]))
        for level, pair in enumerate(((near[n][0][2], near[n][2][2]), (p[1], v[1]), (last_p, last_v))):
            for k in range(2):
                at = 4 * level + 2 * n + k
                bundle[at:at + 1, :] = pair[k]
        bundle[12 + n:13 + n, :] = jnp.full((1, cells), (fringe[0, n] + 1).astype(jnp.float32))
        bundle[14 + n:15 + n, :] = blank
    sent[...] = jnp.broadcast_to(bundle[...][None], sent.shape)
    leave.wait()


def call(kernel, name, inputs, outputs, smem=0):
    return pl.pallas_call(
        kernel,
        out_shape=outputs,
        in_specs=[scalars()] * smem + whole(len(inputs) - smem),
        out_specs=jax.tree.map(lambda _: whole(1)[0], outputs),
        compiler_params=pltpu.CompilerParams(vmem_limit_bytes=VMEM_LIMIT),
        name=name,
    )(*inputs)


def shifted(x, by):
    peers = lax.axis_size("ac")
    pairs = [(i, i + by) for i in range(peers) if 0 <= i + by < peers]
    return lax.ppermute(x, "ac", pairs)


def local(velocity, vorticity, cover, target_line, phase, fringe, acoustic):
    devices = lax.axis_size("les") * lax.axis_size("ac")
    slabs, coarse = velocity.shape[1:]
    lines, cells = acoustic.shape[1:]
    capacity = 2 * slabs * cover.shape[1] // devices
    me = lax.axis_index("les") * lax.axis_size("ac") + lax.axis_index("ac")
    place = (me % (128 // capacity)).reshape(1)

    exact = derivative_matrix(cells)
    high = exact.astype(np.float32).astype(jnp.bfloat16)
    rest = (exact - high.astype(np.float64)).astype(np.float32).astype(jnp.bfloat16)
    dmat = jnp.asarray(np.concatenate([high, rest], axis=1))
    weights = jnp.asarray(lagrange_weights(coarse, cells).astype(jnp.bfloat16))

    state_type = jax.ShapeDtypeStruct(acoustic.shape, jnp.float32)

    def donor(column):
        rows = lax.dynamic_slice_in_dim(acoustic, fringe[0, column], 1, 1)[:, 0]
        return jnp.stack([rows[0], rows[2]])

    ghosts = (shifted(donor(0), 1), shifted(donor(1), -1))
    payload = pack(
        place, velocity, vorticity, cover.T, target_line.T, phase.T, devices, capacity
    )
    payload = lax.all_to_all(payload, AXES, split_axis=0, concat_axis=0, tiled=True)
    rate = call(start_kernel, "start", (acoustic, *ghosts, dmat), state_type)
    peers = lax.axis_size("ac")
    part = devices // PARTS * capacity
    rate, sent = pl.pallas_call(
        receive_kernel,
        out_shape=(state_type, jax.ShapeDtypeStruct((peers, 16, cells), jnp.float32)),
        in_specs=[scalars()] + far(4),
        out_specs=(far(1)[0], whole(1)[0]),
        scratch_shapes=[
            pltpu.VMEM(payload.shape, payload.dtype),
            pltpu.VMEM((lines, part), jnp.bfloat16),
            pltpu.VMEM((part, 3 * PHASES * coarse), jnp.bfloat16),
            pltpu.VMEM((lines, 3 * PHASES * coarse), jnp.float32),
            pltpu.VMEM(weights.shape, weights.dtype),
            pltpu.VMEM(acoustic.shape, jnp.float32),
            pltpu.VMEM(dmat.shape, dmat.dtype),
            pltpu.VMEM((4, lines + 2 * PAD, cells), jnp.float32),
            pltpu.VMEM((16, cells), jnp.float32),
            pltpu.SemaphoreType.DMA((PARTS + 3,)),
            pltpu.SemaphoreType.DMA((1,)),
        ],
        compiler_params=pltpu.CompilerParams(vmem_limit_bytes=VMEM_LIMIT),
        name="receive",
    )(fringe, payload, weights, rate, dmat)
    got = lax.all_to_all(sent, "ac", split_axis=0, concat_axis=0, tiled=True)
    inside = pl.pallas_call(
        inside_kernel,
        out_shape=state_type,
        in_specs=whole(3),
        out_specs=whole(1)[0],
        scratch_shapes=[pltpu.VMEM(acoustic.shape, jnp.float32)] * 2,
        compiler_params=pltpu.CompilerParams(vmem_limit_bytes=VMEM_LIMIT),
        name="inside",
    )(rate, dmat, acoustic)
    return add_edges(inside, dmat, got, lax.axis_index("ac").reshape(1))


def solution(mesh):
    split_rows = P(None, AXES, None)
    pairs = P(AXES, None)
    return jax.shard_map(
        local,
        mesh=mesh,
        in_specs=(split_rows, split_rows, pairs, pairs, pairs, pairs, split_rows),
        out_specs=split_rows,
        check_vma=False,
    )
```

time: 121 us -> 101 us (0.83)
  waiting for transfers between devices: 44.5 us -> 29 us
  starting transfers between devices: 34 us -> 26.5 us
  Pallas kernels: 30.5 us -> 36.9 us
  local copies, waits for them, and re-layouts: 7.88 us -> 4.35 us
    pallas_call x0 -> x3, Pallas kernels: none -> 23 us  [the longest x1 14 us: local(): pl.pallas_call(receive_kernel, out_shape=(state_type, jax.ShapeDtypeStruc...]
    pallas_call x5 -> x1, Pallas kernels: 20.4 us -> 3.97 us  [call(): pl.pallas_call(kernel, out_shape=outputs, in_specs=[scalars()] * smem + w...]
    ppermute x8 -> x2, waiting for transfers between devices: 21.2 us -> 5.99 us  [shifted(): return lax.ppermute(x, 'ac', pairs)]
    ppermute x8 -> x2, starting transfers between devices: 22.1 us -> 7.36 us  [shifted(): return lax.ppermute(x, 'ac', pairs)]
    all_to_all x0 -> x1, starting transfers between devices: none -> 7.61 us  [local(): got = lax.all_to_all(sent, 'ac', split_axis=0, concat_axis=0, tiled=True)]
    unnamed x22 -> x10, local copies, waits for them, and re-layouts: 7.28 us -> 3.01 us
    all_to_all x1, waiting for transfers between devices: 23.3 us -> 21 us  [local(): lax.all_to_all(payload, AXES, split_axis=0, concat_axis=0, tiled=True)]
    all_to_all x0 -> x1, waiting for transfers between devices: none -> 2.02 us  [local(): got = lax.all_to_all(sent, 'ac', split_axis=0, concat_axis=0, tiled=True)]
  transfers between devices with their start and end apart: 9 -> 4, of which waited for: 5 -> 3; matrix products, arithmetic and copies ran while one was open for 1% -> 1% of each run, Pallas kernels for 1% -> 11%
where the time goes in v2:
time: 101 us; the launch traced here: 100 us
  Pallas kernels  36.9 us (37%)
  waiting for transfers between devices  29 us (29%)
  starting transfers between devices  26.5 us (26%)
  local copies, waits for them, and re-layouts  4.35 us (4%)
  between operations  3.75 us (4%)
    all_to_all x1, waiting for transfers between devices, local(): lax.all_to_all(payload, AXES, split_axis=0, concat_axis=0, tiled=True)  21 us
    pallas_call x1, Pallas kernels, local(): pl.pallas_call(receive_kernel, out_shape=(state_type, jax.ShapeDtypeStruc...  14 us
    all_to_all x1, starting transfers between devices, local(): lax.all_to_all(payload, AXES, split_axis=0, concat_axis=0, tiled=True)  11.5 us
    pallas_call x1, Pallas kernels, pack(): pl.pallas_call(pack_kernel, out_shape=jax.ShapeDtypeStruct((devices, 3 *...  9.91 us
    all_to_all x1, starting transfers between devices, local(): got = lax.all_to_all(sent, 'ac', split_axis=0, concat_axis=0, tiled=True)  7.61 us
    ppermute x2, starting transfers between devices, shifted(): return lax.ppermute(x, 'ac', pairs)  7.36 us
    pallas_call x1, Pallas kernels, local(): pl.pallas_call(inside_kernel, out_shape=state_type, in_specs=whole(3), ou...  6.88 us
    ppermute x2, waiting for transfers between devices, shifted(): return lax.ppermute(x, 'ac', pairs)  5.99 us
  transfers between devices with their start and end apart: 4, of which 3 were waited for; matrix products, arithmetic and copies ran while one was open for 1% of the time, Pallas kernels for 11%

profile of v2, /device:TPU:1, one launch (start us, length us, event | category | flops | bytes accessed | tf_op | source)
XLA Modules:
  0.0 100.5 jit_solution(11751622049912128107)
XLA Ops:
  0.0 9.9 %pack.1 = bf16[128,104,128]{2,1,0:T(8,128)(2,1)} custom-call(s32[1]{0:T(128)} %bitcast.1.place, bf16[3,1024,128]{2,1,0:T(8,128)(2,1)} %velocity.1, bf16[3,1024,128]{2,1,0:T(8,128)(2,1)} %vorticity.1, s32[2,1024]{1,0:T(2,128)} %bitcast.15, s32[2,1024]{1,0:T(2,128)} %bitcast.16, s32[2,1024]{1,0:T(2,128)} %bitcast.17), custom_call_target="tpu_custom_call" | custom-call | tf_op jit(solution)/shard_map/pack/pallas_call | solution.py:177
  9.9 0.0 copy-start.2
  9.9 11.5 %all-to-all-start = ((bf16[128,104,128]{2,1,0:T(8,128)(2,1)}), bf16[128,104,128]{2,1,0:T(8,128)(2,1)S(1)}, u32[]{:S(2)}, u32[]{:S(2)}) async-start(bf16[128,104,128]{2,1,0:T(8,128)(2,1)} %pack.1), calls=%async_computation | async-start | bytes 6815744 | tf_op jit(solution)/shard_map/all_to_all | solution.py:512
  21.4 0.0 copy-done.2
  21.4 0.6 fusion
  25.7 0.8 dynamic-slice_bitcast_fusion.1
  26.5 5.4 %collective-permute-start = (f32[2,256]{1,0:T(2,128)S(1)}, f32[2,256]{1,0:T(2,128)S(1)}, u32[]{:S(2)}, u32[]{:S(2)}) collective-permute-start(f32[2,256]{1,0:T(2,128)S(1)} %pad_maximum_fusion), channel_id=1, source_target_pairs={{0,1},{1,2},{2,3},{3,4},{4,5},{5,6},{6,7},{7,8},{8,9},{9,10},{10,1... | collective-permute-start | bytes 6152 | tf_op jit(solution)/shard_map/ppermute | solution.py:485
  31.9 1.9 %collective-permute-start.1 = (f32[2,256]{1,0:T(2,128)S(1)}, f32[2,256]{1,0:T(2,128)S(1)}, u32[]{:S(2)}, u32[]{:S(2)}) collective-permute-start(f32[2,256]{1,0:T(2,128)S(1)} %pad_maximum_fusion.1), channel_id=1, source_target_pairs={{1,0},{2,1},{3,2},{4,3},{5,4},{6,5},{7,6},{8,7},{9,8},{10,9},{11,1... | collective-permute-start | bytes 6152 | tf_op jit(solution)/shard_map/ppermute | solution.py:485
  33.8 0.0 collective-permute-done.low_ghost
  33.9 0.0 copy-start.3
  33.9 6.0 %collective-permute-done.1.high_ghost = f32[2,256]{1,0:T(2,128)S(1)} collective-permute-done((f32[2,256]{1,0:T(2,128)S(1)}, f32[2,256]{1,0:T(2,128)S(1)}, u32[]{:S(2)}, u32[]{:S(2)}) %collective-permute-start.1) | collective-permute-done | bytes 2080 | tf_op jit(solution)/shard_map/ppermute | solution.py:485
  39.9 0.0 copy-done.3
  39.9 0.0 copy-start.4
  39.9 0.6 copy-done.4
  40.4 4.0 %start.1.rate_in = f32[4,512,256]{2,1,0:T(8,128)} custom-call(f32[4,512,256]{2,1,0:T(8,128)} %acoustic.1, f32[2,256]{1,0:T(2,128)} %copy-done.3, f32[2,256]{1,0:T(2,128)} %copy-done.4, bf16[256,512]{1,0:T(8,128)(2,1)} %constant.31.clone.dmat.dmat_in), custom_call_target="tpu_custom_call" | custom-call | tf_op jit(solution)/shard_map/start/pallas_call | solution.py:472
  44.4 21.0 %all-to-all-done.payload = bf16[128,104,128]{2,1,0:T(8,128)(2,1)S(1)} async-done(((bf16[128,104,128]{2,1,0:T(8,128)(2,1)}), bf16[128,104,128]{2,1,0:T(8,128)(2,1)S(1)}, u32[]{:S(2)}, u32[]{:S(2)}) %all-to-all-start) | async-done | bytes 3407904 | tf_op jit(solution)/shard_map/all_to_all | solution.py:512
  65.4 0.0 copy-start
  65.4 1.7 %copy-done = bf16[128,104,128]{2,1,0:T(8,128)(2,1)} copy-done((bf16[128,104,128]{2,1,0:T(8,128)(2,1)}, bf16[128,104,128]{2,1,0:T(8,128)(2,1)S(1)}, u32[]{:S(2)}) %copy-start) | copy-done | bytes 3407896
  67.1 14.0 %receive.1 = (f32[4,512,256]{2,1,0:T(8,128)}, f32[16,16,256]{2,1,0:T(8,128)}) custom-call(s32[1,2]{1,0:T(1,128)} %fringe.1, bf16[128,104,128]{2,1,0:T(8,128)(2,1)} %copy-done, bf16[512,256]{1,0:T(8,128)(2,1)} %constant.32.clone.weights_in, f32[4,512,256]{2,1,0:T(8,128)} %start.1.rate_in, bf16[256,512]{1,0:T(8,128)(2,1)} %constant.31.clone.dmat.dmat_in), custom_call_target="tpu_custom_call" | custom-call | tf_op jit(solution)/shard_map/receive/pallas_call | solution.py:516
  81.1 7.6 %all-to-all-start.1 = ((f32[16,16,256]{2,1,0:T(8,128)}), f32[16,16,256]{2,1,0:T(8,128)S(1)}, u32[]{:S(2)}, u32[]{:S(2)}) async-start(f32[16,16,256]{2,1,0:T(8,128)} %get-tuple-element.7), calls=%async_computation.1 | async-start | bytes 524288 | tf_op jit(solution)/shard_map/all_to_all | solution.py:537
  88.7 6.9 %inside.1 = f32[4,512,256]{2,1,0:T(8,128)} custom-call(f32[4,512,256]{2,1,0:T(8,128)} %get-tuple-element.8.rate, bf16[256,512]{1,0:T(8,128)(2,1)} %constant.31.clone.dmat.dmat_in, f32[4,512,256]{2,1,0:T(8,128)} %acoustic.1), custom_call_target="tpu_custom_call" | custom-call | tf_op jit(solution)/shard_map/inside/pallas_call | solution.py:538
  95.6 2.0 %all-to-all-done.1.got = f32[16,16,256]{2,1,0:T(8,128)S(1)} async-done(((f32[16,16,256]{2,1,0:T(8,128)}), f32[16,16,256]{2,1,0:T(8,128)S(1)}, u32[]{:S(2)}, u32[]{:S(2)}) %all-to-all-start.1) | async-done | bytes 262176 | tf_op jit(solution)/shard_map/all_to_all | solution.py:537
  97.6 0.0 copy-start.1
  97.6 0.7 copy-done.1
  98.3 2.2 %edges.1 = f32[4,512,256]{2,1,0:T(8,128)} custom-call(s32[1]{0:T(128)} %bitcast.here_at, f32[16,16,256]{2,1,0:T(8,128)} %copy-done.1, bf16[256,512]{1,0:T(8,128)(2,1)} %constant.31.clone.dmat.dmat_in, f32[4,512,256]{2,1,0:T(8,128)} %inside.1), custom_call_target="tpu_custom_call", output_to_operand_aliasing={{}: (3, {})} | custom-call | tf_op jit(solution)/shard_map/edges/pallas_call | solution.py:350
  (2 shorter events, 0.0 us)
Async XLA Ops:
  9.9 11.5 %copy-start.2 = (s32[1,2]{1,0:T(1,128)S(1)}, s32[1,2]{1,0:T(1,128)}, u32[]{:S(2)}) copy-start(s32[1,2]{1,0:T(1,128)} %fringe.1) | copy-start | bytes 28
  9.9 55.5 %all-to-all-start = ((bf16[128,104,128]{2,1,0:T(8,128)(2,1)}), bf16[128,104,128]{2,1,0:T(8,128)(2,1)S(1)}, u32[]{:S(2)}, u32[]{:S(2)}) async-start(bf16[128,104,128]{2,1,0:T(8,128)(2,1)} %pack.1), calls=%async_computation | async-start | bytes 6815744 | tf_op jit(solution)/shard_map/all_to_all | solution.py:512
  26.5 7.4 %collective-permute-start = (f32[2,256]{1,0:T(2,128)S(1)}, f32[2,256]{1,0:T(2,128)S(1)}, u32[]{:S(2)}, u32[]{:S(2)}) collective-permute-start(f32[2,256]{1,0:T(2,128)S(1)} %pad_maximum_fusion), channel_id=1, source_target_pairs={{0,1},{1,2},{2,3},{3,4},{4,5},{5,6},{6,7},{7,8},{8,9},{9,10},{10,1... | collective-permute-start | bytes 6152 | tf_op jit(solution)/shard_map/ppermute | solution.py:485
  31.9 7.9 %collective-permute-start.1 = (f32[2,256]{1,0:T(2,128)S(1)}, f32[2,256]{1,0:T(2,128)S(1)}, u32[]{:S(2)}, u32[]{:S(2)}) collective-permute-start(f32[2,256]{1,0:T(2,128)S(1)} %pad_maximum_fusion.1), channel_id=1, source_target_pairs={{1,0},{2,1},{3,2},{4,3},{5,4},{6,5},{7,6},{8,7},{9,8},{10,9},{11,1... | collective-permute-start | bytes 6152 | tf_op jit(solution)/shard_map/ppermute | solution.py:485
  33.9 6.0 %copy-start.3 = (f32[2,256]{1,0:T(2,128)}, f32[2,256]{1,0:T(2,128)S(1)}, u32[]{:S(2)}) copy-start(f32[2,256]{1,0:T(2,128)S(1)} %collective-permute-done.low_ghost) | copy-start | bytes 6148
  39.9 0.6 copy-start.4
  65.4 1.7 %copy-start = (bf16[128,104,128]{2,1,0:T(8,128)(2,1)}, bf16[128,104,128]{2,1,0:T(8,128)(2,1)S(1)}, u32[]{:S(2)}) copy-start(bf16[128,104,128]{2,1,0:T(8,128)(2,1)S(1)} %all-to-all-done.payload) | copy-start | bytes 10223620
  81.1 16.5 %all-to-all-start.1 = ((f32[16,16,256]{2,1,0:T(8,128)}), f32[16,16,256]{2,1,0:T(8,128)S(1)}, u32[]{:S(2)}, u32[]{:S(2)}) async-start(f32[16,16,256]{2,1,0:T(8,128)} %get-tuple-element.7), calls=%async_computation.1 | async-start | bytes 524288 | tf_op jit(solution)/shard_map/all_to_all | solution.py:537
  97.6 0.7 copy-start.1

commit v3 on v2

--- a/solution.py
+++ b/solution.py
@@ -14,10 +14,12 @@
 AXES = ("les", "ac")
 CODE_ROWS = 8
 GROUP = 16
-PARTS = 4
+PARTS = 2
 MIB = 1 << 20
 VMEM_LIMIT = 60 * MIB
-PAD = 8
+DONORS_LIMIT = 60 * MIB
+EDGES_LIMIT = 32 * MIB
+WINDOW = 5
 
 
 def lagrange_weights(coarse, fine):
@@ -168,7 +170,7 @@
         leave(g).wait()
         return carry
 
-    lax.fori_loop(0, devices // GROUP, group, 0)
+    lax.fori_loop(0, devices // GROUP, group, 0, unroll=True)
     lax.fori_loop(0, devices // GROUP, gone, 0)
 
 
@@ -212,6 +214,12 @@
     )
 
 
+def dx_rounded(field, dmat):
+    return jnp.dot(
+        field.astype(jnp.bfloat16), dmat[:, :field.shape[-1]], preferred_element_type=jnp.float32
+    )
+
+
 def dy_inside(field):
     lines = field.shape[0]
     at = lax.broadcasted_iota(jnp.int32, field.shape, 0)
@@ -220,7 +228,7 @@
     return (above - below) * 0.5
 
 
-def homogeneous(state, dmat):
+def homogeneous(state, dmat, dx=dx):
     field = [state[c][...] for c in range(4)]
     dx_p, dx_u = dx(field[0], dmat), dx(field[1], dmat)
     yield 0, -ADVECT * dx_p - dx_u - dy_inside(field[2])
@@ -229,22 +237,21 @@
     yield 3, -ADVECT * dx(field[3], dmat)
 
 
-def start_kernel(state, low_ghost, high_ghost, dmat, out):
-    lines = state.shape[1]
+def start_kernel(fringe, state, low_ghost, high_ghost, dmat, out, near):
+    lines, cells = state.shape[1:]
     for c, value in homogeneous(state, dmat):
         out[c] = value
     for c, n in ((0, 1), (2, 0)):
         out[c, 0:1, :] += 0.5 * low_ghost[n:n + 1]
         out[c, lines - 1:lines, :] -= 0.5 * high_ghost[n:n + 1]
-
-
-def inside_kernel(rate, dmat, acoustic, out, one, two):
-    for c, value in homogeneous(rate, dmat):
-        one[c] = rate[c] + FIRST * value
-    for c, value in homogeneous(one, dmat):
-        two[c] = rate[c] + SECOND * value
-    for c, value in homogeneous(two, dmat):
-        out[c] = acoustic[c] + STEP * (rate[c] + THIRD * value)
+    near[...] = jnp.zeros_like(near)
+    for n in range(2):
+        for c in range(3):
+            for k in range(WINDOW):
+                line = fringe[0, n] + (k - 2)
+                row = out[c, pl.ds(jnp.clip(line, 0, lines - 1), 1), :]
+                at = (n * 3 + c) * 8 + k
+                near[at:at + 1, :] = jnp.where((line >= 0) & (line < lines), row, 0.0)
 
 
 FIRST, SECOND, THIRD = STEP / 4, STEP / 3, STEP / 2
@@ -355,82 +362,71 @@
         out_specs=block,
         scratch_shapes=[pltpu.VMEM((2, fields, 8, cells), jnp.float32)],
         input_output_aliases={3: 0},
-        compiler_params=pltpu.CompilerParams(vmem_limit_bytes=VMEM_LIMIT),
+        compiler_params=pltpu.CompilerParams(vmem_limit_bytes=EDGES_LIMIT),
         name="edges",
     )(here_at, got, dmat, inside)
 
 
-def receive_kernel(
-    fringe, payload, weights_in, rate_in, dmat_in, out, sent,
-    held, lands, rows, total, weights, rate, dmat, state, bundle, arrived, left,
+def codes_of(payload, capacity):
+    per = 128 // capacity
+    codes = f32(payload[:, 3 * capacity:, :])
+    codes = codes.reshape(payload.shape[0] // per, per, CODE_ROWS, 128).sum(axis=1)
+    return codes.sum(axis=1)
+
+
+def in_one_row(values):
+    return jnp.concatenate([values[n:n + 1, :] for n in range(values.shape[0])], axis=1)
+
+
+def donors_kernel(
+    lines, fringe, payload, weights_in, near_in, dmat_in, sent,
+    rows, bundle, weights, near_rows, dmat, arrived,
 ):
+    copies = [
+        pltpu.make_async_copy(src, dst, arrived.at[k])
+        for k, (src, dst) in enumerate(
+            ((weights_in, weights), (near_in, near_rows), (dmat_in, dmat))
+        )
+    ]
+    for copy in copies:
+        copy.start()
     devices, height, coarse = payload.shape
     capacity = (height - CODE_ROWS) // 3
-    lines = rate.shape[1]
-    cells = rate.shape[2]
-    part = devices // PARTS
-    copies = [
-        pltpu.make_async_copy(
-            payload.at[k * part:(k + 1) * part], held.at[k * part:(k + 1) * part], arrived.at[k]
+    slots = devices * capacity
+    cells = weights.shape[1]
+    codes = in_one_row(codes_of(payload, capacity))
+    for c in range(2):
+        rows[:, c * coarse:(c + 1) * coarse] = payload[
+            :, c * capacity:(c + 1) * capacity, :
+        ].reshape(slots, coarse)
+    for copy in copies:
+        copy.wait()
+    side = 24
+    at = lax.broadcasted_iota(jnp.int32, (2 * side, 1), 0)
+    base = jnp.where(at < side, fringe[0, 0], fringe[0, 1])
+    combo = f32((base - 2) * PHASES + at % side)
+    lands = jnp.where(codes == combo, 1.0, 0.0).astype(jnp.bfloat16)
+    gathered = jnp.dot(lands, rows[...], preferred_element_type=jnp.float32)
+    source = jnp.zeros((4 * side, cells), jnp.float32)
+    both = jnp.concatenate([gathered[:, :coarse], gathered[:, coarse:]], axis=0)
+    phase = lax.broadcasted_iota(jnp.int32, both.shape, 0) % PHASES
+    for o in range(PHASES):
+        chosen = jnp.where(phase == o, both, 0.0).astype(jnp.bfloat16)
+        source += jnp.dot(
+            chosen, weights[o * coarse:(o + 1) * coarse, :], preferred_element_type=jnp.float32
         )
-        for k in range(PARTS)
-    ]
-    others = [
-        pltpu.make_async_copy(src, dst, arrived.at[PARTS + k])
-        for k, (src, dst) in enumerate(((weights_in, weights), (rate_in, rate), (dmat_in, dmat)))
-    ]
-    for copy in copies + others:
-        copy.start()
-    per = 128 // capacity
-    tiles = part // per
-    slots = part * capacity
-    one, zero = jnp.bfloat16(1), jnp.bfloat16(0)
-    row16 = lax.broadcasted_iota(jnp.int32, (16, slots), 0)
-    for k, copy in enumerate(copies):
-        copy.wait()
-        mine = held.at[k * part:(k + 1) * part]
-        codes = f32(mine[:, 3 * capacity:, :])
-        codes = codes.reshape(tiles, per, CODE_ROWS, 128).sum(axis=1)
-        codes = codes.sum(axis=1).astype(jnp.int32)
-        phases = f32(codes % PHASES)
-        phases = jnp.concatenate([phases, jnp.zeros((128 - tiles, 128), jnp.float32)], axis=0).T
-        target = f32(codes // PHASES - lines // 2)
-        target = jnp.concatenate([target[n:n + 1, :] for n in range(tiles)], axis=1)
-        target = jnp.broadcast_to(target, (16, slots)).astype(jnp.bfloat16)
-        for n in range(lines // 16):
-            line = f32(row16 + (16 * n - lines // 2)).astype(jnp.bfloat16)
-            lands[16 * n:16 * (n + 1), :] = jnp.where(target == line, one, zero)
-        for n in range(tiles):
-            phase = jnp.broadcast_to(phases[:, n:n + 1], (128, coarse)).astype(jnp.bfloat16)
-            for c in range(3):
-                values = mine[n * per:(n + 1) * per, c * capacity:(c + 1) * capacity, :]
-                values = values.reshape(128, coarse)
-                for o in range(PHASES):
-                    at = (c * PHASES + o) * coarse
-                    rows[128 * n:128 * (n + 1), at:at + coarse] = jnp.where(
-                        phase == jnp.bfloat16(o), values, zero
-                    )
-        landed = jnp.dot(lands[...], rows[...], preferred_element_type=jnp.float32)
-        total[...] = landed if k == 0 else total[...] + landed
-    for copy in others:
-        copy.wait()
-    inner = slice(PAD, PAD + lines)
-    state[:, :PAD, :] = jnp.zeros((4, PAD, cells), jnp.float32)
-    state[:, PAD + lines:, :] = jnp.zeros((4, PAD, cells), jnp.float32)
-    state[0, inner, :] = rate[0]
-    deep = PHASES * coarse
-    for c in range(3):
-        gathered = total[:, c * deep:(c + 1) * deep].astype(jnp.bfloat16)
-        source = jnp.dot(gathered, weights[...], preferred_element_type=jnp.float32)
-        state[c + 1, inner, :] = rate[c + 1] - source
-    leave = pltpu.make_async_copy(state.at[:, inner, :], out, left.at[0])
-    leave.start()
+    source = source.reshape(4 * side // PHASES, PHASES, cells).sum(axis=1)
+
+    def rate_row(n, c, k):
+        first = (n * 3 + c) * 8 + k
+        row = near_rows[first:first + 1, :]
+        if c > 0:
+            first = (c - 1) * 2 * side // PHASES + n * side // PHASES + k
+            row = row - source[first:first + 1]
+        return row
 
     blank = jnp.zeros((1, cells), jnp.float32)
-    near = [
-        [[state[c, pl.ds(PAD + fringe[0, n] + k, 1), :] for k in range(-2, 3)] for c in range(3)]
-        for n in range(2)
-    ]
+    near = [[[rate_row(n, c, k) for k in range(WINDOW)] for c in range(3)] for n in range(2)]
     slopes = [near[n][c][k] for n in range(2) for c in range(3) for k in (1, 2, 3)]
     slopes = dx(jnp.concatenate(slopes + [blank] * 6, axis=0), dmat)
     stage = []
@@ -458,14 +454,84 @@
         dp, du, dv = (slopes[3 * n + c:3 * n + c + 1] for c in range(3))
         last_p = near[n][0][2] + SECOND * (-ADVECT * dp - du - 0.5 * (v[2] - v[0]))
         last_v = near[n][2][2] + SECOND * (-ADVECT * dv - 0.5 * (p[2] - p[0]))
-        for level, pair in enumerate(((near[n][0][2], near[n][2][2]), (p[1], v[1]), (last_p, last_v))):
+        levels = (near[n][0][2], near[n][2][2]), (p[1], v[1]), (last_p, last_v)
+        for level, pair in enumerate(levels):
             for k in range(2):
                 at = 4 * level + 2 * n + k
                 bundle[at:at + 1, :] = pair[k]
         bundle[12 + n:13 + n, :] = jnp.full((1, cells), (fringe[0, n] + 1).astype(jnp.float32))
         bundle[14 + n:15 + n, :] = blank
     sent[...] = jnp.broadcast_to(bundle[...][None], sent.shape)
-    leave.wait()
+
+
+def receive_kernel(
+    payload, weights_in, rate_in, dmat_in, acoustic_in, out,
+    held, lands, rows, total, weights, rate, dmat, acoustic, one, two, arrived, left,
+):
+    devices, height, coarse = payload.shape
+    capacity = (height - CODE_ROWS) // 3
+    lines = rate.shape[1]
+    part = devices // PARTS
+    copies = [
+        pltpu.make_async_copy(
+            payload.at[k * part:(k + 1) * part], held.at[k * part:(k + 1) * part], arrived.at[k]
+        )
+        for k in range(PARTS)
+    ]
+    others = [
+        pltpu.make_async_copy(src, dst, arrived.at[PARTS + k])
+        for k, (src, dst) in enumerate((
+            (weights_in, weights), (rate_in, rate), (dmat_in, dmat), (acoustic_in, acoustic),
+        ))
+    ]
+    for copy in copies + others:
+        copy.start()
+    per = 128 // capacity
+    tiles = part // per
+    slots = part * capacity
+    is_one, zero = jnp.bfloat16(1), jnp.bfloat16(0)
+    row16 = lax.broadcasted_iota(jnp.int32, (16, slots), 0)
+    for k, copy in enumerate(copies):
+        copy.wait()
+        mine = held.at[k * part:(k + 1) * part]
+        slot = k % 2
+        codes = codes_of(mine, capacity).astype(jnp.int32)
+        phases = f32(codes % PHASES)
+        phases = jnp.concatenate([phases, jnp.zeros((128 - tiles, 128), jnp.float32)], axis=0).T
+        target = in_one_row(f32(codes // PHASES - lines // 2))
+        target = jnp.broadcast_to(target, (16, slots)).astype(jnp.bfloat16)
+        for n in range(lines // 16):
+            line = f32(row16 + (16 * n - lines // 2)).astype(jnp.bfloat16)
+            lands[slot, 16 * n:16 * (n + 1), :] = jnp.where(target == line, is_one, zero)
+        for n in range(tiles):
+            phase = jnp.broadcast_to(phases[:, n:n + 1], (128, coarse)).astype(jnp.bfloat16)
+            for c in range(3):
+                values = mine[n * per:(n + 1) * per, c * capacity:(c + 1) * capacity, :]
+                values = values.reshape(128, coarse)
+                for o in range(PHASES):
+                    at = (c * PHASES + o) * coarse
+                    rows[slot, 128 * n:128 * (n + 1), at:at + coarse] = jnp.where(
+                        phase == jnp.bfloat16(o), values, zero
+                    )
+        landed = jnp.dot(lands[slot], rows[slot], preferred_element_type=jnp.float32)
+        total[...] = landed if k == 0 else total[...] + landed
+    for copy in others:
+        copy.wait()
+    deep = PHASES * coarse
+    for c in range(3):
+        gathered = total[:, c * deep:(c + 1) * deep].astype(jnp.bfloat16)
+        rate[c + 1] -= jnp.dot(gathered, weights[...], preferred_element_type=jnp.float32)
+    for c, value in homogeneous(rate, dmat, dx_rounded):
+        one[c] = rate[c] + FIRST * value
+    for c, value in homogeneous(one, dmat, dx_rounded):
+        two[c] = rate[c] + SECOND * value
+    leave = []
+    for c, value in homogeneous(two, dmat, dx_rounded):
+        one[c] = acoustic[c] + STEP * (rate[c] + THIRD * value)
+        leave.append(pltpu.make_async_copy(one.at[c], out.at[c], left.at[c]))
+        leave[-1].start()
+    for copy in leave:
+        copy.wait()
 
 
 def call(kernel, name, inputs, outputs, smem=0):
@@ -510,40 +576,51 @@
         place, velocity, vorticity, cover.T, target_line.T, phase.T, devices, capacity
     )
     payload = lax.all_to_all(payload, AXES, split_axis=0, concat_axis=0, tiled=True)
-    rate = call(start_kernel, "start", (acoustic, *ghosts, dmat), state_type)
+    rate, near = call(
+        start_kernel, "start", (fringe, acoustic, *ghosts, dmat),
+        (state_type, jax.ShapeDtypeStruct((48, cells), jnp.float32)), smem=1,
+    )
     peers = lax.axis_size("ac")
+    sent = pl.pallas_call(
+        functools.partial(donors_kernel, lines),
+        out_shape=jax.ShapeDtypeStruct((peers, 16, cells), jnp.float32),
+        in_specs=[scalars()] + whole(1) + far(3),
+        out_specs=whole(1)[0],
+        scratch_shapes=[
+            pltpu.VMEM((devices * capacity, 2 * coarse), jnp.bfloat16),
+            pltpu.VMEM((16, cells), jnp.float32),
+            pltpu.VMEM(weights.shape, weights.dtype),
+            pltpu.VMEM(near.shape, near.dtype),
+            pltpu.VMEM(dmat.shape, dmat.dtype),
+            pltpu.SemaphoreType.DMA((3,)),
+        ],
+        compiler_params=pltpu.CompilerParams(vmem_limit_bytes=DONORS_LIMIT),
+        name="donors",
+    )(fringe, payload, weights, near, dmat)
+    got = lax.all_to_all(sent, "ac", split_axis=0, concat_axis=0, tiled=True)
     part = devices // PARTS * capacity
-    rate, sent = pl.pallas_call(
+    inside = pl.pallas_call(
         receive_kernel,
-        out_shape=(state_type, jax.ShapeDtypeStruct((peers, 16, cells), jnp.float32)),
-        in_specs=[scalars()] + far(4),
-        out_specs=(far(1)[0], whole(1)[0]),
+        out_shape=state_type,
+        in_specs=far(5),
+        out_specs=far(1)[0],
         scratch_shapes=[
             pltpu.VMEM(payload.shape, payload.dtype),
-            pltpu.VMEM((lines, part), jnp.bfloat16),
-            pltpu.VMEM((part, 3 * PHASES * coarse), jnp.bfloat16),
+            pltpu.VMEM((2, lines, part), jnp.bfloat16),
+            pltpu.VMEM((2, part, 3 * PHASES * coarse), jnp.bfloat16),
             pltpu.VMEM((lines, 3 * PHASES * coarse), jnp.float32),
             pltpu.VMEM(weights.shape, weights.dtype),
             pltpu.VMEM(acoustic.shape, jnp.float32),
             pltpu.VMEM(dmat.shape, dmat.dtype),
-            pltpu.VMEM((4, lines + 2 * PAD, cells), jnp.float32),
-            pltpu.VMEM((16, cells), jnp.float32),
-            pltpu.SemaphoreType.DMA((PARTS + 3,)),
-            pltpu.SemaphoreType.DMA((1,)),
+            pltpu.VMEM(acoustic.shape, jnp.float32),
+            pltpu.VMEM(acoustic.shape, jnp.float32),
+            pltpu.VMEM(acoustic.shape, jnp.float32),
+            pltpu.SemaphoreType.DMA((PARTS + 4,)),
+            pltpu.SemaphoreType.DMA((4,)),
         ],
         compiler_params=pltpu.CompilerParams(vmem_limit_bytes=VMEM_LIMIT),
         name="receive",
-    )(fringe, payload, weights, rate, dmat)
-    got = lax.all_to_all(sent, "ac", split_axis=0, concat_axis=0, tiled=True)
-    inside = pl.pallas_call(
-        inside_kernel,
-        out_shape=state_type,
-        in_specs=whole(3),
-        out_specs=whole(1)[0],
-        scratch_shapes=[pltpu.VMEM(acoustic.shape, jnp.float32)] * 2,
-        compiler_params=pltpu.CompilerParams(vmem_limit_bytes=VMEM_LIMIT),
-        name="inside",
-    )(rate, dmat, acoustic)
+    )(payload, weights, rate, dmat, acoustic)
     return add_edges(inside, dmat, got, lax.axis_index("ac").reshape(1))
 
 

time: 101 us -> 93.2 us (0.923)
  Pallas kernels: 36.9 us -> 31.7 us
  waiting for transfers between devices: 29 us -> 27 us
    pallas_call x1, Pallas kernels: 9.91 us -> 7.26 us  [pack(): pl.pallas_call(pack_kernel, out_shape=jax.ShapeDtypeStruct((devices, 3 *...]
    pallas_call x2, Pallas kernels: 20.9 us -> 18.6 us  [the longest x1 13.6 us: local(): pl.pallas_call(receive_kernel, out_shape=state_type, in_specs=far(5), out...]
    all_to_all x1, waiting for transfers between devices: 2.02 us -> 0.01 us  [local(): got = lax.all_to_all(sent, 'ac', split_axis=0, concat_axis=0, tiled=True)]
  transfers between devices with their start and end apart: 4 -> 4, of which waited for: 3 -> 2; matrix products, arithmetic and copies ran while one was open for 1% -> 1% of each run, Pallas kernels for 11% -> 19%
where the time goes in v3:
time: 93.2 us; the launch traced here: 92.6 us
  Pallas kernels  31.7 us (34%)
  waiting for transfers between devices  27 us (29%)
  starting transfers between devices  26.5 us (28%)
  between operations  3.78 us (4%)
  local copies, waits for them, and re-layouts  3.64 us (4%)
    all_to_all x1, waiting for transfers between devices, local(): lax.all_to_all(payload, AXES, split_axis=0, concat_axis=0, tiled=True)  21 us
    pallas_call x1, Pallas kernels, local(): pl.pallas_call(receive_kernel, out_shape=state_type, in_specs=far(5), out...  13.6 us
    all_to_all x1, starting transfers between devices, local(): lax.all_to_all(payload, AXES, split_axis=0, concat_axis=0, tiled=True)  11.5 us
    all_to_all x1, starting transfers between devices, local(): got = lax.all_to_all(sent, 'ac', split_axis=0, concat_axis=0, tiled=True)  7.63 us
    ppermute x2, starting transfers between devices, shifted(): return lax.ppermute(x, 'ac', pairs)  7.36 us
    pallas_call x1, Pallas kernels, pack(): pl.pallas_call(pack_kernel, out_shape=jax.ShapeDtypeStruct((devices, 3 *...  7.26 us
    ppermute x2, waiting for transfers between devices, shifted(): return lax.ppermute(x, 'ac', pairs)  5.99 us
    pallas_call x1, Pallas kernels, local(): pl.pallas_call(functools.partial(donors_kernel, lines), out_shape=jax.Sha...  4.96 us
  transfers between devices with their start and end apart: 4, of which 2 were waited for; matrix products, arithmetic and copies ran while one was open for 1% of the time, Pallas kernels for 19%

profile of v3, /device:TPU:1, one launch (start us, length us, event | category | flops | bytes accessed | tf_op | source)
XLA Modules:
  0.0 92.6 jit_solution(16345091517398939665)
XLA Ops:
  0.0 7.3 %pack.1 = bf16[128,104,128]{2,1,0:T(8,128)(2,1)} custom-call(s32[1]{0:T(128)} %bitcast.1.place, bf16[3,1024,128]{2,1,0:T(8,128)(2,1)} %velocity.1, bf16[3,1024,128]{2,1,0:T(8,128)(2,1)} %vorticity.1, s32[2,1024]{1,0:T(2,128)} %bitcast.15, s32[2,1024]{1,0:T(2,128)} %bitcast.16, s32[2,1024]{1,0:T(2,128)} %bitcast.17), custom_call_target="tpu_custom_call" | custom-call | tf_op jit(solution)/shard_map/pack/pallas_call | solution.py:179
  7.3 0.0 copy-start.2
  7.3 11.5 %all-to-all-start = ((bf16[128,104,128]{2,1,0:T(8,128)(2,1)}), bf16[128,104,128]{2,1,0:T(8,128)(2,1)S(1)}, u32[]{:S(2)}, u32[]{:S(2)}) async-start(bf16[128,104,128]{2,1,0:T(8,128)(2,1)} %pack.1), calls=%async_computation | async-start | bytes 6815744 | tf_op jit(solution)/shard_map/all_to_all | solution.py:578
  18.8 0.0 copy-done.2
  18.8 0.6 fusion
  23.0 0.8 dynamic-slice_bitcast_fusion.1
  23.8 5.4 %collective-permute-start = (f32[2,256]{1,0:T(2,128)S(1)}, f32[2,256]{1,0:T(2,128)S(1)}, u32[]{:S(2)}, u32[]{:S(2)}) collective-permute-start(f32[2,256]{1,0:T(2,128)S(1)} %pad_maximum_fusion), channel_id=1, source_target_pairs={{0,1},{1,2},{2,3},{3,4},{4,5},{5,6},{6,7},{7,8},{8,9},{9,10},{10,1... | collective-permute-start | bytes 6152 | tf_op jit(solution)/shard_map/ppermute | solution.py:551
  29.3 1.9 %collective-permute-start.1 = (f32[2,256]{1,0:T(2,128)S(1)}, f32[2,256]{1,0:T(2,128)S(1)}, u32[]{:S(2)}, u32[]{:S(2)}) collective-permute-start(f32[2,256]{1,0:T(2,128)S(1)} %pad_maximum_fusion.1), channel_id=1, source_target_pairs={{1,0},{2,1},{3,2},{4,3},{5,4},{6,5},{7,6},{8,7},{9,8},{10,9},{11,1... | collective-permute-start | bytes 6152 | tf_op jit(solution)/shard_map/ppermute | solution.py:551
  31.2 0.0 collective-permute-done.low_ghost
  31.2 0.0 copy-start.3
  31.2 6.0 %collective-permute-done.1.high_ghost = f32[2,256]{1,0:T(2,128)S(1)} collective-permute-done((f32[2,256]{1,0:T(2,128)S(1)}, f32[2,256]{1,0:T(2,128)S(1)}, u32[]{:S(2)}, u32[]{:S(2)}) %collective-permute-start.1) | collective-permute-done | bytes 2080 | tf_op jit(solution)/shard_map/ppermute | solution.py:551
  37.2 0.0 copy-done.3
  37.2 0.0 copy-start.4
  37.2 0.6 copy-done.4
  37.8 4.0 %start.1 = (f32[4,512,256]{2,1,0:T(8,128)}, f32[48,256]{1,0:T(8,128)}) custom-call(s32[1,2]{1,0:T(1,128)} %fringe.3, f32[4,512,256]{2,1,0:T(8,128)} %acoustic_in.1, f32[2,256]{1,0:T(2,128)} %copy-done.3, f32[2,256]{1,0:T(2,128)} %copy-done.4, bf16[256,512]{1,0:T(8,128)(2,1)} %constant.31.clone.dmat.dmat_in), custom_call_target="tpu_custom_call" | custom-call | tf_op jit(solution)/shard_map/start/pallas_call | solution.py:538
  41.8 21.0 %all-to-all-done.payload = bf16[128,104,128]{2,1,0:T(8,128)(2,1)S(1)} async-done(((bf16[128,104,128]{2,1,0:T(8,128)(2,1)}), bf16[128,104,128]{2,1,0:T(8,128)(2,1)S(1)}, u32[]{:S(2)}, u32[]{:S(2)}) %all-to-all-start) | async-done | bytes 3407904 | tf_op jit(solution)/shard_map/all_to_all | solution.py:578
  62.8 0.0 copy-start.1
  62.8 1.7 %copy-done.1 = bf16[128,104,128]{2,1,0:T(8,128)(2,1)} copy-done((bf16[128,104,128]{2,1,0:T(8,128)(2,1)}, bf16[128,104,128]{2,1,0:T(8,128)(2,1)S(1)}, u32[]{:S(2)}) %copy-start.1) | copy-done | bytes 3407896
  64.5 5.0 %donors.1 = f32[16,16,256]{2,1,0:T(8,128)} custom-call(s32[1,2]{1,0:T(1,128)} %fringe.3, bf16[128,104,128]{2,1,0:T(8,128)(2,1)} %copy-done.1, bf16[512,256]{1,0:T(8,128)(2,1)} %constant.32.clone.weights_in, f32[48,256]{1,0:T(8,128)} %get-tuple-element.7.near_in, bf16[256,512]{1,0:T(8,128)(2,1)} %constant.31.clone.dmat.dmat_in), custom_call_target="tpu_custom_call" | custom-call | tf_op jit(solution)/shard_map/donors/pallas_call | solution.py:584
  69.5 7.6 %all-to-all-start.1 = ((f32[16,16,256]{2,1,0:T(8,128)}), f32[16,16,256]{2,1,0:T(8,128)S(1)}, u32[]{:S(2)}, u32[]{:S(2)}) async-start(f32[16,16,256]{2,1,0:T(8,128)} %donors.1), calls=%async_computation.1 | async-start | bytes 524288 | tf_op jit(solution)/shard_map/all_to_all | solution.py:600
  77.1 0.0 copy-start
  77.1 13.6 %receive.1.inside = f32[4,512,256]{2,1,0:T(8,128)} custom-call(bf16[128,104,128]{2,1,0:T(8,128)(2,1)} %copy-done.1, bf16[512,256]{1,0:T(8,128)(2,1)} %constant.32.clone.weights_in, f32[4,512,256]{2,1,0:T(8,128)} %get-tuple-element.8.rate_in, bf16[256,512]{1,0:T(8,128)(2,1)} %constant.31.clone.dmat.dmat_in, f32[4,512,256]{2,1,0:T(8,128)} %acoustic_in.1), custom_call_target="tpu_custom_call" | custom-call | tf_op jit(solution)/shard_map/receive/pallas_call | solution.py:602
  90.7 0.0 all-to-all-done.1.got
  90.7 0.0 copy-done
  90.7 1.9 %edges.1 = f32[4,512,256]{2,1,0:T(8,128)} custom-call(s32[1]{0:T(128)} %bitcast.here_at, f32[16,16,256]{2,1,0:T(8,128)S(1)} %all-to-all-done.1.got, bf16[256,512]{1,0:T(8,128)(2,1)S(1)} %copy-done, f32[4,512,256]{2,1,0:T(8,128)} %receive.1.inside), custom_call_target="tpu_custom_call", output_to_operand_aliasing={{}: (3, {})} | custom-call | tf_op jit(solution)/shard_map/edges/pallas_call | solution.py:357
  (2 shorter events, 0.0 us)
Async XLA Ops:
  7.3 11.5 %copy-start.2 = (s32[1,2]{1,0:T(1,128)S(1)}, s32[1,2]{1,0:T(1,128)}, u32[]{:S(2)}) copy-start(s32[1,2]{1,0:T(1,128)} %fringe.3) | copy-start | bytes 28
  7.3 55.5 %all-to-all-start = ((bf16[128,104,128]{2,1,0:T(8,128)(2,1)}), bf16[128,104,128]{2,1,0:T(8,128)(2,1)S(1)}, u32[]{:S(2)}, u32[]{:S(2)}) async-start(bf16[128,104,128]{2,1,0:T(8,128)(2,1)} %pack.1), calls=%async_computation | async-start | bytes 6815744 | tf_op jit(solution)/shard_map/all_to_all | solution.py:578
  23.8 7.4 %collective-permute-start = (f32[2,256]{1,0:T(2,128)S(1)}, f32[2,256]{1,0:T(2,128)S(1)}, u32[]{:S(2)}, u32[]{:S(2)}) collective-permute-start(f32[2,256]{1,0:T(2,128)S(1)} %pad_maximum_fusion), channel_id=1, source_target_pairs={{0,1},{1,2},{2,3},{3,4},{4,5},{5,6},{6,7},{7,8},{8,9},{9,10},{10,1... | collective-permute-start | bytes 6152 | tf_op jit(solution)/shard_map/ppermute | solution.py:551
  29.3 7.9 %collective-permute-start.1 = (f32[2,256]{1,0:T(2,128)S(1)}, f32[2,256]{1,0:T(2,128)S(1)}, u32[]{:S(2)}, u32[]{:S(2)}) collective-permute-start(f32[2,256]{1,0:T(2,128)S(1)} %pad_maximum_fusion.1), channel_id=1, source_target_pairs={{1,0},{2,1},{3,2},{4,3},{5,4},{6,5},{7,6},{8,7},{9,8},{10,9},{11,1... | collective-permute-start | bytes 6152 | tf_op jit(solution)/shard_map/ppermute | solution.py:551
  31.2 6.0 %copy-start.3 = (f32[2,256]{1,0:T(2,128)}, f32[2,256]{1,0:T(2,128)S(1)}, u32[]{:S(2)}) copy-start(f32[2,256]{1,0:T(2,128)S(1)} %collective-permute-done.low_ghost) | copy-start | bytes 6148
  37.2 0.6 copy-start.4
  62.8 1.7 %copy-start.1 = (bf16[128,104,128]{2,1,0:T(8,128)(2,1)}, bf16[128,104,128]{2,1,0:T(8,128)(2,1)S(1)}, u32[]{:S(2)}) copy-start(bf16[128,104,128]{2,1,0:T(8,128)(2,1)S(1)} %all-to-all-done.payload) | copy-start | bytes 10223620
  69.5 21.2 %all-to-all-start.1 = ((f32[16,16,256]{2,1,0:T(8,128)}), f32[16,16,256]{2,1,0:T(8,128)S(1)}, u32[]{:S(2)}, u32[]{:S(2)}) async-start(f32[16,16,256]{2,1,0:T(8,128)} %donors.1), calls=%async_computation.1 | async-start | bytes 524288 | tf_op jit(solution)/shard_map/all_to_all | solution.py:600
  77.1 13.6 %copy-start = (bf16[256,512]{1,0:T(8,128)(2,1)S(1)}, bf16[256,512]{1,0:T(8,128)(2,1)}, u32[]{:S(2)}) copy-start(bf16[256,512]{1,0:T(8,128)(2,1)} %constant.31.clone.dmat.dmat_in) | copy-start | bytes 786436

commit v4 on v3

--- a/solution.py
+++ b/solution.py
@@ -17,7 +17,7 @@
 PARTS = 2
 MIB = 1 << 20
 VMEM_LIMIT = 60 * MIB
-DONORS_LIMIT = 60 * MIB
+DONORS_LIMIT = 52000 << 10
 EDGES_LIMIT = 32 * MIB
 WINDOW = 5
 
@@ -466,7 +466,7 @@
 
 def receive_kernel(
     payload, weights_in, rate_in, dmat_in, acoustic_in, out,
-    held, lands, rows, total, weights, rate, dmat, acoustic, one, two, arrived, left,
+    held, total, weights, rate, dmat, acoustic, one, two, arrived, left,
 ):
     devices, height, coarse = payload.shape
     capacity = (height - CODE_ROWS) // 3
@@ -494,27 +494,47 @@
     for k, copy in enumerate(copies):
         copy.wait()
         mine = held.at[k * part:(k + 1) * part]
-        slot = k % 2
         codes = codes_of(mine, capacity).astype(jnp.int32)
         phases = f32(codes % PHASES)
         phases = jnp.concatenate([phases, jnp.zeros((128 - tiles, 128), jnp.float32)], axis=0).T
         target = in_one_row(f32(codes // PHASES - lines // 2))
         target = jnp.broadcast_to(target, (16, slots)).astype(jnp.bfloat16)
-        for n in range(lines // 16):
-            line = f32(row16 + (16 * n - lines // 2)).astype(jnp.bfloat16)
-            lands[slot, 16 * n:16 * (n + 1), :] = jnp.where(target == line, is_one, zero)
-        for n in range(tiles):
-            phase = jnp.broadcast_to(phases[:, n:n + 1], (128, coarse)).astype(jnp.bfloat16)
-            for c in range(3):
+        lands = jnp.concatenate(
+            [
+                jnp.where(
+                    target == f32(row16 + (16 * n - lines // 2)).astype(jnp.bfloat16), is_one, zero
+                )
+                for n in range(lines // 16)
+            ],
+            axis=0,
+        )
+        phase_of = [
+            jnp.broadcast_to(phases[:, n:n + 1], (128, coarse)).astype(jnp.bfloat16)
+            for n in range(tiles)
+        ]
+
+        def rows_of(c, o):
+            pieces = []
+            for n in range(tiles):
                 values = mine[n * per:(n + 1) * per, c * capacity:(c + 1) * capacity, :]
                 values = values.reshape(128, coarse)
-                for o in range(PHASES):
-                    at = (c * PHASES + o) * coarse
-                    rows[slot, 128 * n:128 * (n + 1), at:at + coarse] = jnp.where(
-                        phase == jnp.bfloat16(o), values, zero
-                    )
-        landed = jnp.dot(lands[slot], rows[slot], preferred_element_type=jnp.float32)
-        total[...] = landed if k == 0 else total[...] + landed
+                pieces.append(jnp.concatenate(
+                    [
+                        jnp.where(phase_of[n] == jnp.bfloat16(p), values, zero)
+                        for p in (o, o + 1)
+                    ],
+                    axis=1,
+                ))
+            return jnp.concatenate(pieces, axis=0)
+
+        wanted = [(c, o) for c in range(3) for o in range(0, PHASES, 2)]
+        rows = rows_of(*wanted[0])
+        for n, (c, o) in enumerate(wanted):
+            later = rows_of(*wanted[n + 1]) if n + 1 < len(wanted) else None
+            landed = jnp.dot(lands, rows, preferred_element_type=jnp.float32)
+            columns = slice((c * PHASES + o) * coarse, (c * PHASES + o + 2) * coarse)
+            total[:, columns] = landed if k == 0 else total[:, columns] + landed
+            rows = later
     for copy in others:
         copy.wait()
     deep = PHASES * coarse
@@ -540,7 +560,7 @@
         out_shape=outputs,
         in_specs=[scalars()] * smem + whole(len(inputs) - smem),
         out_specs=jax.tree.map(lambda _: whole(1)[0], outputs),
-        compiler_params=pltpu.CompilerParams(vmem_limit_bytes=VMEM_LIMIT),
+        compiler_params=pltpu.CompilerParams(vmem_limit_bytes=52000 << 10),
         name=name,
     )(*inputs)
 
@@ -598,7 +618,6 @@
         name="donors",
     )(fringe, payload, weights, near, dmat)
     got = lax.all_to_all(sent, "ac", split_axis=0, concat_axis=0, tiled=True)
-    part = devices // PARTS * capacity
     inside = pl.pallas_call(
         receive_kernel,
         out_shape=state_type,
@@ -606,8 +625,6 @@
         out_specs=far(1)[0],
         scratch_shapes=[
             pltpu.VMEM(payload.shape, payload.dtype),
-            pltpu.VMEM((2, lines, part), jnp.bfloat16),
-            pltpu.VMEM((2, part, 3 * PHASES * coarse), jnp.bfloat16),
             pltpu.VMEM((lines, 3 * PHASES * coarse), jnp.float32),
             pltpu.VMEM(weights.shape, weights.dtype),
             pltpu.VMEM(acoustic.shape, jnp.float32),

time: 93.2 us -> 88.3 us (0.947)
  Pallas kernels: 31.7 us -> 28.2 us
    pallas_call x1, Pallas kernels: 13.6 us -> 12.1 us  [local(): pl.pallas_call(receive_kernel, out_shape=state_type, in_specs=far(5), out...]
    pallas_call x1, Pallas kernels: 4.01 us -> 2.66 us  [call(): pl.pallas_call(kernel, out_shape=outputs, in_specs=[scalars()] * smem + w...]
    all_to_all x1, starting transfers between devices: 7.63 us -> 6.5 us  [local(): got = lax.all_to_all(sent, 'ac', split_axis=0, concat_axis=0, tiled=True)]
  transfers between devices with their start and end apart: 4 -> 4, of which waited for: 2 -> 2; matrix products, arithmetic and copies ran while one was open for 1% -> 2% of each run, Pallas kernels for 19% -> 17%
where the time goes in v4:
time: 88.3 us; the launch traced here: 87.7 us
  Pallas kernels  28.2 us (32%)
  waiting for transfers between devices  27 us (31%)
  starting transfers between devices  25.8 us (29%)
  between operations  3.95 us (4%)
  local copies, waits for them, and re-layouts  2.76 us (3%)
    all_to_all x1, waiting for transfers between devices, local(): lax.all_to_all(payload, AXES, split_axis=0, concat_axis=0, tiled=True)  21.5 us
    pallas_call x1, Pallas kernels, local(): pl.pallas_call(receive_kernel, out_shape=state_type, in_specs=far(5), out...  12.1 us
    all_to_all x1, starting transfers between devices, local(): lax.all_to_all(payload, AXES, split_axis=0, concat_axis=0, tiled=True)  11.9 us
    ppermute x2, starting transfers between devices, shifted(): return lax.ppermute(x, 'ac', pairs)  7.36 us
    pallas_call x1, Pallas kernels, pack(): pl.pallas_call(pack_kernel, out_shape=jax.ShapeDtypeStruct((devices, 3 *...  7.24 us
    all_to_all x1, starting transfers between devices, local(): got = lax.all_to_all(sent, 'ac', split_axis=0, concat_axis=0, tiled=True)  6.5 us
    ppermute x2, waiting for transfers between devices, shifted(): return lax.ppermute(x, 'ac', pairs)  5.49 us
    pallas_call x1, Pallas kernels, local(): pl.pallas_call(functools.partial(donors_kernel, lines), out_shape=jax.Sha...  4.39 us
  transfers between devices with their start and end apart: 4, of which 2 were waited for; matrix products, arithmetic and copies ran while one was open for 2% of the time, Pallas kernels for 17%

profile of v4, /device:TPU:1, one launch (start us, length us, event | category | flops | bytes accessed | tf_op | source)
XLA Modules:
  0.0 87.7 jit_solution(13567962235186986712)
XLA Ops:
  0.0 7.2 %pack.1 = bf16[128,104,128]{2,1,0:T(8,128)(2,1)} custom-call(s32[1]{0:T(128)} %bitcast.1.place, bf16[3,1024,128]{2,1,0:T(8,128)(2,1)} %velocity.1, bf16[3,1024,128]{2,1,0:T(8,128)(2,1)} %vorticity.1, s32[2,1024]{1,0:T(2,128)} %bitcast.15, s32[2,1024]{1,0:T(2,128)} %bitcast.16, s32[2,1024]{1,0:T(2,128)} %bitcast.17), custom_call_target="tpu_custom_call" | custom-call | tf_op jit(solution)/shard_map/pack/pallas_call | solution.py:179
  7.2 0.0 copy-start.4
  7.3 0.0 copy-start
  7.3 11.9 %all-to-all-start = ((bf16[128,104,128]{2,1,0:T(8,128)(2,1)}), bf16[128,104,128]{2,1,0:T(8,128)(2,1)}, u32[]{:S(2)}, u32[]{:S(2)}) async-start(bf16[128,104,128]{2,1,0:T(8,128)(2,1)} %pack.1), calls=%async_computation | async-start | bytes 6815744 | tf_op jit(solution)/shard_map/all_to_all | solution.py:598
  19.2 0.0 copy-done.4
  19.2 0.0 copy-start.3
  19.2 0.6 fusion
  23.6 0.8 dynamic-slice_bitcast_fusion.1
  24.4 5.4 %collective-permute-start = (f32[2,256]{1,0:T(2,128)S(1)}, f32[2,256]{1,0:T(2,128)S(1)}, u32[]{:S(2)}, u32[]{:S(2)}) collective-permute-start(f32[2,256]{1,0:T(2,128)S(1)} %pad_maximum_fusion), channel_id=1, source_target_pairs={{0,1},{1,2},{2,3},{3,4},{4,5},{5,6},{6,7},{7,8},{8,9},{9,10},{10,1... | collective-permute-start | bytes 6152 | tf_op jit(solution)/shard_map/ppermute | solution.py:571
  29.8 1.9 %collective-permute-start.1 = (f32[2,256]{1,0:T(2,128)S(1)}, f32[2,256]{1,0:T(2,128)S(1)}, u32[]{:S(2)}, u32[]{:S(2)}) collective-permute-start(f32[2,256]{1,0:T(2,128)S(1)} %pad_maximum_fusion.1), channel_id=1, source_target_pairs={{1,0},{2,1},{3,2},{4,3},{5,4},{6,5},{7,6},{8,7},{9,8},{10,9},{11,1... | collective-permute-start | bytes 6152 | tf_op jit(solution)/shard_map/ppermute | solution.py:571
  31.8 0.0 collective-permute-done.low_ghost
  31.8 5.5 %collective-permute-done.1.high_ghost = f32[2,256]{1,0:T(2,128)S(1)} collective-permute-done((f32[2,256]{1,0:T(2,128)S(1)}, f32[2,256]{1,0:T(2,128)S(1)}, u32[]{:S(2)}, u32[]{:S(2)}) %collective-permute-start.1) | collective-permute-done | bytes 2080 | tf_op jit(solution)/shard_map/ppermute | solution.py:571
  37.3 0.0 copy-done
  37.3 2.7 %start.1 = (f32[4,512,256]{2,1,0:T(8,128)S(1)}, f32[48,256]{1,0:T(8,128)S(1)}) custom-call(s32[1,2]{1,0:T(1,128)S(1)} %copy-done.4, f32[4,512,256]{2,1,0:T(8,128)} %acoustic_in.1, f32[2,256]{1,0:T(2,128)S(1)} %collective-permute-done.low_ghost, f32[2,256]{1,0:T(2,128)S(1)} %collective-permute-done.1.high_ghost, bf16[256,512]{1,0:T(8,128)(2,1)S(1)} %copy-done), custom_call_target="tpu_custom_call" | custom-call | tf_op jit(solution)/shard_map/start/pallas_call | solution.py:558
  39.9 0.0 copy-start.2
  39.9 1.4 %copy-done.2 = f32[4,512,256]{2,1,0:T(8,128)} copy-done((f32[4,512,256]{2,1,0:T(8,128)}, f32[4,512,256]{2,1,0:T(8,128)S(1)}, u32[]{:S(2)}) %copy-start.2) | copy-done | bytes 2097176
  41.3 21.5 %all-to-all-done.payload = bf16[128,104,128]{2,1,0:T(8,128)(2,1)} async-done(((bf16[128,104,128]{2,1,0:T(8,128)(2,1)}), bf16[128,104,128]{2,1,0:T(8,128)(2,1)}, u32[]{:S(2)}, u32[]{:S(2)}) %all-to-all-start) | async-done | bytes 3407904 | tf_op jit(solution)/shard_map/all_to_all | solution.py:598
  62.9 0.0 copy-done.3
  62.9 4.4 %donors.1 = f32[16,16,256]{2,1,0:T(8,128)} custom-call(s32[1,2]{1,0:T(1,128)S(1)} %copy-done.4, bf16[128,104,128]{2,1,0:T(8,128)(2,1)} %all-to-all-done.payload, bf16[512,256]{1,0:T(8,128)(2,1)S(1)} %copy-done.3, f32[48,256]{1,0:T(8,128)S(1)} %get-tuple-element.7.near_in, bf16[256,512]{1,0:T(8,128)(2,1)S(1)} %copy-done), custom_call_target="tpu_custom_call" | custom-call | tf_op jit(solution)/shard_map/donors/pallas_call | solution.py:604
  67.3 6.5 %all-to-all-start.1 = ((f32[16,16,256]{2,1,0:T(8,128)}), f32[16,16,256]{2,1,0:T(8,128)S(1)}, u32[]{:S(2)}, u32[]{:S(2)}) async-start(f32[16,16,256]{2,1,0:T(8,128)} %donors.1), calls=%async_computation.1 | async-start | bytes 524288 | tf_op jit(solution)/shard_map/all_to_all | solution.py:620
  73.8 0.0 copy-start.1
  73.8 12.1 %receive.1.inside = f32[4,512,256]{2,1,0:T(8,128)} custom-call(bf16[128,104,128]{2,1,0:T(8,128)(2,1)} %all-to-all-done.payload, bf16[512,256]{1,0:T(8,128)(2,1)} %constant.32.clone.weights_in, f32[4,512,256]{2,1,0:T(8,128)} %copy-done.2, bf16[256,512]{1,0:T(8,128)(2,1)} %constant.31.clone.dmat.dmat_in, f32[4,512,256]{2,1,0:T(8,128)} %acoustic_in.1), custom_call_target="tpu_custom_call" | custom-call | tf_op jit(solution)/shard_map/receive/pallas_call | solution.py:621
  85.8 0.0 all-to-all-done.1.got
  85.9 0.0 copy-done.1
  85.9 1.9 %edges.1 = f32[4,512,256]{2,1,0:T(8,128)} custom-call(s32[1]{0:T(128)} %bitcast.here_at, f32[16,16,256]{2,1,0:T(8,128)S(1)} %all-to-all-done.1.got, bf16[256,512]{1,0:T(8,128)(2,1)S(1)} %copy-done.1, f32[4,512,256]{2,1,0:T(8,128)} %receive.1.inside), custom_call_target="tpu_custom_call", output_to_operand_aliasing={{}: (3, {})} | custom-call | tf_op jit(solution)/shard_map/edges/pallas_call | solution.py:357
  (2 shorter events, 0.0 us)
Async XLA Ops:
  7.2 11.9 %copy-start.4 = (s32[1,2]{1,0:T(1,128)S(1)}, s32[1,2]{1,0:T(1,128)}, u32[]{:S(2)}) copy-start(s32[1,2]{1,0:T(1,128)} %fringe.3) | copy-start | bytes 28
  7.3 30.0 %copy-start = (bf16[256,512]{1,0:T(8,128)(2,1)S(1)}, bf16[256,512]{1,0:T(8,128)(2,1)}, u32[]{:S(2)}) copy-start(bf16[256,512]{1,0:T(8,128)(2,1)} %constant.31.clone.dmat.dmat_in) | copy-start | bytes 786436
  7.3 55.6 %all-to-all-start = ((bf16[128,104,128]{2,1,0:T(8,128)(2,1)}), bf16[128,104,128]{2,1,0:T(8,128)(2,1)}, u32[]{:S(2)}, u32[]{:S(2)}) async-start(bf16[128,104,128]{2,1,0:T(8,128)(2,1)} %pack.1), calls=%async_computation | async-start | bytes 6815744 | tf_op jit(solution)/shard_map/all_to_all | solution.py:598
  19.2 43.7 %copy-start.3 = (bf16[512,256]{1,0:T(8,128)(2,1)S(1)}, bf16[512,256]{1,0:T(8,128)(2,1)}, u32[]{:S(2)}) copy-start(bf16[512,256]{1,0:T(8,128)(2,1)} %constant.32.clone.weights_in) | copy-start | bytes 786436
  24.4 7.4 %collective-permute-start = (f32[2,256]{1,0:T(2,128)S(1)}, f32[2,256]{1,0:T(2,128)S(1)}, u32[]{:S(2)}, u32[]{:S(2)}) collective-permute-start(f32[2,256]{1,0:T(2,128)S(1)} %pad_maximum_fusion), channel_id=1, source_target_pairs={{0,1},{1,2},{2,3},{3,4},{4,5},{5,6},{6,7},{7,8},{8,9},{9,10},{10,1... | collective-permute-start | bytes 6152 | tf_op jit(solution)/shard_map/ppermute | solution.py:571
  29.8 7.4 %collective-permute-start.1 = (f32[2,256]{1,0:T(2,128)S(1)}, f32[2,256]{1,0:T(2,128)S(1)}, u32[]{:S(2)}, u32[]{:S(2)}) collective-permute-start(f32[2,256]{1,0:T(2,128)S(1)} %pad_maximum_fusion.1), channel_id=1, source_target_pairs={{1,0},{2,1},{3,2},{4,3},{5,4},{6,5},{7,6},{8,7},{9,8},{10,9},{11,1... | collective-permute-start | bytes 6152 | tf_op jit(solution)/shard_map/ppermute | solution.py:571
  39.9 1.4 %copy-start.2 = (f32[4,512,256]{2,1,0:T(8,128)}, f32[4,512,256]{2,1,0:T(8,128)S(1)}, u32[]{:S(2)}) copy-start(f32[4,512,256]{2,1,0:T(8,128)S(1)} %get-tuple-element.8.rate_in) | copy-start | bytes 6291460
  67.3 18.6 %all-to-all-start.1 = ((f32[16,16,256]{2,1,0:T(8,128)}), f32[16,16,256]{2,1,0:T(8,128)S(1)}, u32[]{:S(2)}, u32[]{:S(2)}) async-start(f32[16,16,256]{2,1,0:T(8,128)} %donors.1), calls=%async_computation.1 | async-start | bytes 524288 | tf_op jit(solution)/shard_map/all_to_all | solution.py:620
  73.8 12.1 %copy-start.1 = (bf16[256,512]{1,0:T(8,128)(2,1)S(1)}, bf16[256,512]{1,0:T(8,128)(2,1)}, u32[]{:S(2)}) copy-start(bf16[256,512]{1,0:T(8,128)(2,1)} %constant.31.clone.dmat.dmat_in) | copy-start | bytes 786436

commit v5 on v4

--- a/solution.py
+++ b/solution.py
@@ -15,6 +15,7 @@
 CODE_ROWS = 8
 GROUP = 16
 PARTS = 2
+QUARTERS = 4
 MIB = 1 << 20
 VMEM_LIMIT = 60 * MIB
 DONORS_LIMIT = 52000 << 10
@@ -237,13 +238,10 @@
     yield 3, -ADVECT * dx(field[3], dmat)
 
 
-def start_kernel(fringe, state, low_ghost, high_ghost, dmat, out, near):
+def start_kernel(fringe, state, dmat, out, near):
     lines, cells = state.shape[1:]
     for c, value in homogeneous(state, dmat):
         out[c] = value
-    for c, n in ((0, 1), (2, 0)):
-        out[c, 0:1, :] += 0.5 * low_ghost[n:n + 1]
-        out[c, lines - 1:lines, :] -= 0.5 * high_ghost[n:n + 1]
     near[...] = jnp.zeros_like(near)
     for n in range(2):
         for c in range(3):
@@ -379,34 +377,49 @@
 
 
 def donors_kernel(
-    lines, fringe, payload, weights_in, near_in, dmat_in, sent,
-    rows, bundle, weights, near_rows, dmat, arrived,
+    lines, fringe, low_in, high_in, payload, weights_in, near_in, dmat_in, sent,
+    held, low_ghost, high_ghost, bundle, weights, near_rows, dmat, arrived, landed,
 ):
     copies = [
         pltpu.make_async_copy(src, dst, arrived.at[k])
         for k, (src, dst) in enumerate(
-            ((weights_in, weights), (near_in, near_rows), (dmat_in, dmat))
+            (
+                (weights_in, weights), (near_in, near_rows), (dmat_in, dmat),
+                (low_in, low_ghost), (high_in, high_ghost),
+            )
         )
     ]
-    for copy in copies:
-        copy.start()
     devices, height, coarse = payload.shape
     capacity = (height - CODE_ROWS) // 3
-    slots = devices * capacity
     cells = weights.shape[1]
-    codes = in_one_row(codes_of(payload, capacity))
-    for c in range(2):
-        rows[:, c * coarse:(c + 1) * coarse] = payload[
-            :, c * capacity:(c + 1) * capacity, :
-        ].reshape(slots, coarse)
-    for copy in copies:
-        copy.wait()
+    part = devices // QUARTERS
+    parts = [
+        pltpu.make_async_copy(
+            payload.at[k * part:(k + 1) * part], held.at[k * part:(k + 1) * part], landed.at[k]
+        )
+        for k in range(QUARTERS)
+    ]
+    for copy in parts + copies:
+        copy.start()
     side = 24
     at = lax.broadcasted_iota(jnp.int32, (2 * side, 1), 0)
     base = jnp.where(at < side, fringe[0, 0], fringe[0, 1])
     combo = f32((base - 2) * PHASES + at % side)
-    lands = jnp.where(codes == combo, 1.0, 0.0).astype(jnp.bfloat16)
-    gathered = jnp.dot(lands, rows[...], preferred_element_type=jnp.float32)
+    gathered = jnp.zeros((2 * side, 2 * coarse), jnp.float32)
+    for k, copy in enumerate(parts):
+        copy.wait()
+        mine = held.at[k * part:(k + 1) * part]
+        codes = in_one_row(codes_of(mine, capacity))
+        lands = jnp.where(codes == combo, 1.0, 0.0).astype(jnp.bfloat16)
+        rows = [
+            mine[:, c * capacity:(c + 1) * capacity, :].reshape(part * capacity, coarse)
+            for c in range(2)
+        ]
+        gathered += jnp.dot(
+            lands, jnp.concatenate(rows, axis=1), preferred_element_type=jnp.float32
+        )
+    for copy in copies:
+        copy.wait()
     source = jnp.zeros((4 * side, cells), jnp.float32)
     both = jnp.concatenate([gathered[:, :coarse], gathered[:, coarse:]], axis=0)
     phase = lax.broadcasted_iota(jnp.int32, both.shape, 0) % PHASES
@@ -420,6 +433,11 @@
     def rate_row(n, c, k):
         first = (n * 3 + c) * 8 + k
         row = near_rows[first:first + 1, :]
+        line = fringe[0, n] + (k - 2)
+        if c != 1:
+            other = slice(1, 2) if c == 0 else slice(0, 1)
+            row = row + jnp.where(line == 0, 0.5 * low_ghost[other, :], 0.0)
+            row = row - jnp.where(line == lines - 1, 0.5 * high_ghost[other, :], 0.0)
         if c > 0:
             first = (c - 1) * 2 * side // PHASES + n * side // PHASES + k
             row = row - source[first:first + 1]
@@ -465,8 +483,8 @@
 
 
 def receive_kernel(
-    payload, weights_in, rate_in, dmat_in, acoustic_in, out,
-    held, total, weights, rate, dmat, acoustic, one, two, arrived, left,
+    low_in, high_in, payload, weights_in, rate_in, dmat_in, acoustic_in, out,
+    held, low_ghost, high_ghost, total, weights, rate, dmat, acoustic, one, two, arrived, left,
 ):
     devices, height, coarse = payload.shape
     capacity = (height - CODE_ROWS) // 3
@@ -482,6 +500,7 @@
         pltpu.make_async_copy(src, dst, arrived.at[PARTS + k])
         for k, (src, dst) in enumerate((
             (weights_in, weights), (rate_in, rate), (dmat_in, dmat), (acoustic_in, acoustic),
+            (low_in, low_ghost), (high_in, high_ghost),
         ))
     ]
     for copy in copies + others:
@@ -537,6 +556,9 @@
             rows = later
     for copy in others:
         copy.wait()
+    for c, n in ((0, 1), (2, 0)):
+        rate[c, 0:1, :] += 0.5 * low_ghost[n:n + 1, :]
+        rate[c, lines - 1:lines, :] -= 0.5 * high_ghost[n:n + 1, :]
     deep = PHASES * coarse
     for c in range(3):
         gathered = total[:, c * deep:(c + 1) * deep].astype(jnp.bfloat16)
@@ -597,34 +619,39 @@
     )
     payload = lax.all_to_all(payload, AXES, split_axis=0, concat_axis=0, tiled=True)
     rate, near = call(
-        start_kernel, "start", (fringe, acoustic, *ghosts, dmat),
+        start_kernel, "start", (fringe, acoustic, dmat),
         (state_type, jax.ShapeDtypeStruct((48, cells), jnp.float32)), smem=1,
     )
     peers = lax.axis_size("ac")
     sent = pl.pallas_call(
         functools.partial(donors_kernel, lines),
         out_shape=jax.ShapeDtypeStruct((peers, 16, cells), jnp.float32),
-        in_specs=[scalars()] + whole(1) + far(3),
+        in_specs=[scalars()] + far(6),
         out_specs=whole(1)[0],
         scratch_shapes=[
-            pltpu.VMEM((devices * capacity, 2 * coarse), jnp.bfloat16),
+            pltpu.VMEM(payload.shape, payload.dtype),
+            pltpu.VMEM((2, cells), jnp.float32),
+            pltpu.VMEM((2, cells), jnp.float32),
             pltpu.VMEM((16, cells), jnp.float32),
             pltpu.VMEM(weights.shape, weights.dtype),
             pltpu.VMEM(near.shape, near.dtype),
             pltpu.VMEM(dmat.shape, dmat.dtype),
-            pltpu.SemaphoreType.DMA((3,)),
+            pltpu.SemaphoreType.DMA((5,)),
+            pltpu.SemaphoreType.DMA((QUARTERS,)),
         ],
         compiler_params=pltpu.CompilerParams(vmem_limit_bytes=DONORS_LIMIT),
         name="donors",
-    )(fringe, payload, weights, near, dmat)
+    )(fringe, *ghosts, payload, weights, near, dmat)
     got = lax.all_to_all(sent, "ac", split_axis=0, concat_axis=0, tiled=True)
     inside = pl.pallas_call(
         receive_kernel,
         out_shape=state_type,
-        in_specs=far(5),
+        in_specs=far(7),
         out_specs=far(1)[0],
         scratch_shapes=[
             pltpu.VMEM(payload.shape, payload.dtype),
+            pltpu.VMEM((2, cells), jnp.float32),
+            pltpu.VMEM((2, cells), jnp.float32),
             pltpu.VMEM((lines, 3 * PHASES * coarse), jnp.float32),
             pltpu.VMEM(weights.shape, weights.dtype),
             pltpu.VMEM(acoustic.shape, jnp.float32),
@@ -632,12 +659,12 @@
             pltpu.VMEM(acoustic.shape, jnp.float32),
             pltpu.VMEM(acoustic.shape, jnp.float32),
             pltpu.VMEM(acoustic.shape, jnp.float32),
-            pltpu.SemaphoreType.DMA((PARTS + 4,)),
+            pltpu.SemaphoreType.DMA((PARTS + 6,)),
             pltpu.SemaphoreType.DMA((4,)),
         ],
         compiler_params=pltpu.CompilerParams(vmem_limit_bytes=VMEM_LIMIT),
         name="receive",
-    )(payload, weights, rate, dmat, acoustic)
+    )(*ghosts, payload, weights, rate, dmat, acoustic)
     return add_edges(inside, dmat, got, lax.axis_index("ac").reshape(1))
 
 

time: 88.3 us -> 87.3 us (0.989)
  starting transfers between devices: 25.8 us -> 24.9 us
    ppermute x2, waiting for transfers between devices: 5.49 us -> 0.01 us  [shifted(): return lax.ppermute(x, 'ac', pairs)]
    all_to_all x1, waiting for transfers between devices: 21.5 us -> 27 us  [local(): lax.all_to_all(payload, AXES, split_axis=0, concat_axis=0, tiled=True)]
  transfers between devices with their start and end apart: 4 -> 4, of which waited for: 2 -> 1; matrix products, arithmetic and copies ran while one was open for 2% -> 2% of each run, Pallas kernels for 17% -> 17%
where the time goes in v5:
time: 87.3 us; the launch traced here: 86.7 us
  Pallas kernels  28 us (32%)
  waiting for transfers between devices  27 us (31%)
  starting transfers between devices  24.9 us (29%)
  between operations  4.01 us (5%)
  local copies, waits for them, and re-layouts  2.77 us (3%)
    all_to_all x1, waiting for transfers between devices, local(): lax.all_to_all(payload, AXES, split_axis=0, concat_axis=0, tiled=True)  27 us
    pallas_call x1, Pallas kernels, local(): pl.pallas_call(receive_kernel, out_shape=state_type, in_specs=far(7), out...  12.1 us
    all_to_all x1, starting transfers between devices, local(): lax.all_to_all(payload, AXES, split_axis=0, concat_axis=0, tiled=True)  11.9 us
    ppermute x2, starting transfers between devices, shifted(): return lax.ppermute(x, 'ac', pairs)  7.36 us
    pallas_call x1, Pallas kernels, pack(): pl.pallas_call(pack_kernel, out_shape=jax.ShapeDtypeStruct((devices, 3 *...  7.25 us
    all_to_all x1, starting transfers between devices, local(): got = lax.all_to_all(sent, 'ac', split_axis=0, concat_axis=0, tiled=True)  5.64 us
    pallas_call x1, Pallas kernels, local(): pl.pallas_call(functools.partial(donors_kernel, lines), out_shape=jax.Sha...  4.18 us
    pallas_call x1, Pallas kernels, call(): pl.pallas_call(kernel, out_shape=outputs, in_specs=[scalars()] * smem + w...  2.66 us
  transfers between devices with their start and end apart: 4, of which 1 were waited for; matrix products, arithmetic and copies ran while one was open for 2% of the time, Pallas kernels for 17%

profile of v5, /device:TPU:1, one launch (start us, length us, event | category | flops | bytes accessed | tf_op | source)
XLA Modules:
  0.0 86.7 jit_solution(16500783262040381737)
XLA Ops:
  0.0 7.2 %pack.1 = bf16[128,104,128]{2,1,0:T(8,128)(2,1)} custom-call(s32[1]{0:T(128)} %bitcast.7.place, bf16[3,1024,128]{2,1,0:T(8,128)(2,1)} %velocity.1, bf16[3,1024,128]{2,1,0:T(8,128)(2,1)} %vorticity.1, s32[2,1024]{1,0:T(2,128)} %bitcast.15, s32[2,1024]{1,0:T(2,128)} %bitcast.16, s32[2,1024]{1,0:T(2,128)} %bitcast.17), custom_call_target="tpu_custom_call" | custom-call | tf_op jit(solution)/shard_map/pack/pallas_call | solution.py:180
  7.3 0.0 copy-start.6
  7.3 0.0 copy-start
  7.3 11.9 %all-to-all-start = ((bf16[128,104,128]{2,1,0:T(8,128)(2,1)}), bf16[128,104,128]{2,1,0:T(8,128)(2,1)}, u32[]{:S(2)}, u32[]{:S(2)}) async-start(bf16[128,104,128]{2,1,0:T(8,128)(2,1)} %pack.1), calls=%async_computation | async-start | bytes 6815744 | tf_op jit(solution)/shard_map/all_to_all | solution.py:620
  19.2 0.0 copy-done.6
  19.2 0.0 copy-start.3
  19.2 0.6 fusion
  23.7 0.8 dynamic-slice_bitcast_fusion.1
  24.4 3.0 %collective-permute-start.1 = (f32[2,256]{1,0:T(2,128)S(1)}, f32[2,256]{1,0:T(2,128)S(1)}, u32[]{:S(2)}, u32[]{:S(2)}) collective-permute-start(f32[2,256]{1,0:T(2,128)S(1)} %pad_maximum_fusion.1), channel_id=1, source_target_pairs={{1,0},{2,1},{3,2},{4,3},{5,4},{6,5},{7,6},{8,7},{9,8},{10,9},{11,1... | collective-permute-start | bytes 6152 | tf_op jit(solution)/shard_map/ppermute | solution.py:593
  27.5 4.3 %collective-permute-start = (f32[2,256]{1,0:T(2,128)S(1)}, f32[2,256]{1,0:T(2,128)S(1)}, u32[]{:S(2)}, u32[]{:S(2)}) collective-permute-start(f32[2,256]{1,0:T(2,128)S(1)} %pad_maximum_fusion), channel_id=1, source_target_pairs={{0,1},{1,2},{2,3},{3,4},{4,5},{5,6},{6,7},{7,8},{8,9},{9,10},{10,1... | collective-permute-start | bytes 6152 | tf_op jit(solution)/shard_map/ppermute | solution.py:593
  31.8 0.0 copy-done
  31.8 2.7 %start.1 = (f32[4,512,256]{2,1,0:T(8,128)S(1)}, f32[48,256]{1,0:T(8,128)S(1)}) custom-call(s32[1,2]{1,0:T(1,128)S(1)} %copy-done.6, f32[4,512,256]{2,1,0:T(8,128)} %acoustic_in.1, bf16[256,512]{1,0:T(8,128)(2,1)S(1)} %copy-done), custom_call_target="tpu_custom_call" | custom-call | tf_op jit(solution)/shard_map/start/pallas_call | solution.py:580
  34.5 0.0 copy-start.2
  34.5 1.4 %copy-done.2 = f32[4,512,256]{2,1,0:T(8,128)} copy-done((f32[4,512,256]{2,1,0:T(8,128)}, f32[4,512,256]{2,1,0:T(8,128)S(1)}, u32[]{:S(2)}) %copy-start.2) | copy-done | bytes 2097176
  35.9 0.0 collective-permute-done.1.high_in
  35.9 0.0 copy-start.4
  35.9 0.0 collective-permute-done.low_in
  35.9 0.0 copy-start.5
  35.9 27.0 %all-to-all-done.payload = bf16[128,104,128]{2,1,0:T(8,128)(2,1)} async-done(((bf16[128,104,128]{2,1,0:T(8,128)(2,1)}), bf16[128,104,128]{2,1,0:T(8,128)(2,1)}, u32[]{:S(2)}, u32[]{:S(2)}) %all-to-all-start) | async-done | bytes 3407904 | tf_op jit(solution)/shard_map/all_to_all | solution.py:620
  62.9 0.0 copy-done.3
  62.9 4.2 %donors.1 = f32[16,16,256]{2,1,0:T(8,128)} custom-call(s32[1,2]{1,0:T(1,128)S(1)} %copy-done.6, f32[2,256]{1,0:T(2,128)S(1)} %collective-permute-done.low_in, f32[2,256]{1,0:T(2,128)S(1)} %collective-permute-done.1.high_in, bf16[128,104,128]{2,1,0:T(8,128)(2,1)} %all-to-all-done.payload, bf16[512,256]{1,0:T(8,128)(2,1)S(1)} %copy-done.3, ...), custom_call_target="tpu_custom_call" | custom-call | tf_op jit(solution)/shard_map/donors/pallas_call | solution.py:626
  67.1 0.0 copy-done.4
  67.1 0.0 copy-done.5
  67.1 5.6 %all-to-all-start.1 = ((f32[16,16,256]{2,1,0:T(8,128)}), f32[16,16,256]{2,1,0:T(8,128)S(1)}, u32[]{:S(2)}, u32[]{:S(2)}) async-start(f32[16,16,256]{2,1,0:T(8,128)} %donors.1), calls=%async_computation.1 | async-start | bytes 524288 | tf_op jit(solution)/shard_map/all_to_all | solution.py:645
  72.7 0.0 copy-start.1
  72.7 12.1 %receive.1.inside = f32[4,512,256]{2,1,0:T(8,128)} custom-call(f32[2,256]{1,0:T(2,128)} %copy-done.5, f32[2,256]{1,0:T(2,128)} %copy-done.4, bf16[128,104,128]{2,1,0:T(8,128)(2,1)} %all-to-all-done.payload, bf16[512,256]{1,0:T(8,128)(2,1)} %constant.32.clone.weights_in, f32[4,512,256]{2,1,0:T(8,128)} %copy-done.2, ...), custom_call_target="tpu_custom_call" | custom-call | tf_op jit(solution)/shard_map/receive/pallas_call | solution.py:646
  84.8 0.0 all-to-all-done.1.got
  84.8 0.0 copy-done.1
  84.9 1.9 %edges.1 = f32[4,512,256]{2,1,0:T(8,128)} custom-call(s32[1]{0:T(128)} %bitcast.here_at, f32[16,16,256]{2,1,0:T(8,128)S(1)} %all-to-all-done.1.got, bf16[256,512]{1,0:T(8,128)(2,1)S(1)} %copy-done.1, f32[4,512,256]{2,1,0:T(8,128)} %receive.1.inside), custom_call_target="tpu_custom_call", output_to_operand_aliasing={{}: (3, {})} | custom-call | tf_op jit(solution)/shard_map/edges/pallas_call | solution.py:355
  (2 shorter events, 0.0 us)
Async XLA Ops:
  7.3 11.9 %copy-start.6 = (s32[1,2]{1,0:T(1,128)S(1)}, s32[1,2]{1,0:T(1,128)}, u32[]{:S(2)}) copy-start(s32[1,2]{1,0:T(1,128)} %fringe.3) | copy-start | bytes 28
  7.3 24.5 %copy-start = (bf16[256,512]{1,0:T(8,128)(2,1)S(1)}, bf16[256,512]{1,0:T(8,128)(2,1)}, u32[]{:S(2)}) copy-start(bf16[256,512]{1,0:T(8,128)(2,1)} %constant.31.clone.dmat.dmat_in) | copy-start | bytes 786436
  7.3 55.6 %all-to-all-start = ((bf16[128,104,128]{2,1,0:T(8,128)(2,1)}), bf16[128,104,128]{2,1,0:T(8,128)(2,1)}, u32[]{:S(2)}, u32[]{:S(2)}) async-start(bf16[128,104,128]{2,1,0:T(8,128)(2,1)} %pack.1), calls=%async_computation | async-start | bytes 6815744 | tf_op jit(solution)/shard_map/all_to_all | solution.py:620
  19.2 43.7 %copy-start.3 = (bf16[512,256]{1,0:T(8,128)(2,1)S(1)}, bf16[512,256]{1,0:T(8,128)(2,1)}, u32[]{:S(2)}) copy-start(bf16[512,256]{1,0:T(8,128)(2,1)} %constant.32.clone.weights_in) | copy-start | bytes 786436
  24.4 11.5 %collective-permute-start.1 = (f32[2,256]{1,0:T(2,128)S(1)}, f32[2,256]{1,0:T(2,128)S(1)}, u32[]{:S(2)}, u32[]{:S(2)}) collective-permute-start(f32[2,256]{1,0:T(2,128)S(1)} %pad_maximum_fusion.1), channel_id=1, source_target_pairs={{1,0},{2,1},{3,2},{4,3},{5,4},{6,5},{7,6},{8,7},{9,8},{10,9},{11,1... | collective-permute-start | bytes 6152 | tf_op jit(solution)/shard_map/ppermute | solution.py:593
  27.5 8.4 %collective-permute-start = (f32[2,256]{1,0:T(2,128)S(1)}, f32[2,256]{1,0:T(2,128)S(1)}, u32[]{:S(2)}, u32[]{:S(2)}) collective-permute-start(f32[2,256]{1,0:T(2,128)S(1)} %pad_maximum_fusion), channel_id=1, source_target_pairs={{0,1},{1,2},{2,3},{3,4},{4,5},{5,6},{6,7},{7,8},{8,9},{9,10},{10,1... | collective-permute-start | bytes 6152 | tf_op jit(solution)/shard_map/ppermute | solution.py:593
  34.5 1.4 %copy-start.2 = (f32[4,512,256]{2,1,0:T(8,128)}, f32[4,512,256]{2,1,0:T(8,128)S(1)}, u32[]{:S(2)}) copy-start(f32[4,512,256]{2,1,0:T(8,128)S(1)} %get-tuple-element.8.rate_in) | copy-start | bytes 6291460
  35.9 31.2 %copy-start.4 = (f32[2,256]{1,0:T(2,128)}, f32[2,256]{1,0:T(2,128)S(1)}, u32[]{:S(2)}) copy-start(f32[2,256]{1,0:T(2,128)S(1)} %collective-permute-done.1.high_in) | copy-start | bytes 6148
  35.9 31.2 %copy-start.5 = (f32[2,256]{1,0:T(2,128)}, f32[2,256]{1,0:T(2,128)S(1)}, u32[]{:S(2)}) copy-start(f32[2,256]{1,0:T(2,128)S(1)} %collective-permute-done.low_in) | copy-start | bytes 6148
  67.1 17.7 %all-to-all-start.1 = ((f32[16,16,256]{2,1,0:T(8,128)}), f32[16,16,256]{2,1,0:T(8,128)S(1)}, u32[]{:S(2)}, u32[]{:S(2)}) async-start(f32[16,16,256]{2,1,0:T(8,128)} %donors.1), calls=%async_computation.1 | async-start | bytes 524288 | tf_op jit(solution)/shard_map/all_to_all | solution.py:645
  72.7 12.1 %copy-start.1 = (bf16[256,512]{1,0:T(8,128)(2,1)S(1)}, bf16[256,512]{1,0:T(8,128)(2,1)}, u32[]{:S(2)}) copy-start(bf16[256,512]{1,0:T(8,128)(2,1)} %constant.31.clone.dmat.dmat_in) | copy-start | bytes 786436

commit v6 on v5

--- a/solution.py
+++ b/solution.py
@@ -140,14 +140,16 @@
             shift //= 2
         return jnp.where(my_part, total, 0.0)[:, None, :]
 
-    def group(g, carry):
-        first = pl.multiple_of(g * GROUP, GROUP)
+    def chosen(first):
         mine = ranks[pl.ds(first, GROUP), :]
         pieces = []
         for n in range(GROUP):
             row = jnp.broadcast_to(mine[n:n + 1, :], (16, slabs)).astype(jnp.bfloat16)
             pieces += [jnp.where(row == slot, one, zero) for slot in slots]
-        choose = jnp.concatenate(pieces, axis=0)
+        return jnp.concatenate(pieces, axis=0)
+
+    def group(g, choose):
+        first = g * GROUP
         picked = jnp.dot(choose, table[...], preferred_element_type=jnp.float32)
         for c in range(3):
             rows = picked[:, c * coarse:(c + 1) * coarse].reshape(GROUP, capacity, coarse)
@@ -161,17 +163,20 @@
         tile = jnp.where(which_row == 0, upper, jnp.where(which_row == 1, lower, 0.0))
         payload[pl.ds(first, GROUP), 3 * capacity:, :] = tile.astype(jnp.bfloat16)
         leave(g).start()
-        return carry
 
     def leave(g):
-        mine = pl.ds(pl.multiple_of(g * GROUP, GROUP), GROUP)
+        mine = pl.ds(g * GROUP, GROUP)
         return pltpu.make_async_copy(payload.at[mine], payload_out.at[mine], left.at[g])
 
     def gone(g, carry):
         leave(g).wait()
         return carry
 
-    lax.fori_loop(0, devices // GROUP, group, 0, unroll=True)
+    choose = chosen(0)
+    for g in range(devices // GROUP):
+        later = chosen((g + 1) * GROUP) if (g + 1) * GROUP < devices else None
+        group(g, choose)
+        choose = later
     lax.fori_loop(0, devices // GROUP, gone, 0)
 
 

time: 87.3 us -> 87.3 us (level)
  no operation moved by 1% of the time
where the time goes in v6:
time: 87.3 us; the launch traced here: 86.7 us
  Pallas kernels  28 us (32%)
  waiting for transfers between devices  27 us (31%)
  starting transfers between devices  24.9 us (29%)
  between operations  4.01 us (5%)
  local copies, waits for them, and re-layouts  2.77 us (3%)
    all_to_all x1, waiting for transfers between devices, local(): lax.all_to_all(payload, AXES, split_axis=0, concat_axis=0, tiled=True)  27 us
    pallas_call x1, Pallas kernels, local(): pl.pallas_call(receive_kernel, out_shape=state_type, in_specs=far(7), out...  12.1 us
    all_to_all x1, starting transfers between devices, local(): lax.all_to_all(payload, AXES, split_axis=0, concat_axis=0, tiled=True)  11.9 us
    ppermute x2, starting transfers between devices, shifted(): return lax.ppermute(x, 'ac', pairs)  7.36 us
    pallas_call x1, Pallas kernels, pack(): pl.pallas_call(pack_kernel, out_shape=jax.ShapeDtypeStruct((devices, 3 *...  7.25 us
    all_to_all x1, starting transfers between devices, local(): got = lax.all_to_all(sent, 'ac', split_axis=0, concat_axis=0, tiled=True)  5.64 us
    pallas_call x1, Pallas kernels, local(): pl.pallas_call(functools.partial(donors_kernel, lines), out_shape=jax.Sha...  4.18 us
    pallas_call x1, Pallas kernels, call(): pl.pallas_call(kernel, out_shape=outputs, in_specs=[scalars()] * smem + w...  2.66 us
  transfers between devices with their start and end apart: 4, of which 1 were waited for; matrix products, arithmetic and copies ran while one was open for 2% of the time, Pallas kernels for 17%

profile of v6, /device:TPU:1, one launch (start us, length us, event | category | flops | bytes accessed | tf_op | source)
XLA Modules:
  0.0 86.7 jit_solution(16500783262040381737)
XLA Ops:
  0.0 7.2 %pack.1 = bf16[128,104,128]{2,1,0:T(8,128)(2,1)} custom-call(s32[1]{0:T(128)} %bitcast.7.place, bf16[3,1024,128]{2,1,0:T(8,128)(2,1)} %velocity.1, bf16[3,1024,128]{2,1,0:T(8,128)(2,1)} %vorticity.1, s32[2,1024]{1,0:T(2,128)} %bitcast.15, s32[2,1024]{1,0:T(2,128)} %bitcast.16, s32[2,1024]{1,0:T(2,128)} %bitcast.17), custom_call_target="tpu_custom_call" | custom-call | tf_op jit(solution)/shard_map/pack/pallas_call | solution.py:185
  7.3 0.0 copy-start.6
  7.3 0.0 copy-start
  7.3 11.9 %all-to-all-start = ((bf16[128,104,128]{2,1,0:T(8,128)(2,1)}), bf16[128,104,128]{2,1,0:T(8,128)(2,1)}, u32[]{:S(2)}, u32[]{:S(2)}) async-start(bf16[128,104,128]{2,1,0:T(8,128)(2,1)} %pack.1), calls=%async_computation | async-start | bytes 6815744 | tf_op jit(solution)/shard_map/all_to_all | solution.py:625
  19.2 0.0 copy-done.6
  19.2 0.0 copy-start.3
  19.2 0.6 fusion
  23.7 0.8 dynamic-slice_bitcast_fusion.1
  24.4 3.0 %collective-permute-start.1 = (f32[2,256]{1,0:T(2,128)S(1)}, f32[2,256]{1,0:T(2,128)S(1)}, u32[]{:S(2)}, u32[]{:S(2)}) collective-permute-start(f32[2,256]{1,0:T(2,128)S(1)} %pad_maximum_fusion.1), channel_id=1, source_target_pairs={{1,0},{2,1},{3,2},{4,3},{5,4},{6,5},{7,6},{8,7},{9,8},{10,9},{11,1... | collective-permute-start | bytes 6152 | tf_op jit(solution)/shard_map/ppermute | solution.py:598
  27.5 4.3 %collective-permute-start = (f32[2,256]{1,0:T(2,128)S(1)}, f32[2,256]{1,0:T(2,128)S(1)}, u32[]{:S(2)}, u32[]{:S(2)}) collective-permute-start(f32[2,256]{1,0:T(2,128)S(1)} %pad_maximum_fusion), channel_id=1, source_target_pairs={{0,1},{1,2},{2,3},{3,4},{4,5},{5,6},{6,7},{7,8},{8,9},{9,10},{10,1... | collective-permute-start | bytes 6152 | tf_op jit(solution)/shard_map/ppermute | solution.py:598
  31.8 0.0 copy-done
  31.8 2.7 %start.1 = (f32[4,512,256]{2,1,0:T(8,128)S(1)}, f32[48,256]{1,0:T(8,128)S(1)}) custom-call(s32[1,2]{1,0:T(1,128)S(1)} %copy-done.6, f32[4,512,256]{2,1,0:T(8,128)} %acoustic_in.1, bf16[256,512]{1,0:T(8,128)(2,1)S(1)} %copy-done), custom_call_target="tpu_custom_call" | custom-call | tf_op jit(solution)/shard_map/start/pallas_call | solution.py:585
  34.5 0.0 copy-start.2
  34.5 1.4 %copy-done.2 = f32[4,512,256]{2,1,0:T(8,128)} copy-done((f32[4,512,256]{2,1,0:T(8,128)}, f32[4,512,256]{2,1,0:T(8,128)S(1)}, u32[]{:S(2)}) %copy-start.2) | copy-done | bytes 2097176
  35.9 0.0 collective-permute-done.1.high_in
  35.9 0.0 copy-start.4
  35.9 0.0 collective-permute-done.low_in
  35.9 0.0 copy-start.5
  35.9 27.0 %all-to-all-done.payload = bf16[128,104,128]{2,1,0:T(8,128)(2,1)} async-done(((bf16[128,104,128]{2,1,0:T(8,128)(2,1)}), bf16[128,104,128]{2,1,0:T(8,128)(2,1)}, u32[]{:S(2)}, u32[]{:S(2)}) %all-to-all-start) | async-done | bytes 3407904 | tf_op jit(solution)/shard_map/all_to_all | solution.py:625
  62.9 0.0 copy-done.3
  62.9 4.2 %donors.1 = f32[16,16,256]{2,1,0:T(8,128)} custom-call(s32[1,2]{1,0:T(1,128)S(1)} %copy-done.6, f32[2,256]{1,0:T(2,128)S(1)} %collective-permute-done.low_in, f32[2,256]{1,0:T(2,128)S(1)} %collective-permute-done.1.high_in, bf16[128,104,128]{2,1,0:T(8,128)(2,1)} %all-to-all-done.payload, bf16[512,256]{1,0:T(8,128)(2,1)S(1)} %copy-done.3, ...), custom_call_target="tpu_custom_call" | custom-call | tf_op jit(solution)/shard_map/donors/pallas_call | solution.py:631
  67.1 0.0 copy-done.4
  67.1 0.0 copy-done.5
  67.1 5.6 %all-to-all-start.1 = ((f32[16,16,256]{2,1,0:T(8,128)}), f32[16,16,256]{2,1,0:T(8,128)S(1)}, u32[]{:S(2)}, u32[]{:S(2)}) async-start(f32[16,16,256]{2,1,0:T(8,128)} %donors.1), calls=%async_computation.1 | async-start | bytes 524288 | tf_op jit(solution)/shard_map/all_to_all | solution.py:650
  72.7 0.0 copy-start.1
  72.7 12.1 %receive.1.inside = f32[4,512,256]{2,1,0:T(8,128)} custom-call(f32[2,256]{1,0:T(2,128)} %copy-done.5, f32[2,256]{1,0:T(2,128)} %copy-done.4, bf16[128,104,128]{2,1,0:T(8,128)(2,1)} %all-to-all-done.payload, bf16[512,256]{1,0:T(8,128)(2,1)} %constant.32.clone.weights_in, f32[4,512,256]{2,1,0:T(8,128)} %copy-done.2, ...), custom_call_target="tpu_custom_call" | custom-call | tf_op jit(solution)/shard_map/receive/pallas_call | solution.py:651
  84.8 0.0 all-to-all-done.1.got
  84.8 0.0 copy-done.1
  84.9 1.9 %edges.1 = f32[4,512,256]{2,1,0:T(8,128)} custom-call(s32[1]{0:T(128)} %bitcast.here_at, f32[16,16,256]{2,1,0:T(8,128)S(1)} %all-to-all-done.1.got, bf16[256,512]{1,0:T(8,128)(2,1)S(1)} %copy-done.1, f32[4,512,256]{2,1,0:T(8,128)} %receive.1.inside), custom_call_target="tpu_custom_call", output_to_operand_aliasing={{}: (3, {})} | custom-call | tf_op jit(solution)/shard_map/edges/pallas_call | solution.py:360
  (2 shorter events, 0.0 us)
Async XLA Ops:
  7.3 11.9 %copy-start.6 = (s32[1,2]{1,0:T(1,128)S(1)}, s32[1,2]{1,0:T(1,128)}, u32[]{:S(2)}) copy-start(s32[1,2]{1,0:T(1,128)} %fringe.3) | copy-start | bytes 28
  7.3 24.5 %copy-start = (bf16[256,512]{1,0:T(8,128)(2,1)S(1)}, bf16[256,512]{1,0:T(8,128)(2,1)}, u32[]{:S(2)}) copy-start(bf16[256,512]{1,0:T(8,128)(2,1)} %constant.31.clone.dmat.dmat_in) | copy-start | bytes 786436
  7.3 55.6 %all-to-all-start = ((bf16[128,104,128]{2,1,0:T(8,128)(2,1)}), bf16[128,104,128]{2,1,0:T(8,128)(2,1)}, u32[]{:S(2)}, u32[]{:S(2)}) async-start(bf16[128,104,128]{2,1,0:T(8,128)(2,1)} %pack.1), calls=%async_computation | async-start | bytes 6815744 | tf_op jit(solution)/shard_map/all_to_all | solution.py:625
  19.2 43.7 %copy-start.3 = (bf16[512,256]{1,0:T(8,128)(2,1)S(1)}, bf16[512,256]{1,0:T(8,128)(2,1)}, u32[]{:S(2)}) copy-start(bf16[512,256]{1,0:T(8,128)(2,1)} %constant.32.clone.weights_in) | copy-start | bytes 786436
  24.4 11.5 %collective-permute-start.1 = (f32[2,256]{1,0:T(2,128)S(1)}, f32[2,256]{1,0:T(2,128)S(1)}, u32[]{:S(2)}, u32[]{:S(2)}) collective-permute-start(f32[2,256]{1,0:T(2,128)S(1)} %pad_maximum_fusion.1), channel_id=1, source_target_pairs={{1,0},{2,1},{3,2},{4,3},{5,4},{6,5},{7,6},{8,7},{9,8},{10,9},{11,1... | collective-permute-start | bytes 6152 | tf_op jit(solution)/shard_map/ppermute | solution.py:598
  27.5 8.4 %collective-permute-start = (f32[2,256]{1,0:T(2,128)S(1)}, f32[2,256]{1,0:T(2,128)S(1)}, u32[]{:S(2)}, u32[]{:S(2)}) collective-permute-start(f32[2,256]{1,0:T(2,128)S(1)} %pad_maximum_fusion), channel_id=1, source_target_pairs={{0,1},{1,2},{2,3},{3,4},{4,5},{5,6},{6,7},{7,8},{8,9},{9,10},{10,1... | collective-permute-start | bytes 6152 | tf_op jit(solution)/shard_map/ppermute | solution.py:598
  34.5 1.4 %copy-start.2 = (f32[4,512,256]{2,1,0:T(8,128)}, f32[4,512,256]{2,1,0:T(8,128)S(1)}, u32[]{:S(2)}) copy-start(f32[4,512,256]{2,1,0:T(8,128)S(1)} %get-tuple-element.8.rate_in) | copy-start | bytes 6291460
  35.9 31.2 %copy-start.4 = (f32[2,256]{1,0:T(2,128)}, f32[2,256]{1,0:T(2,128)S(1)}, u32[]{:S(2)}) copy-start(f32[2,256]{1,0:T(2,128)S(1)} %collective-permute-done.1.high_in) | copy-start | bytes 6148
  35.9 31.2 %copy-start.5 = (f32[2,256]{1,0:T(2,128)}, f32[2,256]{1,0:T(2,128)S(1)}, u32[]{:S(2)}) copy-start(f32[2,256]{1,0:T(2,128)S(1)} %collective-permute-done.low_in) | copy-start | bytes 6148
  67.1 17.7 %all-to-all-start.1 = ((f32[16,16,256]{2,1,0:T(8,128)}), f32[16,16,256]{2,1,0:T(8,128)S(1)}, u32[]{:S(2)}, u32[]{:S(2)}) async-start(f32[16,16,256]{2,1,0:T(8,128)} %donors.1), calls=%async_computation.1 | async-start | bytes 524288 | tf_op jit(solution)/shard_map/all_to_all | solution.py:650
  72.7 12.1 %copy-start.1 = (bf16[256,512]{1,0:T(8,128)(2,1)S(1)}, bf16[256,512]{1,0:T(8,128)(2,1)}, u32[]{:S(2)}) copy-start(bf16[256,512]{1,0:T(8,128)(2,1)} %constant.31.clone.dmat.dmat_in) | copy-start | bytes 786436

commit v7 on v5

--- a/solution.py
+++ b/solution.py
@@ -15,7 +15,7 @@
 CODE_ROWS = 8
 GROUP = 16
 PARTS = 2
-QUARTERS = 4
+QUARTERS = 8
 MIB = 1 << 20
 VMEM_LIMIT = 60 * MIB
 DONORS_LIMIT = 52000 << 10

time: 87.3 us -> 87.2 us (level)
  no operation moved by 1% of the time
where the time goes in v7:
time: 87.2 us; the launch traced here: 86.7 us
  Pallas kernels  28 us (32%)
  waiting for transfers between devices  27 us (31%)
  starting transfers between devices  24.9 us (29%)
  between operations  4.01 us (5%)
  local copies, waits for them, and re-layouts  2.77 us (3%)
    all_to_all x1, waiting for transfers between devices, local(): lax.all_to_all(payload, AXES, split_axis=0, concat_axis=0, tiled=True)  27 us
    pallas_call x1, Pallas kernels, local(): pl.pallas_call(receive_kernel, out_shape=state_type, in_specs=far(7), out...  12.1 us
    all_to_all x1, starting transfers between devices, local(): lax.all_to_all(payload, AXES, split_axis=0, concat_axis=0, tiled=True)  11.9 us
    ppermute x2, starting transfers between devices, shifted(): return lax.ppermute(x, 'ac', pairs)  7.36 us
    pallas_call x1, Pallas kernels, pack(): pl.pallas_call(pack_kernel, out_shape=jax.ShapeDtypeStruct((devices, 3 *...  7.25 us
    all_to_all x1, starting transfers between devices, local(): got = lax.all_to_all(sent, 'ac', split_axis=0, concat_axis=0, tiled=True)  5.64 us
    pallas_call x1, Pallas kernels, local(): pl.pallas_call(functools.partial(donors_kernel, lines), out_shape=jax.Sha...  4.13 us
    pallas_call x1, Pallas kernels, call(): pl.pallas_call(kernel, out_shape=outputs, in_specs=[scalars()] * smem + w...  2.66 us
  transfers between devices with their start and end apart: 4, of which 1 were waited for; matrix products, arithmetic and copies ran while one was open for 2% of the time, Pallas kernels for 17%

profile of v7, /device:TPU:1, one launch (start us, length us, event | category | flops | bytes accessed | tf_op | source)
XLA Modules:
  0.0 86.7 jit_solution(14932258164110622860)
XLA Ops:
  0.0 7.2 %pack.1 = bf16[128,104,128]{2,1,0:T(8,128)(2,1)} custom-call(s32[1]{0:T(128)} %bitcast.7.place, bf16[3,1024,128]{2,1,0:T(8,128)(2,1)} %velocity.1, bf16[3,1024,128]{2,1,0:T(8,128)(2,1)} %vorticity.1, s32[2,1024]{1,0:T(2,128)} %bitcast.15, s32[2,1024]{1,0:T(2,128)} %bitcast.16, s32[2,1024]{1,0:T(2,128)} %bitcast.17), custom_call_target="tpu_custom_call" | custom-call | tf_op jit(solution)/shard_map/pack/pallas_call | solution.py:180
  7.3 0.0 copy-start.6
  7.3 0.0 copy-start
  7.3 11.9 %all-to-all-start = ((bf16[128,104,128]{2,1,0:T(8,128)(2,1)}), bf16[128,104,128]{2,1,0:T(8,128)(2,1)}, u32[]{:S(2)}, u32[]{:S(2)}) async-start(bf16[128,104,128]{2,1,0:T(8,128)(2,1)} %pack.1), calls=%async_computation | async-start | bytes 6815744 | tf_op jit(solution)/shard_map/all_to_all | solution.py:620
  19.2 0.0 copy-done.6
  19.2 0.0 copy-start.3
  19.2 0.6 fusion
  23.7 0.8 dynamic-slice_bitcast_fusion.1
  24.4 3.0 %collective-permute-start.1 = (f32[2,256]{1,0:T(2,128)S(1)}, f32[2,256]{1,0:T(2,128)S(1)}, u32[]{:S(2)}, u32[]{:S(2)}) collective-permute-start(f32[2,256]{1,0:T(2,128)S(1)} %pad_maximum_fusion.1), channel_id=1, source_target_pairs={{1,0},{2,1},{3,2},{4,3},{5,4},{6,5},{7,6},{8,7},{9,8},{10,9},{11,1... | collective-permute-start | bytes 6152 | tf_op jit(solution)/shard_map/ppermute | solution.py:593
  27.5 4.3 %collective-permute-start = (f32[2,256]{1,0:T(2,128)S(1)}, f32[2,256]{1,0:T(2,128)S(1)}, u32[]{:S(2)}, u32[]{:S(2)}) collective-permute-start(f32[2,256]{1,0:T(2,128)S(1)} %pad_maximum_fusion), channel_id=1, source_target_pairs={{0,1},{1,2},{2,3},{3,4},{4,5},{5,6},{6,7},{7,8},{8,9},{9,10},{10,1... | collective-permute-start | bytes 6152 | tf_op jit(solution)/shard_map/ppermute | solution.py:593
  31.8 0.0 copy-done
  31.8 2.7 %start.1 = (f32[4,512,256]{2,1,0:T(8,128)S(1)}, f32[48,256]{1,0:T(8,128)S(1)}) custom-call(s32[1,2]{1,0:T(1,128)S(1)} %copy-done.6, f32[4,512,256]{2,1,0:T(8,128)} %acoustic_in.1, bf16[256,512]{1,0:T(8,128)(2,1)S(1)} %copy-done), custom_call_target="tpu_custom_call" | custom-call | tf_op jit(solution)/shard_map/start/pallas_call | solution.py:580
  34.5 0.0 copy-start.2
  34.5 1.4 %copy-done.2 = f32[4,512,256]{2,1,0:T(8,128)} copy-done((f32[4,512,256]{2,1,0:T(8,128)}, f32[4,512,256]{2,1,0:T(8,128)S(1)}, u32[]{:S(2)}) %copy-start.2) | copy-done | bytes 2097176
  35.9 0.0 collective-permute-done.1.high_in
  35.9 0.0 copy-start.4
  35.9 0.0 collective-permute-done.low_in
  35.9 0.0 copy-start.5
  35.9 27.0 %all-to-all-done.payload = bf16[128,104,128]{2,1,0:T(8,128)(2,1)} async-done(((bf16[128,104,128]{2,1,0:T(8,128)(2,1)}), bf16[128,104,128]{2,1,0:T(8,128)(2,1)}, u32[]{:S(2)}, u32[]{:S(2)}) %all-to-all-start) | async-done | bytes 3407904 | tf_op jit(solution)/shard_map/all_to_all | solution.py:620
  62.9 0.0 copy-done.3
  62.9 4.1 %donors.1 = f32[16,16,256]{2,1,0:T(8,128)} custom-call(s32[1,2]{1,0:T(1,128)S(1)} %copy-done.6, f32[2,256]{1,0:T(2,128)S(1)} %collective-permute-done.low_in, f32[2,256]{1,0:T(2,128)S(1)} %collective-permute-done.1.high_in, bf16[128,104,128]{2,1,0:T(8,128)(2,1)} %all-to-all-done.payload, bf16[512,256]{1,0:T(8,128)(2,1)S(1)} %copy-done.3, ...), custom_call_target="tpu_custom_call" | custom-call | tf_op jit(solution)/shard_map/donors/pallas_call | solution.py:626
  67.0 0.0 copy-done.4
  67.0 0.0 copy-done.5
  67.0 5.6 %all-to-all-start.1 = ((f32[16,16,256]{2,1,0:T(8,128)}), f32[16,16,256]{2,1,0:T(8,128)S(1)}, u32[]{:S(2)}, u32[]{:S(2)}) async-start(f32[16,16,256]{2,1,0:T(8,128)} %donors.1), calls=%async_computation.1 | async-start | bytes 524288 | tf_op jit(solution)/shard_map/all_to_all | solution.py:645
  72.7 0.0 copy-start.1
  72.7 12.1 %receive.1.inside = f32[4,512,256]{2,1,0:T(8,128)} custom-call(f32[2,256]{1,0:T(2,128)} %copy-done.5, f32[2,256]{1,0:T(2,128)} %copy-done.4, bf16[128,104,128]{2,1,0:T(8,128)(2,1)} %all-to-all-done.payload, bf16[512,256]{1,0:T(8,128)(2,1)} %constant.32.clone.weights_in, f32[4,512,256]{2,1,0:T(8,128)} %copy-done.2, ...), custom_call_target="tpu_custom_call" | custom-call | tf_op jit(solution)/shard_map/receive/pallas_call | solution.py:646
  84.8 0.0 all-to-all-done.1.got
  84.8 0.0 copy-done.1
  84.8 1.9 %edges.1 = f32[4,512,256]{2,1,0:T(8,128)} custom-call(s32[1]{0:T(128)} %bitcast.here_at, f32[16,16,256]{2,1,0:T(8,128)S(1)} %all-to-all-done.1.got, bf16[256,512]{1,0:T(8,128)(2,1)S(1)} %copy-done.1, f32[4,512,256]{2,1,0:T(8,128)} %receive.1.inside), custom_call_target="tpu_custom_call", output_to_operand_aliasing={{}: (3, {})} | custom-call | tf_op jit(solution)/shard_map/edges/pallas_call | solution.py:355
  (2 shorter events, 0.0 us)
Async XLA Ops:
  7.3 11.9 %copy-start.6 = (s32[1,2]{1,0:T(1,128)S(1)}, s32[1,2]{1,0:T(1,128)}, u32[]{:S(2)}) copy-start(s32[1,2]{1,0:T(1,128)} %fringe.3) | copy-start | bytes 28
  7.3 24.5 %copy-start = (bf16[256,512]{1,0:T(8,128)(2,1)S(1)}, bf16[256,512]{1,0:T(8,128)(2,1)}, u32[]{:S(2)}) copy-start(bf16[256,512]{1,0:T(8,128)(2,1)} %constant.31.clone.dmat.dmat_in) | copy-start | bytes 786436
  7.3 55.6 %all-to-all-start = ((bf16[128,104,128]{2,1,0:T(8,128)(2,1)}), bf16[128,104,128]{2,1,0:T(8,128)(2,1)}, u32[]{:S(2)}, u32[]{:S(2)}) async-start(bf16[128,104,128]{2,1,0:T(8,128)(2,1)} %pack.1), calls=%async_computation | async-start | bytes 6815744 | tf_op jit(solution)/shard_map/all_to_all | solution.py:620
  19.2 43.7 %copy-start.3 = (bf16[512,256]{1,0:T(8,128)(2,1)S(1)}, bf16[512,256]{1,0:T(8,128)(2,1)}, u32[]{:S(2)}) copy-start(bf16[512,256]{1,0:T(8,128)(2,1)} %constant.32.clone.weights_in) | copy-start | bytes 786436
  24.4 11.5 %collective-permute-start.1 = (f32[2,256]{1,0:T(2,128)S(1)}, f32[2,256]{1,0:T(2,128)S(1)}, u32[]{:S(2)}, u32[]{:S(2)}) collective-permute-start(f32[2,256]{1,0:T(2,128)S(1)} %pad_maximum_fusion.1), channel_id=1, source_target_pairs={{1,0},{2,1},{3,2},{4,3},{5,4},{6,5},{7,6},{8,7},{9,8},{10,9},{11,1... | collective-permute-start | bytes 6152 | tf_op jit(solution)/shard_map/ppermute | solution.py:593
  27.5 8.4 %collective-permute-start = (f32[2,256]{1,0:T(2,128)S(1)}, f32[2,256]{1,0:T(2,128)S(1)}, u32[]{:S(2)}, u32[]{:S(2)}) collective-permute-start(f32[2,256]{1,0:T(2,128)S(1)} %pad_maximum_fusion), channel_id=1, source_target_pairs={{0,1},{1,2},{2,3},{3,4},{4,5},{5,6},{6,7},{7,8},{8,9},{9,10},{10,1... | collective-permute-start | bytes 6152 | tf_op jit(solution)/shard_map/ppermute | solution.py:593
  34.5 1.4 %copy-start.2 = (f32[4,512,256]{2,1,0:T(8,128)}, f32[4,512,256]{2,1,0:T(8,128)S(1)}, u32[]{:S(2)}) copy-start(f32[4,512,256]{2,1,0:T(8,128)S(1)} %get-tuple-element.8.rate_in) | copy-start | bytes 6291460
  35.9 31.1 %copy-start.4 = (f32[2,256]{1,0:T(2,128)}, f32[2,256]{1,0:T(2,128)S(1)}, u32[]{:S(2)}) copy-start(f32[2,256]{1,0:T(2,128)S(1)} %collective-permute-done.1.high_in) | copy-start | bytes 6148
  35.9 31.1 %copy-start.5 = (f32[2,256]{1,0:T(2,128)}, f32[2,256]{1,0:T(2,128)S(1)}, u32[]{:S(2)}) copy-start(f32[2,256]{1,0:T(2,128)S(1)} %collective-permute-done.low_in) | copy-start | bytes 6148
  67.0 17.7 %all-to-all-start.1 = ((f32[16,16,256]{2,1,0:T(8,128)}), f32[16,16,256]{2,1,0:T(8,128)S(1)}, u32[]{:S(2)}, u32[]{:S(2)}) async-start(f32[16,16,256]{2,1,0:T(8,128)} %donors.1), calls=%async_computation.1 | async-start | bytes 524288 | tf_op jit(solution)/shard_map/all_to_all | solution.py:645
  72.7 12.1 %copy-start.1 = (bf16[256,512]{1,0:T(8,128)(2,1)S(1)}, bf16[256,512]{1,0:T(8,128)(2,1)}, u32[]{:S(2)}) copy-start(bf16[256,512]{1,0:T(8,128)(2,1)} %constant.31.clone.dmat.dmat_in) | copy-start | bytes 786436
